TPU v7x, 32 devices: a whole 2x2x4 slice. The times are simulated.
32 devices in a mesh: sub: 8 (over z, y), grp: 4 (over x, core).
Axes of the slice: x: 2, y: 2, z: 4, core: 2. Of those that a mesh axis runs over, the one named last changes fastest.
Arguments:
- rhs: float32 [8, 4, 64, 128], P('sub', 'grp')
- guess: float32 [8, 4, 64, 128], P('sub', 'grp'), may hold values from -6 to 6
- blocks: bfloat16 [8, 4, 64, 64, 128], P('sub', 'grp')
- valve: int32 [8, 4, 128], P('sub', 'grp'), may hold values 0 or 1
- jscale: float32 [8, 4, 64, 128], P('sub', 'grp'), may hold values from 0.1 to 0.4
- prolong: float32 [8, 4, 64, 128], P('sub', 'grp'), may hold values from -0.75 to 0.75
- agg_map: int32 [8, 4, 128], P('sub', 'grp'), may hold values from 0 to 47
- cdiag: float32 [1536], P(('sub', 'grp')), may hold values from 0.5 to 2
- coff: bfloat16 [1536, 1536], P(('sub', 'grp')), may hold values from -0.3125 to 0.3125
- send_rows: int32 [8, 4, 2, 128], P('sub', 'grp'), may hold values from 0 to 127
- recv_rows: int32 [8, 4, 2, 128], P('sub', 'grp'), may hold values from 0 to 127
- live_counts: int32 [8, 4, 2], P('sub', 'grp'), may hold values from 32 to 128, as said below
Outputs:
- solution: float32 [8, 4, 64, 128], P('sub', 'grp')
- next_basis: float32 [8, 4, 64, 128], P('sub', 'grp')
Inputs may be any that keep to these rules, and one draw needn't show every extreme that they name: `send_rows`: block numbers of the sending subdomain. `recv_rows`: block numbers of the receiving subdomain; several slots may name one block. `live_counts`: some subdomain has every slot live in both lists. `agg_map`: aggregates may be empty.
All inputs are finite; a program needn't handle non-finite values. No bound on the sum of `valve` on one device may be relied on, other than what follows from the above.
Results may differ from a plain program's by a relative error of at most 0.003.
Values may be sent and summed in bfloat16 or wider, within the bound.
No kernel may reach another device: no remote copies, remote signals or barrier semaphores. Data moves between devices by JAX's collectives and lax.ppermute only.
A program may use at most 64 MiB of HBM per device.

v0:
```python
import jax
import jax.numpy as jnp
from jax import lax
from jax.sharding import PartitionSpec as P

ITERS = 2


penalty_gain = 3.0
coupling = 0.5


def extended(cells, sides, width):
    for axis, dim in sides:
        count = lax.axis_size(axis)
        ends = count - 1
        head = lax.slice_in_dim(cells, 0, width, axis=dim)
        tail = lax.slice_in_dim(cells, cells.shape[dim] - width, cells.shape[dim], axis=dim)
        cells = jnp.concatenate(
            [
                lax.ppermute(tail, axis, [(i, (i + 1) % count) for i in range(ends)]),
                cells,
                lax.ppermute(head, axis, [((i + 1) % count, i) for i in range(ends)]),
            ],
            axis=dim,
        )
    return cells


def solve_small(gram, target):
    count = target.shape[0]
    matrix = [[gram[row, col] for col in range(count)] for row in range(count)]
    vector = [target[row] for row in range(count)]
    for pivot in range(count):
        for row in range(pivot + 1, count):
            factor = matrix[row][pivot] / matrix[pivot][pivot]
            for col in range(pivot, count):
                matrix[row][col] = matrix[row][col] - factor * matrix[pivot][col]
            vector[row] = vector[row] - factor * vector[pivot]
    result = [None] * count
    for row in range(count - 1, -1, -1):
        total = vector[row]
        for col in range(row + 1, count):
            total = total - matrix[row][col] * result[col]
        result[row] = total / matrix[row][row]
    return result


def on_device(
    rhs,
    guess,
    blocks,
    valve,
    jscale,
    prolong,
    agg_map,
    cdiag,
    coff,
    send_rows,
    recv_rows,
    live_counts,
):
    highest = lax.Precision.HIGHEST
    right = rhs[0, 0]
    start_vec = guess[0, 0]
    block_mat = blocks[0, 0].astype(jnp.float32)
    scaling = jscale[0, 0]
    weights = prolong[0, 0]
    nblk = right.shape[1]
    places = jnp.arange(nblk, dtype=jnp.int32)
    slots = jnp.arange(send_rows.shape[3], dtype=jnp.int32)
    send_sel = [
        (places[:, None] == send_rows[0, 0, side][None, :]).astype(jnp.float32) for side in (0, 1)
    ]
    recv_sel = [
        (
            (recv_rows[0, 0, side][:, None] == places[None, :])
            & (slots < live_counts[0, 0, side])[:, None]
        ).astype(jnp.float32)
        for side in (0, 1)
    ]
    penalty_row = penalty_gain * valve[0, 0].astype(jnp.float32)
    coarse_count = cdiag.shape[0]
    agg_sel = (agg_map[0, 0][:, None] == jnp.arange(coarse_count, dtype=jnp.int32)[None, :]).astype(
        jnp.float32
    )

    def operate(field):
        out = (
            jnp.einsum("ijb,jb->ib", block_mat, field, precision=highest)
            + penalty_row[None, :] * field
        )
        upward = jnp.dot(field, send_sel[0], precision=highest)
        downward = jnp.dot(field, send_sel[1], precision=highest)
        stacked = jnp.stack([upward, downward])[None]
        padded = extended(stacked, (("sub", 0),), 1)
        below = padded[0, 0]
        above = padded[2, 1]
        incoming = jnp.dot(below, recv_sel[0], precision=highest) + jnp.dot(
            above, recv_sel[1], precision=highest
        )
        return out - coupling * incoming

    first = right - operate(start_vec)
    directions = []
    hess = jnp.zeros((ITERS + 1, ITERS), jnp.float32)
    beta = jnp.sqrt(lax.psum(jnp.sum(first * first), ("sub", "grp")))
    basis = [first / beta]
    for column in range(ITERS):
        precondition_field = basis[column]
        weighted = jnp.sum(weights * precondition_field, axis=0)
        precondition_coarse = jnp.dot(weighted, agg_sel, precision=highest)
        coarse_half = precondition_coarse.astype(jnp.bfloat16)
        gathered = lax.all_gather(coarse_half, ("sub", "grp"), axis=0, tiled=True)
        precondition_product = jnp.dot(coff, gathered, preferred_element_type=jnp.float32)
        coarse_sol = cdiag * precondition_coarse + precondition_product
        spread = jnp.dot(agg_sel, coarse_sol, precision=highest)
        direction = scaling * precondition_field + weights * spread[None, :]
        image = operate(direction)
        local_terms = jnp.stack(
            [jnp.sum(vector * image) for vector in basis] + [jnp.sum(image * image)]
        )
        totals = lax.psum(local_terms, ("sub", "grp"))
        extend_image = image
        extend_hess = hess
        heights = totals[: column + 1]
        energy = totals[column + 1]
        for row in range(column + 1):
            extend_image = extend_image - heights[row] * basis[row]
        remainder = energy - jnp.sum(heights * heights)
        height = jnp.sqrt(jnp.maximum(remainder, 0.01 * energy))
        extend_hess = (
            extend_hess.at[: column + 1, column].set(heights).at[column + 1, column].set(height)
        )
        heights, height, fresh, hess = (heights, height, extend_image / height, extend_hess)
        basis.append(fresh)
        directions.append(direction)
    gram = jnp.dot(hess.T, hess, precision=highest)
    coeffs = solve_small(gram, beta * hess[0])
    solution = start_vec
    for column in range(ITERS):
        solution = solution + coeffs[column] * directions[column]
    return (solution[None, None], basis[ITERS][None, None])


def solution(mesh):
    return jax.shard_map(
        on_device,
        mesh=mesh,
        in_specs=(
            P("sub", "grp", None, None),
            P("sub", "grp", None, None),
            P("sub", "grp", None, None, None),
            P("sub", "grp", None),
            P("sub", "grp", None, None),
            P("sub", "grp", None, None),
            P("sub", "grp", None),
            P(("sub", "grp")),
            P(("sub", "grp"), None),
            P("sub", "grp", None, None),
            P("sub", "grp", None, None),
            P("sub", "grp", None),
        ),
        out_specs=(P("sub", "grp", None, None), P("sub", "grp", None, None)),
        check_vma=False,
    )
```

profile of v0, /device:TPU:0, one launch (start us, length us, event | category | flops | bytes accessed | tf_op | source)
XLA Modules:
  0.0 269.7 jit_solution(8175977812884645228)
XLA Ops:
  0.7 0.8 slice_bitcast_fusion.15
  1.5 0.9 convolution_bitcast_fusion.4
  2.4 0.9 convolution_bitcast_fusion.5
  3.4 1.3 collective-permute-start.1
  4.7 5.5 %collective-permute-start = (f32[1,2,64,128]{3,2,1,0:T(8,128)S(1)}, f32[1,2,64,128]{3,2,1,0:T(8,128)S(1)}, u32[]{:S(2)}, u32[]{:S(2)}) collective-permute-start(f32[1,2,64,128]{3,2,1,0:T(8,128)S(1)} %maximum_bitcast_fusion), channel_id=1, source_target_pairs={{0,4},{4,8},{8,12},{12,16},{16,20},{20,24},{24,28},{1,5},{5,9},{9,... | collective-permute-start | bytes 196616 | tf_op jit(solution)/shard_map/ppermute | solution.py:21
  10.2 1.3 fusion.62
  11.5 0.6 iota_compare_fusion.15
  12.2 0.8 slice_bitcast_fusion.13
  12.9 0.7 multiply_bitcast_fusion
  13.6 0.6 fusion.60
  14.2 1.7 fusion
  15.9 0.7 iota_compare_fusion.16
  16.6 0.3 fusion.23
  16.9 0.9 multiply_reduce_fusion.5
  17.7 42.1 %psum.21 = f32[]{:T(128)} all-reduce(f32[]{:T(128)} %get-tuple-element.76), channel_id=1, replica_groups=mesh['sub'=8,'grp'=4] {'sub','grp'}, use_global_device_ids=true, to_apply=%region_1.0 | all-reduce | flops 1 | bytes 8 | tf_op jit(solution)/shard_map/psum | solution.py:107
  60.8 0.2 dynamic-update-slice.8
  61.1 39.3 %all-reduce.1 = bf16[1536]{0:T(1024)(128)(2,1)S(1)} all-reduce(bf16[1536]{0:T(1024)(128)(2,1)S(1)} %dynamic-update-slice.8), channel_id=1, replica_groups=mesh['sub'=8,'grp'=4] {'sub','grp'}, use_global_device_ids=true, to_apply=%add.1 | all-reduce | flops 1536 | bytes 6144
  100.5 0.2 convolution_bitcast_fusion.10
  101.2 1.3 collective-permute-start.3
  102.5 4.8 %collective-permute-start.2 = (f32[1,2,64,128]{3,2,1,0:T(8,128)S(1)}, f32[1,2,64,128]{3,2,1,0:T(8,128)S(1)}, u32[]{:S(2)}, u32[]{:S(2)}) collective-permute-start(f32[1,2,64,128]{3,2,1,0:T(8,128)S(1)} %maximum_bitcast_fusion.1), channel_id=1, source_target_pairs={{0,4},{4,8},{8,12},{12,16},{16,20},{20,24},{24,28},{1,5},{5,9},{9,... | collective-permute-start | bytes 196616 | tf_op jit(solution)/shard_map/ppermute | solution.py:21
  107.3 0.3 fusion.1
  107.7 0.3 fusion.21
  107.9 1.3 collective-permute-done.2
  109.2 0.9 multiply_reduce_fusion.4
  110.1 1.4 pad_maximum_fusion
  111.4 0.6 compare_reduce_fusion
  112.1 42.4 %psum.22 = f32[2]{0:T(128)S(1)} all-reduce(f32[2]{0:T(128)S(1)} %pad_maximum_fusion), channel_id=1, replica_groups=mesh['sub'=8,'grp'=4] {'sub','grp'}, use_global_device_ids=true, to_apply=%region_5.0 | all-reduce | flops 2 | bytes 16 | tf_op jit(solution)/shard_map/psum | solution.py:123
  154.5 0.6 fusion.61
  157.7 0.7 fusion.27
  158.6 0.2 dynamic-update-slice.9
  158.8 41.0 %all-reduce.2 = bf16[1536]{0:T(1024)(128)(2,1)S(1)} all-reduce(bf16[1536]{0:T(1024)(128)(2,1)S(1)} %dynamic-update-slice.9), channel_id=1, replica_groups=mesh['sub'=8,'grp'=4] {'sub','grp'}, use_global_device_ids=true, to_apply=%add.2 | all-reduce | flops 1536 | bytes 6144
  200.0 0.2 convolution_bitcast_fusion.8
  200.6 1.3 collective-permute-start.5
  201.9 4.8 %collective-permute-start.4 = (f32[1,2,64,128]{3,2,1,0:T(8,128)S(1)}, f32[1,2,64,128]{3,2,1,0:T(8,128)S(1)}, u32[]{:S(2)}, u32[]{:S(2)}) collective-permute-start(f32[1,2,64,128]{3,2,1,0:T(8,128)S(1)} %maximum_bitcast_fusion.2), channel_id=1, source_target_pairs={{0,4},{4,8},{8,12},{12,16},{16,20},{20,24},{24,28},{1,5},{5,9},{9,... | collective-permute-start | bytes 196616 | tf_op jit(solution)/shard_map/ppermute | solution.py:21
  206.7 0.3 fusion.2
  207.1 0.7 scatter.14
  207.8 0.3 fusion.19
  208.0 0.6 collective-permute-done.4
  208.6 0.9 multiply_reduce_fusion.2
  209.6 2.0 pad_maximum_fusion.1
  211.6 42.5 %psum.23 = f32[3]{0:T(128)S(1)} all-reduce(f32[3]{0:T(128)S(1)} %pad_maximum_fusion.1), channel_id=1, replica_groups=mesh['sub'=8,'grp'=4] {'sub','grp'}, use_global_device_ids=true, to_apply=%region_11.0 | all-reduce | flops 3 | bytes 24 | tf_op jit(solution)/shard_map/psum | solution.py:123
  254.2 0.6 fusion.59
  254.8 0.6 multiply_reduce_fusion.6
  257.4 1.9 broadcast_select_fusion
  259.3 1.4 scatter.16
  260.9 0.7 fusion.57
  261.6 0.5 fusion.58
  267.9 1.9 fusion.32
  (43 shorter events, 2.0 us)
Async XLA Ops:
  0.6 99.8 %copy-start = (bf16[48,1536]{1,0:T(8,128)(2,1)S(1)}, bf16[48,1536]{1,0:T(8,128)(2,1)}, u32[]{:S(2)}) copy-start(bf16[48,1536]{1,0:T(8,128)(2,1)} %param.28) | copy-start | bytes 442372
  0.6 16.2 %copy-start.2 = (f32[1,1,64,128]{3,2,1,0:T(8,128)S(1)}, f32[1,1,64,128]{3,2,1,0:T(8,128)}, u32[]{:S(2)}) copy-start(f32[1,1,64,128]{3,2,1,0:T(8,128)} %param.21) | copy-start | bytes 98308
  0.7 16.2 %copy-start.5 = (f32[1,1,64,128]{3,2,1,0:T(8,128)S(1)}, f32[1,1,64,128]{3,2,1,0:T(8,128)}, u32[]{:S(2)}) copy-start(f32[1,1,64,128]{3,2,1,0:T(8,128)} %param.20) | copy-start | bytes 98308
  0.7 59.9 %copy-start.3 = (f32[1,1,64,128]{3,2,1,0:T(8,128)S(1)}, f32[1,1,64,128]{3,2,1,0:T(8,128)}, u32[]{:S(2)}) copy-start(f32[1,1,64,128]{3,2,1,0:T(8,128)} %param.25) | copy-start | bytes 98308
  0.7 59.9 %copy-start.7 = (s32[1,1,128]{2,1,0:T(1,128)S(1)}, s32[1,1,128]{2,1,0:T(1,128)}, u32[]{:S(2)}) copy-start(s32[1,1,128]{2,1,0:T(1,128)} %param.26) | copy-start | bytes 1540
  0.7 99.7 %copy-start.6 = (f32[48]{0:T(128)S(1)}, f32[48]{0:T(128)}, u32[]{:S(2)}) copy-start(f32[48]{0:T(128)} %param.27) | copy-start | bytes 580
  2.4 98.4 %copy-start.4 = (f32[1,1,64,128]{3,2,1,0:T(8,128)S(1)}, f32[1,1,64,128]{3,2,1,0:T(8,128)}, u32[]{:S(2)}) copy-start(f32[1,1,64,128]{3,2,1,0:T(8,128)} %param.24) | copy-start | bytes 98308
  3.4 13.2 %collective-permute-start.1 = (f32[1,2,64,128]{3,2,1,0:T(8,128)S(1)}, f32[1,2,64,128]{3,2,1,0:T(8,128)S(1)}, u32[]{:S(2)}, u32[]{:S(2)}) collective-permute-start(f32[1,2,64,128]{3,2,1,0:T(8,128)S(1)} %maximum_bitcast_fusion), channel_id=1, source_target_pairs={{4,0},{8,4},{12,8},{16,12},{20,16},{24,20},{28,24},{5,1},{9,5},{13... | collective-permute-start | bytes 196616 | tf_op jit(solution)/shard_map/ppermute | solution.py:23
  4.7 12.2 %collective-permute-start = (f32[1,2,64,128]{3,2,1,0:T(8,128)S(1)}, f32[1,2,64,128]{3,2,1,0:T(8,128)S(1)}, u32[]{:S(2)}, u32[]{:S(2)}) collective-permute-start(f32[1,2,64,128]{3,2,1,0:T(8,128)S(1)} %maximum_bitcast_fusion), channel_id=1, source_target_pairs={{0,4},{4,8},{8,12},{12,16},{16,20},{20,24},{24,28},{1,5},{5,9},{9,... | collective-permute-start | bytes 196616 | tf_op jit(solution)/shard_map/ppermute | solution.py:21
  14.2 93.1 %copy-start.1 = (bf16[1,1,64,64,128]{4,3,2,1,0:T(8,128)(2,1)S(1)}, bf16[1,1,64,64,128]{4,3,2,1,0:T(8,128)(2,1)}, u32[]{:S(2)}) copy-start(bf16[1,1,64,64,128]{4,3,2,1,0:T(8,128)(2,1)} %param.22) | copy-start | bytes 3145732
  101.2 6.5 %collective-permute-start.3 = (f32[1,2,64,128]{3,2,1,0:T(8,128)S(1)}, f32[1,2,64,128]{3,2,1,0:T(8,128)S(1)}, u32[]{:S(2)}, u32[]{:S(2)}) collective-permute-start(f32[1,2,64,128]{3,2,1,0:T(8,128)S(1)} %maximum_bitcast_fusion.1), channel_id=1, source_target_pairs={{4,0},{8,4},{12,8},{16,12},{20,16},{24,20},{28,24},{5,1},{9,5},{13... | collective-permute-start | bytes 196616 | tf_op jit(solution)/shard_map/ppermute | solution.py:23
  102.5 6.7 %collective-permute-start.2 = (f32[1,2,64,128]{3,2,1,0:T(8,128)S(1)}, f32[1,2,64,128]{3,2,1,0:T(8,128)S(1)}, u32[]{:S(2)}, u32[]{:S(2)}) collective-permute-start(f32[1,2,64,128]{3,2,1,0:T(8,128)S(1)} %maximum_bitcast_fusion.1), channel_id=1, source_target_pairs={{0,4},{4,8},{8,12},{12,16},{16,20},{20,24},{24,28},{1,5},{5,9},{9,... | collective-permute-start | bytes 196616 | tf_op jit(solution)/shard_map/ppermute | solution.py:21
  200.6 7.1 %collective-permute-start.5 = (f32[1,2,64,128]{3,2,1,0:T(8,128)S(1)}, f32[1,2,64,128]{3,2,1,0:T(8,128)S(1)}, u32[]{:S(2)}, u32[]{:S(2)}) collective-permute-start(f32[1,2,64,128]{3,2,1,0:T(8,128)S(1)} %maximum_bitcast_fusion.2), channel_id=1, source_target_pairs={{4,0},{8,4},{12,8},{16,12},{20,16},{24,20},{28,24},{5,1},{9,5},{13... | collective-permute-start | bytes 196616 | tf_op jit(solution)/shard_map/ppermute | solution.py:23
  201.9 6.7 %collective-permute-start.4 = (f32[1,2,64,128]{3,2,1,0:T(8,128)S(1)}, f32[1,2,64,128]{3,2,1,0:T(8,128)S(1)}, u32[]{:S(2)}, u32[]{:S(2)}) collective-permute-start(f32[1,2,64,128]{3,2,1,0:T(8,128)S(1)} %maximum_bitcast_fusion.2), channel_id=1, source_target_pairs={{0,4},{4,8},{8,12},{12,16},{16,20},{20,24},{24,28},{1,5},{5,9},{9,... | collective-permute-start | bytes 196616 | tf_op jit(solution)/shard_map/ppermute | solution.py:21
where the time goes:
time: 271 us; the launch traced here: 270 us
  blocking collectives  207 us (76%)
  starting transfers between devices  19 us (7%)
  other arithmetic  13.6 us (5%)
  between operations  12.1 us (4%)
  local copies, waits for them, and re-layouts  8.65 us (3%)
  matrix products  7.16 us (3%)
    psum x2, blocking collectives, on_device(): totals = lax.psum(local_terms, ('sub', 'grp'))  84.9 us
    unnamed x2, blocking collectives  80.4 us
    psum x1, blocking collectives, on_device(): beta = jnp.sqrt(lax.psum(jnp.sum(first * first), ('sub', 'grp')))  42.1 us
    ppermute x3, starting transfers between devices, extended(): lax.ppermute(tail, axis, [(i, (i + 1) % count) for i in range(ends)])  15.1 us
  transfers between devices with their start and end apart: 6, of which 2 were waited for; matrix products, arithmetic and copies ran while one was open for 3% of the time, Pallas kernels for 0%

commit v1 on v0

v1 whole, which is shorter than its diff:
```python
import functools
import math

import jax
import jax.numpy as jnp
from jax import lax
from jax.experimental import pallas as pl
from jax.experimental.pallas import tpu as pltpu
from jax.sharding import PartitionSpec as P

penalty_gain = 3.0
coupling = 0.5

LANES = 128
SLOT = 64
AXES = ("sub", "grp")
f32 = jnp.float32
bf16 = jnp.bfloat16


def call(body, outs, *args, smem=()):
    vmem = pl.BlockSpec(memory_space=pltpu.VMEM)
    scalars = pl.BlockSpec(memory_space=pltpu.SMEM)
    return pl.pallas_call(
        body,
        out_shape=[jax.ShapeDtypeStruct(shape, kind) for shape, kind in outs],
        in_specs=[scalars if at in smem else vmem for at in range(len(args))],
        out_specs=[vmem] * len(outs),
        compiler_params=pltpu.CompilerParams(vmem_limit_bytes=32 * 1024 * 1024),
    )(*args)


def pick(field, places):
    return jnp.take_along_axis(field, jnp.broadcast_to(places, field.shape), axis=1)


def pieces(field):
    high = field.astype(bf16)
    return high, (field - high.astype(f32)).astype(bf16)


def block_product(blocks_ref, field):
    rows = []
    for at in range(0, blocks_ref.shape[0], 8):
        part = blocks_ref[at : at + 8].astype(f32) * field[None]
        rows.append(jnp.sum(part, axis=1))
    return jnp.concatenate(rows, axis=0)


def received(below, above, arrive_ref):
    high, low = pieces(jnp.concatenate([below, above], axis=1))
    both = jnp.dot(
        jnp.concatenate([high, low], axis=0), arrive_ref[...], preferred_element_type=f32
    )
    count = below.shape[0]
    return both[:count] + both[count:]


def restricted(weighted, gather_ref):
    high = weighted.astype(bf16).astype(f32)
    rest = weighted - high
    middle = rest.astype(bf16).astype(f32)
    last = rest - middle
    row = lax.broadcasted_iota(jnp.int32, (8, weighted.shape[1]), 0)
    stack = jnp.where(row == 0, high, jnp.where(row == 1, middle, jnp.where(row == 2, last, 0.0)))
    sums = jnp.dot(stack.astype(bf16), gather_ref[...], preferred_element_type=f32)
    return jnp.sum(sums, axis=0, keepdims=True)


def total(field):
    value = jnp.sum(jnp.sum(field, axis=0, keepdims=True), axis=1, keepdims=True)
    return jnp.broadcast_to(value, (1, LANES))


def to_all(ref, parts):
    row = jnp.concatenate(parts, axis=1)
    ref[...] = jnp.broadcast_to(row, ref.shape)


def first_send(guess_ref, send_ref, up_ref, down_ref):
    guess = guess_ref[...]
    up_ref[...] = pick(guess, send_ref[0:1, :])
    down_ref[...] = pick(guess, send_ref[1:2, :])


def prepare(live_ref, guess_ref, rhs_ref, blocks_ref, valve_ref, agg_ref, recv_ref, cpd,
            local_ref, arrive_ref, gather_ref):
    guess = guess_ref[...]
    penalty = penalty_gain * valve_ref[...].astype(f32)
    local_ref[...] = rhs_ref[...] - (block_product(blocks_ref, guess) + penalty * guess)
    place = lax.axis_index("sub")
    ends = (place > 0, place < lax.axis_size("sub") - 1)
    count = arrive_ref.shape[1]
    slots = recv_ref.shape[1]
    row = lax.broadcasted_iota(jnp.int32, (count, slots), 0)
    slot = lax.broadcasted_iota(jnp.int32, (count, slots), 1)
    for side in (0, 1):
        live = jnp.where(ends[side], live_ref[0, side], 0)
        hit = (recv_ref[side : side + 1, :] == row) & (slot < live)
        arrive_ref[side * slots : (side + 1) * slots, :] = jnp.where(hit, 1.0, 0.0).T.astype(bf16)
    period = gather_ref.shape[1]
    coarse = lax.rem(lax.broadcasted_iota(jnp.int32, (period, count), 0), cpd)
    gather_ref[...] = jnp.where(agg_ref[...] == coarse, 1.0, 0.0).T.astype(bf16)


def residual(local_ref, below_ref, above_ref, arrive_ref, gather_ref, prolong_ref, jscale_ref,
             send_ref, agg_ref, cdiag_ref, first_ref, out_ref, up_ref, down_ref):
    first = local_ref[...] + coupling * received(below_ref[...], above_ref[...], arrive_ref)
    first_ref[...] = first
    prolong = prolong_ref[...]
    weighted = jnp.sum(prolong * first, axis=0, keepdims=True)
    to_all(out_ref, [restricted(weighted, gather_ref), total(first * first)])
    scaled = jscale_ref[...] * first
    size = first.shape[0]
    agg = jnp.broadcast_to(agg_ref[...].astype(f32), (8, LANES))
    cdiag = jnp.broadcast_to(cdiag_ref[...], (8, LANES))
    for side, ref in ((0, up_ref), (1, down_ref)):
        places = send_ref[side : side + 1, :]
        ref[0:size, :] = pick(scaled, places)
        ref[size : 2 * size, :] = pick(prolong, places)
        ref[2 * size : 2 * size + 8, :] = pick(agg, places)
        ref[2 * size + 8 : 2 * size + 16, :] = cdiag


def own_rows(ref_value, grp_size):
    count = ref_value.shape[0]
    me = lax.axis_index("sub") * grp_size + lax.axis_index("grp")
    return [lax.rem(me + shift + count, count) for shift in (0, -grp_size, grp_size)]


def coarse_solve(coarse_ref, cpd, grp_size, coff_refs, cdiags):
    count, period = coarse_ref.shape
    group = period // cpd
    owner = lax.broadcasted_iota(jnp.int32, (group, period), 1) // cpd
    mask = owner == lax.broadcasted_iota(jnp.int32, (group, period), 0)
    value = jnp.concatenate(
        [
            jnp.where(mask, coarse_ref[at : at + group, :], 0.0)
            for at in range(0, count, group)
        ],
        axis=1,
    ).astype(bf16)
    filler = jnp.zeros((SLOT - cpd, coff_refs[0].shape[1]), bf16)
    matrix = jnp.concatenate([part for ref in coff_refs for part in (ref[...], filler)], axis=0)
    product = lax.dot_general(
        value, matrix, (((1,), (1,)), ((), ())), preferred_element_type=f32
    )
    product = jnp.sum(product, axis=0, keepdims=True)
    product = jnp.concatenate([product, jnp.zeros((1, SLOT), f32)], axis=1)
    low, top = product[:, :LANES], product[:, LANES:]
    shares = [low, pltpu.roll(jnp.broadcast_to(low, (8, LANES)), SLOT, 1)[0:1], top]
    result = []
    head = coarse_ref[:, 0:LANES]
    place = lax.broadcasted_iota(jnp.int32, head.shape, 0)
    for row, cdiag, share in zip(own_rows(coarse_ref, grp_size), cdiags, shares):
        coarse = jnp.sum(jnp.where(place == row, head, 0.0), axis=0, keepdims=True)
        result.append(cdiag * coarse + share)
    return result


def spread_of(solution, agg):
    wide = jnp.broadcast_to(solution, (8, LANES))
    return jnp.take_along_axis(wide, jnp.broadcast_to(agg, (8, LANES)), axis=1)[0:1]


def step_tail(direction, near, blocks_ref, valve_ref, arrive_ref):
    penalty = penalty_gain * valve_ref[...].astype(f32)
    image = block_product(blocks_ref, direction) + penalty * direction
    return image - coupling * received(near[0], near[1], arrive_ref)


def near_constants(ref, size):
    return (
        ref[size : 2 * size, :],
        ref[2 * size : 2 * size + 1, :].astype(jnp.int32),
        ref[2 * size + 8 : 2 * size + 9, :],
    )


def first_step(got_ref, below_ref, above_ref, coff_ref, coff_b_ref, coff_a_ref, cdiag_ref,
               first_ref, jscale_ref, prolong_ref, agg_ref, blocks_ref, valve_ref, arrive_ref,
               gather_ref, send_ref, cpd, grp_size,
               basis_ref, direction_ref, image_ref, coarse_ref, out_ref, up_ref, down_ref):
    size = first_ref.shape[0]
    period = coarse_ref.shape[1]
    sums = jnp.sum(got_ref[:, period : period + LANES], axis=0, keepdims=True)
    beta = jnp.sqrt(sums)
    for at in range(0, period, LANES):
        coarse_ref[:, at : at + LANES] = got_ref[:, at : at + LANES] / beta
    basis = first_ref[...] / beta
    basis_ref[...] = basis
    near = [near_constants(ref, size) for ref in (below_ref, above_ref)]
    solved = coarse_solve(coarse_ref, cpd, grp_size, (coff_ref, coff_b_ref, coff_a_ref),
                          [cdiag_ref[...]] + [item[2] for item in near])
    jscale, prolong = jscale_ref[...], prolong_ref[...]
    direction = jscale * basis + prolong * spread_of(solved[0], agg_ref[...])
    direction_ref[...] = direction
    fields = []
    for ref, (weights, agg, _), part in zip((below_ref, above_ref), near, solved[1:]):
        fields.append(ref[0:size, :] / beta + weights * spread_of(part, agg))
    image = step_tail(direction, fields, blocks_ref, valve_ref, arrive_ref)
    image_ref[...] = image
    weighted = jnp.sum(prolong * image, axis=0, keepdims=True)
    to_all(out_ref, [restricted(weighted, gather_ref), total(basis * image), total(image * image)])
    scaled = jscale * image
    up_ref[...] = pick(scaled, send_ref[0:1, :])
    down_ref[...] = pick(scaled, send_ref[1:2, :])


def second_step(got_ref, first_got_ref, below_ref, above_ref, below_first_ref, above_first_ref,
                coff_ref, coff_b_ref, coff_a_ref, cdiag_ref, basis_ref, image_ref, coarse_ref,
                jscale_ref, prolong_ref, agg_ref, blocks_ref, valve_ref, arrive_ref,
                cpd, grp_size,
                basis_two_ref, direction_ref, image_two_ref, scalars_ref, out_ref, work_ref):
    size = basis_ref.shape[0]
    period = coarse_ref.shape[1]
    beta = jnp.sqrt(jnp.sum(first_got_ref[:, period : period + LANES], axis=0, keepdims=True))
    totals = jnp.sum(got_ref[:, period : period + 2 * LANES], axis=0, keepdims=True)
    along, energy = totals[:, :LANES], totals[:, LANES:]
    height = jnp.sqrt(jnp.maximum(energy - along * along, 0.01 * energy))
    for at in range(0, period, LANES):
        work_ref[:, at : at + LANES] = (
            got_ref[:, at : at + LANES] - along * coarse_ref[:, at : at + LANES]
        ) / height
    basis = (image_ref[...] - along * basis_ref[...]) / height
    basis_two_ref[...] = basis
    near = [near_constants(ref, size) for ref in (below_first_ref, above_first_ref)]
    solved = coarse_solve(work_ref, cpd, grp_size, (coff_ref, coff_b_ref, coff_a_ref),
                          [cdiag_ref[...]] + [item[2] for item in near])
    direction = jscale_ref[...] * basis + prolong_ref[...] * spread_of(solved[0], agg_ref[...])
    direction_ref[...] = direction
    fields = []
    for ref, first_near, (weights, agg, _), part in zip(
        (below_ref, above_ref), (below_first_ref, above_first_ref), near, solved[1:]
    ):
        scaled = (ref[...] - along * (first_near[0:size, :] / beta)) / height
        fields.append(scaled + weights * spread_of(part, agg))
    image = step_tail(direction, fields, blocks_ref, valve_ref, arrive_ref)
    image_two_ref[...] = image
    scalars_ref[0:1, :] = beta
    scalars_ref[1:2, :] = along
    scalars_ref[2:3, :] = height
    scalars_ref[3:8, :] = jnp.zeros((5, LANES), f32)
    to_all(out_ref, [total(basis_ref[...] * image), total(basis * image), total(image * image)])


def finish(got_ref, scalars_ref, guess_ref, basis_ref, basis_two_ref, direction_ref,
           direction_two_ref, image_ref, solution_ref, next_ref):
    beta, h11, h21 = scalars_ref[0:1, :], scalars_ref[1:2, :], scalars_ref[2:3, :]
    totals = jnp.sum(got_ref[...], axis=0, keepdims=True)
    h12, h22, energy = totals[:, :LANES], totals[:, LANES : 2 * LANES], totals[:, 2 * LANES :]
    h32 = jnp.sqrt(jnp.maximum(energy - (h12 * h12 + h22 * h22), 0.01 * energy))
    g00 = h11 * h11 + h21 * h21
    g01 = h11 * h12 + h21 * h22
    g11 = h12 * h12 + h22 * h22 + h32 * h32
    t0, t1 = beta * h11, beta * h12
    factor = g01 / g00
    c1 = (t1 - factor * t0) / (g11 - factor * g01)
    c0 = (t0 - g01 * c1) / g00
    solution_ref[...] = guess_ref[...] + c0 * direction_ref[...] + c1 * direction_two_ref[...]
    next_ref[...] = (image_ref[...] - h12 * basis_ref[...] - h22 * basis_two_ref[...]) / h32


def on_device(rhs, guess, blocks, valve, jscale, prolong, agg_map, cdiag, coff, send_rows,
              recv_rows, live_counts):
    rhs, guess, blocks, jscale, prolong = rhs[0, 0], guess[0, 0], blocks[0, 0], jscale[0, 0], prolong[0, 0]
    valve, agg, live = valve[0], agg_map[0], live_counts[0]
    send, recv = send_rows[0, 0], recv_rows[0, 0]
    size, count = guess.shape
    slots = send.shape[1]
    cpd = cdiag.shape[0]
    subs, grps = lax.axis_size("sub"), lax.axis_size("grp")
    devices = subs * grps
    period = math.lcm(cpd, LANES)
    cdiag_row = jnp.pad(cdiag[None, :], ((0, 0), (0, LANES - cpd)))
    upward = [(at, (at + 1) % subs) for at in range(subs)]
    downward = [((at + 1) % subs, at) for at in range(subs)]

    def exchange(up, down):
        return lax.ppermute(up, "sub", upward), lax.ppermute(down, "sub", downward)

    def everyone(rows):
        return lax.all_to_all(rows, AXES, 0, 0, tiled=True)

    field = ((size, count), f32)
    near = ((size, slots), f32)
    up, down = call(first_send, [near, near], guess, send)
    below, above = exchange(up, down)
    coff_below, coff_above = exchange(coff, coff)
    local, arrive, gather = call(
        lambda *refs: prepare(*refs[:7], cpd, *refs[7:]),
        [field, ((2 * slots, count), bf16), ((count, period), bf16)],
        live, guess, rhs, blocks, valve, agg, recv, smem=(0,),
    )
    packed = ((2 * size + 16, slots), f32)
    first, rows, up, down = call(
        residual,
        [field, ((devices, period + LANES), f32), packed, packed],
        local, below, above, arrive, gather, prolong, jscale, send, agg, cdiag_row,
    )
    below_first, above_first = exchange(up, down)
    first_got = everyone(rows)
    basis, direction, image, coarse, rows, up, down = call(
        lambda *refs: first_step(*refs[:16], cpd, grps, *refs[16:]),
        [field, field, field, ((devices, period), f32), ((devices, period + 2 * LANES), f32), near, near],
        first_got, below_first, above_first, coff, coff_below, coff_above, cdiag_row, first, jscale,
        prolong, agg, blocks, valve, arrive, gather, send,
    )
    below, above = exchange(up, down)
    got = everyone(rows)
    basis_two, direction_two, image_two, scalars, rows, _ = call(
        lambda *refs: second_step(*refs[:19], cpd, grps, *refs[19:]),
        [field, field, field, ((8, LANES), f32), ((devices, 3 * LANES), f32), ((devices, period), f32)],
        got, first_got, below, above, below_first, above_first, coff, coff_below, coff_above,
        cdiag_row, basis, image, coarse, jscale, prolong, agg, blocks, valve, arrive,
    )
    got = everyone(rows)
    solution, next_basis = call(
        finish, [field, field],
        got, scalars, guess, basis, basis_two, direction, direction_two, image_two,
    )
    return solution[None, None], next_basis[None, None]


def solution(mesh):
    return jax.shard_map(
        on_device,
        mesh=mesh,
        in_specs=(
            P("sub", "grp", None, None),
            P("sub", "grp", None, None),
            P("sub", "grp", None, None, None),
            P("sub", "grp", None),
            P("sub", "grp", None, None),
            P("sub", "grp", None, None),
            P("sub", "grp", None),
            P(("sub", "grp")),
            P(("sub", "grp"), None),
            P("sub", "grp", None, None),
            P("sub", "grp", None, None),
            P("sub", "grp", None),
        ),
        out_specs=(P("sub", "grp", None, None), P("sub", "grp", None, None)),
        check_vma=False,
    )
```

time: 271 us -> 58.6 us (0.22)
  blocking collectives: 207 us -> 12.3 us
  other arithmetic: 13.6 us -> 0 us
  between operations: 12.1 us -> 0.79 us
  starting transfers between devices: 19 us -> 28.7 us
  matrix products: 7.16 us -> 0 us
  waiting for transfers between devices: 1.88 us -> 6.58 us
  Pallas kernels: 0 us -> 4.26 us
  local copies, waits for them, and re-layouts: 8.65 us -> 5.59 us
    psum x3 -> x0, blocking collectives: 127 us -> none  [the longest x2 84.9 us: on_device(): totals = lax.psum(local_terms, ('sub', 'grp'))]
    unnamed x2 -> x0, blocking collectives: 80.4 us -> none
    all_to_all x0 -> x1, blocking collectives: none -> 12.3 us  [everyone(): return lax.all_to_all(rows, AXES, 0, 0, tiled=True)]
    all_to_all x0 -> x2, starting transfers between devices: none -> 11 us  [everyone(): return lax.all_to_all(rows, AXES, 0, 0, tiled=True)]
    dot_general x19 -> x0, matrix products: 7.16 us -> none  [the longest x3 2.67 us: operate(): jnp.dot(below, recv_sel[0], precision=highest)]
    all_to_all x0 -> x2, waiting for transfers between devices: none -> 5.91 us  [everyone(): return lax.all_to_all(rows, AXES, 0, 0, tiled=True)]
    another operation x4 -> x0, other arithmetic: 5.91 us -> none  [the longest x2 3.33 us: on_device(): jnp.stack([jnp.sum(vector * image) for vector in basis] + [jnp.sum(image...]
    pallas_call x0 -> x6, Pallas kernels: none -> 4.26 us  [call(): pl.pallas_call(body, out_shape=[jax.ShapeDtypeStruct(shape, kind) for sha...]
  transfers between devices with their start and end apart: 6 -> 10, of which waited for: 2 -> 3; matrix products, arithmetic and copies ran while one was open for 3% -> 1% of each run, Pallas kernels for 0% -> 2%
where the time goes in v1:
time: 58.6 us; the launch traced here: 58.2 us
  starting transfers between devices  28.7 us (49%)
  blocking collectives  12.3 us (21%)
  waiting for transfers between devices  6.58 us (11%)
  local copies, waits for them, and re-layouts  5.59 us (10%)
  Pallas kernels  4.26 us (7%)
  between operations  0.79 us (1%)
    all_to_all x1, blocking collectives, everyone(): return lax.all_to_all(rows, AXES, 0, 0, tiled=True)  12.3 us
    all_to_all x2, starting transfers between devices, everyone(): return lax.all_to_all(rows, AXES, 0, 0, tiled=True)  11 us
    ppermute x4, starting transfers between devices, exchange(): lax.ppermute(down, 'sub', downward)  11 us
    ppermute x4, starting transfers between devices, exchange(): lax.ppermute(up, 'sub', upward)  6.71 us
    all_to_all x2, waiting for transfers between devices, everyone(): return lax.all_to_all(rows, AXES, 0, 0, tiled=True)  5.91 us
    pallas_call x6, Pallas kernels, call(): pl.pallas_call(body, out_shape=[jax.ShapeDtypeStruct(shape, kind) for sha...  4.26 us
    unnamed x31, local copies, waits for them, and re-layouts  4.11 us
    all_to_all x3, local copies, waits for them, and re-layouts, everyone(): return lax.all_to_all(rows, AXES, 0, 0, tiled=True)  1.48 us
  transfers between devices with their start and end apart: 10, of which 3 were waited for; matrix products, arithmetic and copies ran while one was open for 1% of the time, Pallas kernels for 2%

profile of v1, /device:TPU:0, one launch (start us, length us, event | category | flops | bytes accessed | tf_op | source)
XLA Modules:
  0.0 58.2 jit_solution(8634469214371541281)
XLA Ops:
  0.6 0.0 copy-start.8
  0.6 0.7 %copy-done.8 = s32[1,1,2,128]{3,2,1,0:T(2,128)S(1)} copy-done((s32[1,1,2,128]{3,2,1,0:T(2,128)S(1)}, s32[1,1,2,128]{3,2,1,0:T(2,128)}, u32[]{:S(2)}) %copy-start.8) | copy-done | bytes 1048
  1.3 0.8 %copy-done.5 = f32[1,1,64,128]{3,2,1,0:T(8,128)S(1)} copy-done((f32[1,1,64,128]{3,2,1,0:T(8,128)S(1)}, f32[1,1,64,128]{3,2,1,0:T(8,128)}, u32[]{:S(2)}) %copy-start.5) | copy-done | bytes 32792
  2.1 0.1 shard_map.132
  2.1 3.0 %collective-permute-start = (f32[64,128]{1,0:T(8,128)S(1)}, f32[64,128]{1,0:T(8,128)S(1)}, u32[]{:S(2)}, u32[]{:S(2)}) collective-permute-start(f32[64,128]{1,0:T(8,128)S(1)} %get-tuple-element.26), channel_id=1, source_target_pairs={{0,4},{4,8},{8,12},{12,16},{16,20},{20,24},{24,28},{28,0},{1,5},{5... | collective-permute-start | bytes 98312 | tf_op jit(solution)/shard_map/ppermute | solution.py:280
  5.1 3.1 %collective-permute-start.1 = (f32[64,128]{1,0:T(8,128)S(1)}, f32[64,128]{1,0:T(8,128)S(1)}, u32[]{:S(2)}, u32[]{:S(2)}) collective-permute-start(f32[64,128]{1,0:T(8,128)S(1)} %get-tuple-element.27), channel_id=1, source_target_pairs={{4,0},{8,4},{12,8},{16,12},{20,16},{24,20},{28,24},{0,28},{5,1},{9... | collective-permute-start | bytes 98312 | tf_op jit(solution)/shard_map/ppermute | solution.py:280
  8.3 1.9 %collective-permute-start.5 = (bf16[48,1536]{1,0:T(8,128)(2,1)}, bf16[48,1536]{1,0:T(8,128)(2,1)S(1)}, u32[]{:S(2)}, u32[]{:S(2)}) collective-permute-start(bf16[48,1536]{1,0:T(8,128)(2,1)} %refs_6_.1), channel_id=1, source_target_pairs={{4,0},{8,4},{12,8},{16,12},{20,16},{24,20},{28,24},{0,28},{5,1},{9... | collective-permute-start | bytes 442376 | tf_op jit(solution)/shard_map/ppermute | solution.py:280
  10.2 0.1 collective-permute-start.4
  10.3 0.0 copy-done.13
  10.3 0.0 copy-start.9
  10.3 0.0 copy-start.10
  10.3 0.0 copy-start.12
  10.3 0.0 copy-done.6
  10.3 0.6 %copy-done.11 = s32[1,1,2,128]{3,2,1,0:T(2,128)S(1)} copy-done((s32[1,1,2,128]{3,2,1,0:T(2,128)S(1)}, s32[1,1,2,128]{3,2,1,0:T(2,128)}, u32[]{:S(2)}) %copy-start.11) | copy-done | bytes 1048
  11.0 0.0 copy-done.9
  11.0 0.0 copy-done.10
  11.0 0.0 copy-done.12
  11.0 1.2 %copy-done = bf16[1,1,64,64,128]{4,3,2,1,0:T(8,128)(2,1)S(1)} copy-done((bf16[1,1,64,64,128]{4,3,2,1,0:T(8,128)(2,1)S(1)}, bf16[1,1,64,64,128]{4,3,2,1,0:T(8,128)(2,1)}, u32[]{:S(2)}) %copy-start) | copy-done | bytes 1048600
  12.2 0.8 %copy-done.7 = f32[1,1,64,128]{3,2,1,0:T(8,128)S(1)} copy-done((f32[1,1,64,128]{3,2,1,0:T(8,128)S(1)}, f32[1,1,64,128]{3,2,1,0:T(8,128)}, u32[]{:S(2)}) %copy-start.7) | copy-done | bytes 32792
  13.0 0.9 %shard_map.131 = (f32[64,128]{1,0:T(8,128)S(1)}, bf16[256,128]{1,0:T(8,128)(2,1)S(1)}, bf16[128,384]{1,0:T(8,128)(2,1)S(1)}) custom-call(s32[1,2]{1,0:T(1,128)S(1)} %bitcast.56, f32[64,128]{1,0:T(8,128)S(1)} %bitcast.38, f32[64,128]{1,0:T(8,128)S(1)} %bitcast.44, bf16[64,64,128]{2,1,0:T(8,128)(2,1)S(1)} %bitcast.25, s32[1,128]{1,0:T(1,128)S(1)} %bitcast.52, ...), custom_call_target="tpu_custom_call" | custom-call | tf_op jit(solution)/shard_map/pallas_call | solution.py:24
  13.9 0.0 collective-permute-done.below_ref
  13.9 0.0 collective-permute-done.1.above_ref
  13.9 0.0 copy-done.3
  13.9 0.0 copy-done.4
  13.9 0.3 shard_map.133
  14.3 0.7 %copy.14 = f32[32,1,512]{2,1,0:T(1,128)} copy(f32[32,1,512]{2,0,1:T(8,128)S(1)} %bitcast.42) | data formatting | bytes 131072 | tf_op jit(solution)/shard_map/all_to_all | solution.py:283
  15.0 5.9 %all-to-all-start = ((f32[32,1,512]{2,1,0:T(1,128)}), f32[32,1,512]{2,1,0:T(1,128)S(1)}, u32[]{:S(2)}, u32[]{:S(2)}) async-start(f32[32,1,512]{2,1,0:T(1,128)} %copy.14), calls=%async_computation | async-start | bytes 131072 | tf_op jit(solution)/shard_map/all_to_all | solution.py:283
  20.9 1.8 %collective-permute-start.2 = (f32[144,128]{1,0:T(8,128)S(1)}, f32[144,128]{1,0:T(8,128)S(1)}, u32[]{:S(2)}, u32[]{:S(2)}) collective-permute-start(f32[144,128]{1,0:T(8,128)S(1)} %get-tuple-element.31), channel_id=1, source_target_pairs={{0,4},{4,8},{8,12},{12,16},{16,20},{20,24},{24,28},{28,0},{1,5},{5... | collective-permute-start | bytes 221192 | tf_op jit(solution)/shard_map/ppermute | solution.py:280
  22.7 3.0 %collective-permute-start.3 = (f32[144,128]{1,0:T(8,128)S(1)}, f32[144,128]{1,0:T(8,128)S(1)}, u32[]{:S(2)}, u32[]{:S(2)}) collective-permute-start(f32[144,128]{1,0:T(8,128)S(1)} %get-tuple-element.32), channel_id=1, source_target_pairs={{4,0},{8,4},{12,8},{16,12},{20,16},{24,20},{28,24},{0,28},{5,1},{9... | collective-permute-start | bytes 221192 | tf_op jit(solution)/shard_map/ppermute | solution.py:280
  25.7 2.9 %all-to-all-done = f32[32,1,512]{2,1,0:T(1,128)S(1)} async-done(((f32[32,1,512]{2,1,0:T(1,128)}), f32[32,1,512]{2,1,0:T(1,128)S(1)}, u32[]{:S(2)}, u32[]{:S(2)}) %all-to-all-start) | async-done | bytes 65568 | tf_op jit(solution)/shard_map/all_to_all | solution.py:283
  28.6 0.7 %collective-permute-done.2.refs_1_.refs_4_ = f32[144,128]{1,0:T(8,128)S(1)} collective-permute-done((f32[144,128]{1,0:T(8,128)S(1)}, f32[144,128]{1,0:T(8,128)S(1)}, u32[]{:S(2)}, u32[]{:S(2)}) %collective-permute-start.2) | collective-permute-done | bytes 73760 | tf_op jit(solution)/shard_map/ppermute | solution.py:280
  29.2 0.0 collective-permute-done.3.refs_2_.refs_5_
  29.2 0.0 collective-permute-done.5.refs_5_.refs_8_
  29.2 0.0 collective-permute-done.4.refs_4_.refs_7_
  29.3 0.0 copy-done.1
  29.3 0.0 copy-done.2
  29.3 0.9 %shard_map.134 = (f32[64,128]{1,0:T(8,128)S(1)}, f32[64,128]{1,0:T(8,128)S(1)}, f32[64,128]{1,0:T(8,128)S(1)}, f32[32,384]{1,0:T(8,128)S(1)}, f32[32,640]{1,0:T(...) custom-call(f32[32,512]{1,0:T(8,128)S(1)} %bitcast.28, f32[144,128]{1,0:T(8,128)S(1)} %collective-permute-done.2.refs_1_.refs_4_, ...), custom_call_target="tpu_custom_call" | custom-call | tf_op jit(solution)/shard_map/pallas_call | solution.py:24
  30.2 0.7 %copy.15 = f32[32,1,640]{2,1,0:T(1,128)} copy(f32[32,1,640]{2,0,1:T(8,128)S(1)} %bitcast.41) | data formatting | bytes 163840 | tf_op jit(solution)/shard_map/all_to_all | solution.py:283
  30.9 5.1 %all-to-all-start.1 = ((f32[32,1,640]{2,1,0:T(1,128)}), f32[32,1,640]{2,1,0:T(1,128)S(1)}, u32[]{:S(2)}, u32[]{:S(2)}) async-start(f32[32,1,640]{2,1,0:T(1,128)} %copy.15), calls=%async_computation.1 | async-start | bytes 163840 | tf_op jit(solution)/shard_map/all_to_all | solution.py:283
  36.0 1.8 %collective-permute-start.6 = (f32[64,128]{1,0:T(8,128)S(1)}, f32[64,128]{1,0:T(8,128)S(1)}, u32[]{:S(2)}, u32[]{:S(2)}) collective-permute-start(f32[64,128]{1,0:T(8,128)S(1)} %get-tuple-element.35), channel_id=1, source_target_pairs={{0,4},{4,8},{8,12},{12,16},{16,20},{20,24},{24,28},{28,0},{1,5},{5... | collective-permute-start | bytes 98312 | tf_op jit(solution)/shard_map/ppermute | solution.py:280
  37.8 3.0 %collective-permute-start.7 = (f32[64,128]{1,0:T(8,128)S(1)}, f32[64,128]{1,0:T(8,128)S(1)}, u32[]{:S(2)}, u32[]{:S(2)}) collective-permute-start(f32[64,128]{1,0:T(8,128)S(1)} %get-tuple-element.36), channel_id=1, source_target_pairs={{4,0},{8,4},{12,8},{16,12},{20,16},{24,20},{28,24},{0,28},{5,1},{9... | collective-permute-start | bytes 98312 | tf_op jit(solution)/shard_map/ppermute | solution.py:280
  40.8 3.0 %all-to-all-done.1 = f32[32,1,640]{2,1,0:T(1,128)S(1)} async-done(((f32[32,1,640]{2,1,0:T(1,128)}), f32[32,1,640]{2,1,0:T(1,128)S(1)}, u32[]{:S(2)}, u32[]{:S(2)}) %all-to-all-start.1) | async-done | bytes 81952 | tf_op jit(solution)/shard_map/all_to_all | solution.py:283
  43.8 0.0 collective-permute-done.6.refs_2_
  43.8 0.0 collective-permute-done.7.refs_3_
  43.8 1.4 %shard_map.135 = (f32[64,128]{1,0:T(8,128)S(1)}, f32[64,128]{1,0:T(8,128)S(1)}, f32[64,128]{1,0:T(8,128)S(1)}, f32[8,128]{1,0:T(8,128)S(1)}, f32[32,384]{1,0:T(8,128)S(1)}, /*index=5*/f32[32,384]{1,0:T(8,128)}) custom-call(f32[32,640]{1,0:T(8,128)S(1)} %bitcast.30, f32[32,512]{1,0:T(8,128)S(1)} %bitcast.29, f32[64,128]{1,0:T(8,128)S(1)} %collective-permute-done.6.refs_2_, ...), custom_call_target="tpu_custom_call" | custom-call | tf_op jit(solution)/shard_map/pallas_call | solution.py:24
  45.2 0.1 copy.16
  45.2 12.3 %all_to_all.33 = f32[32,1,384]{2,1,0:T(1,128)S(1)} all-to-all(f32[32,1,384]{2,1,0:T(1,128)S(1)} %copy.16), channel_id=1, replica_groups=mesh['sub'=8,'grp'=4] {'sub','grp'}, dimensions={0} | all-to-all | bytes 98304 | tf_op jit(solution)/shard_map/all_to_all | solution.py:283
  57.5 0.7 %shard_map.136 = (f32[64,128]{1,0:T(8,128)}, f32[64,128]{1,0:T(8,128)}) custom-call(f32[32,384]{1,0:T(8,128)S(1)} %bitcast.40, f32[8,128]{1,0:T(8,128)S(1)} %get-tuple-element.41.scalars_ref, f32[64,128]{1,0:T(8,128)S(1)} %bitcast.39, f32[64,128]{1,0:T(8,128)S(1)} %get-tuple-element.37.refs_10_.basis_ref, f32[64,128]{1,0:T(8,128)S(1)} %get-tuple-element.42.basis_two_ref, ...), custom_call_target="tpu_custom_call" | custom-call | tf_op jit(solution)/shard_map/pallas_call | solution.py:24
  (14 shorter events, 0.0 us)
Async XLA Ops:
  0.6 0.7 %copy-start.8 = (s32[1,1,2,128]{3,2,1,0:T(2,128)S(1)}, s32[1,1,2,128]{3,2,1,0:T(2,128)}, u32[]{:S(2)}) copy-start(s32[1,1,2,128]{3,2,1,0:T(2,128)} %param.21) | copy-start | bytes 3076
  1.3 0.8 %copy-start.5 = (f32[1,1,64,128]{3,2,1,0:T(8,128)S(1)}, f32[1,1,64,128]{3,2,1,0:T(8,128)}, u32[]{:S(2)}) copy-start(f32[1,1,64,128]{3,2,1,0:T(8,128)} %param.13) | copy-start | bytes 98308
  2.1 8.3 %copy-start.6 = (f32[1,1,64,128]{3,2,1,0:T(8,128)S(1)}, f32[1,1,64,128]{3,2,1,0:T(8,128)}, u32[]{:S(2)}) copy-start(f32[1,1,64,128]{3,2,1,0:T(8,128)} %param.13) | copy-start | bytes 98308
  2.1 11.8 %collective-permute-start = (f32[64,128]{1,0:T(8,128)S(1)}, f32[64,128]{1,0:T(8,128)S(1)}, u32[]{:S(2)}, u32[]{:S(2)}) collective-permute-start(f32[64,128]{1,0:T(8,128)S(1)} %get-tuple-element.26), channel_id=1, source_target_pairs={{0,4},{4,8},{8,12},{12,16},{16,20},{20,24},{24,28},{28,0},{1,5},{5... | collective-permute-start | bytes 98312 | tf_op jit(solution)/shard_map/ppermute | solution.py:280
  5.1 5.1 %copy-start.13 = (f32[48]{0:T(128)S(1)}, f32[48]{0:T(128)}, u32[]{:S(2)}) copy-start(f32[48]{0:T(128)} %param.19) | copy-start | bytes 580
  5.1 8.8 %collective-permute-start.1 = (f32[64,128]{1,0:T(8,128)S(1)}, f32[64,128]{1,0:T(8,128)S(1)}, u32[]{:S(2)}, u32[]{:S(2)}) collective-permute-start(f32[64,128]{1,0:T(8,128)S(1)} %get-tuple-element.27), channel_id=1, source_target_pairs={{4,0},{8,4},{12,8},{16,12},{20,16},{24,20},{28,24},{0,28},{5,1},{9... | collective-permute-start | bytes 98312 | tf_op jit(solution)/shard_map/ppermute | solution.py:280
  8.3 21.0 %collective-permute-start.5 = (bf16[48,1536]{1,0:T(8,128)(2,1)}, bf16[48,1536]{1,0:T(8,128)(2,1)S(1)}, u32[]{:S(2)}, u32[]{:S(2)}) collective-permute-start(bf16[48,1536]{1,0:T(8,128)(2,1)} %refs_6_.1), channel_id=1, source_target_pairs={{4,0},{8,4},{12,8},{16,12},{20,16},{24,20},{28,24},{0,28},{5,1},{9... | collective-permute-start | bytes 442376 | tf_op jit(solution)/shard_map/ppermute | solution.py:280
  10.2 19.0 %collective-permute-start.4 = (bf16[48,1536]{1,0:T(8,128)(2,1)}, bf16[48,1536]{1,0:T(8,128)(2,1)S(1)}, u32[]{:S(2)}, u32[]{:S(2)}) collective-permute-start(bf16[48,1536]{1,0:T(8,128)(2,1)} %refs_6_.1), channel_id=1, source_target_pairs={{0,4},{4,8},{8,12},{12,16},{16,20},{20,24},{24,28},{28,0},{1,5},{5... | collective-permute-start | bytes 442376 | tf_op jit(solution)/shard_map/ppermute | solution.py:280
  10.3 0.7 %copy-start.11 = (s32[1,1,2,128]{3,2,1,0:T(2,128)S(1)}, s32[1,1,2,128]{3,2,1,0:T(2,128)}, u32[]{:S(2)}) copy-start(s32[1,1,2,128]{3,2,1,0:T(2,128)} %param.22) | copy-start | bytes 3076
  10.3 0.7 %copy-start.9 = (s32[1,1,128]{2,1,0:T(1,128)S(1)}, s32[1,1,128]{2,1,0:T(1,128)}, u32[]{:S(2)}) copy-start(s32[1,1,128]{2,1,0:T(1,128)} %param.18) | copy-start | bytes 1540
  10.3 0.7 %copy-start.10 = (s32[1,1,128]{2,1,0:T(1,128)S(1)}, s32[1,1,128]{2,1,0:T(1,128)}, u32[]{:S(2)}) copy-start(s32[1,1,128]{2,1,0:T(1,128)} %param.15) | copy-start | bytes 1540
  10.3 0.7 %copy-start.12 = (s32[1,1,2]{2,1,0:T(1,128)S(1)}, s32[1,1,2]{2,1,0:T(1,128)}, u32[]{:S(2)}) copy-start(s32[1,1,2]{2,1,0:T(1,128)} %param.23) | copy-start | bytes 28
  11.0 1.2 %copy-start = (bf16[1,1,64,64,128]{4,3,2,1,0:T(8,128)(2,1)S(1)}, bf16[1,1,64,64,128]{4,3,2,1,0:T(8,128)(2,1)}, u32[]{:S(2)}) copy-start(bf16[1,1,64,64,128]{4,3,2,1,0:T(8,128)(2,1)} %param.14) | copy-start | bytes 3145732
  12.2 0.8 %copy-start.7 = (f32[1,1,64,128]{3,2,1,0:T(8,128)S(1)}, f32[1,1,64,128]{3,2,1,0:T(8,128)}, u32[]{:S(2)}) copy-start(f32[1,1,64,128]{3,2,1,0:T(8,128)} %param.12) | copy-start | bytes 98308
  13.0 0.9 %copy-start.3 = (f32[1,1,64,128]{3,2,1,0:T(8,128)S(1)}, f32[1,1,64,128]{3,2,1,0:T(8,128)}, u32[]{:S(2)}) copy-start(f32[1,1,64,128]{3,2,1,0:T(8,128)} %param.17) | copy-start | bytes 98308
  13.0 1.0 %copy-start.4 = (f32[1,1,64,128]{3,2,1,0:T(8,128)S(1)}, f32[1,1,64,128]{3,2,1,0:T(8,128)}, u32[]{:S(2)}) copy-start(f32[1,1,64,128]{3,2,1,0:T(8,128)} %param.16) | copy-start | bytes 98308
  13.0 16.3 %copy-start.1 = (bf16[1,1,64,64,128]{4,3,2,1,0:T(8,128)(2,1)S(1)}, bf16[1,1,64,64,128]{4,3,2,1,0:T(8,128)(2,1)}, u32[]{:S(2)}) copy-start(bf16[1,1,64,64,128]{4,3,2,1,0:T(8,128)(2,1)} %param.14) | copy-start | bytes 3145732
  15.0 14.3 %copy-start.2 = (bf16[48,1536]{1,0:T(8,128)(2,1)S(1)}, bf16[48,1536]{1,0:T(8,128)(2,1)}, u32[]{:S(2)}) copy-start(bf16[48,1536]{1,0:T(8,128)(2,1)} %refs_6_.1) | copy-start | bytes 442372
  15.0 13.6 %all-to-all-start = ((f32[32,1,512]{2,1,0:T(1,128)}), f32[32,1,512]{2,1,0:T(1,128)S(1)}, u32[]{:S(2)}, u32[]{:S(2)}) async-start(f32[32,1,512]{2,1,0:T(1,128)} %copy.14), calls=%async_computation | async-start | bytes 131072 | tf_op jit(solution)/shard_map/all_to_all | solution.py:283
  20.9 8.3 %collective-permute-start.2 = (f32[144,128]{1,0:T(8,128)S(1)}, f32[144,128]{1,0:T(8,128)S(1)}, u32[]{:S(2)}, u32[]{:S(2)}) collective-permute-start(f32[144,128]{1,0:T(8,128)S(1)} %get-tuple-element.31), channel_id=1, source_target_pairs={{0,4},{4,8},{8,12},{12,16},{16,20},{20,24},{24,28},{28,0},{1,5},{5... | collective-permute-start | bytes 221192 | tf_op jit(solution)/shard_map/ppermute | solution.py:280
  22.7 6.5 %collective-permute-start.3 = (f32[144,128]{1,0:T(8,128)S(1)}, f32[144,128]{1,0:T(8,128)S(1)}, u32[]{:S(2)}, u32[]{:S(2)}) collective-permute-start(f32[144,128]{1,0:T(8,128)S(1)} %get-tuple-element.32), channel_id=1, source_target_pairs={{4,0},{8,4},{12,8},{16,12},{20,16},{24,20},{28,24},{0,28},{5,1},{9... | collective-permute-start | bytes 221192 | tf_op jit(solution)/shard_map/ppermute | solution.py:280
  30.9 12.9 %all-to-all-start.1 = ((f32[32,1,640]{2,1,0:T(1,128)}), f32[32,1,640]{2,1,0:T(1,128)S(1)}, u32[]{:S(2)}, u32[]{:S(2)}) async-start(f32[32,1,640]{2,1,0:T(1,128)} %copy.15), calls=%async_computation.1 | async-start | bytes 163840 | tf_op jit(solution)/shard_map/all_to_all | solution.py:283
  36.0 7.8 %collective-permute-start.6 = (f32[64,128]{1,0:T(8,128)S(1)}, f32[64,128]{1,0:T(8,128)S(1)}, u32[]{:S(2)}, u32[]{:S(2)}) collective-permute-start(f32[64,128]{1,0:T(8,128)S(1)} %get-tuple-element.35), channel_id=1, source_target_pairs={{0,4},{4,8},{8,12},{12,16},{16,20},{20,24},{24,28},{28,0},{1,5},{5... | collective-permute-start | bytes 98312 | tf_op jit(solution)/shard_map/ppermute | solution.py:280
  37.8 6.0 %collective-permute-start.7 = (f32[64,128]{1,0:T(8,128)S(1)}, f32[64,128]{1,0:T(8,128)S(1)}, u32[]{:S(2)}, u32[]{:S(2)}) collective-permute-start(f32[64,128]{1,0:T(8,128)S(1)} %get-tuple-element.36), channel_id=1, source_target_pairs={{4,0},{8,4},{12,8},{16,12},{20,16},{24,20},{28,24},{0,28},{5,1},{9... | collective-permute-start | bytes 98312 | tf_op jit(solution)/shard_map/ppermute | solution.py:280

commit v2 on v1

v2 whole, which is shorter than its diff:
```python
import math

import jax
import jax.numpy as jnp
from jax import lax
from jax.experimental import pallas as pl
from jax.experimental.pallas import tpu as pltpu
from jax.sharding import PartitionSpec as P

penalty_gain = 3.0
coupling = 0.5

LANES = 128
SLOT = 64
AXES = ("sub", "grp")
f32 = jnp.float32
bf16 = jnp.bfloat16


def call(body, outs, *args, smem=(), hbm=(), scratch=(), limit=32):
    def spec(at):
        if at in hbm:
            return pl.BlockSpec(memory_space=pl.ANY)
        return pl.BlockSpec(memory_space=pltpu.SMEM if at in smem else pltpu.VMEM)

    return pl.pallas_call(
        body,
        out_shape=[jax.ShapeDtypeStruct(shape, kind) for shape, kind in outs],
        in_specs=[spec(at) for at in range(len(args))],
        out_specs=[pl.BlockSpec(memory_space=pltpu.VMEM)] * len(outs),
        scratch_shapes=list(scratch),
        compiler_params=pltpu.CompilerParams(vmem_limit_bytes=limit * 1024 * 1024),
    )(*args)


def partner(place, side):
    return place + 1 - 2 * ((place + side) % 2)


def pairing(subs, grps, side):
    moves = []
    for place in range(subs):
        other = partner(place, side)
        for group in range(grps):
            if 0 <= other < subs:
                target = other * grps + group
            else:
                target = place * grps + (group ^ 1 if group ^ 1 < grps else group)
            moves.append((place * grps + group, target))
    return moves


def row_of(ref, flipped):
    return jnp.where(flipped == 0, ref[0:1, :], ref[1:2, :])


def parity(side):
    return (lax.axis_index("sub") + side) % 2


def pick(field, places):
    return jnp.take_along_axis(field, jnp.broadcast_to(places, field.shape), axis=1)


def pieces(field):
    high = field.astype(bf16)
    return high, (field - high.astype(f32)).astype(bf16)


def local_product(blocks_ref, valve_ref, field):
    rows = []
    for at in range(0, blocks_ref.shape[0], 8):
        part = blocks_ref[at : at + 8].astype(f32) * field[None]
        rows.append(jnp.sum(part, axis=1))
    return jnp.concatenate(rows, axis=0) + penalty_gain * valve_ref[...].astype(f32) * field


def received(near, arrive_ref):
    high, low = pieces(jnp.concatenate(near, axis=1))
    both = jnp.dot(
        jnp.concatenate([high, low], axis=0), arrive_ref[...], preferred_element_type=f32
    )
    count = near[0].shape[0]
    return both[:count] + both[count:]


def restricted(weighted, gather_ref):
    high = weighted.astype(bf16).astype(f32)
    rest = weighted - high
    middle = rest.astype(bf16).astype(f32)
    last = rest - middle
    row = lax.broadcasted_iota(jnp.int32, (8, weighted.shape[1]), 0)
    stack = jnp.where(row == 0, high, jnp.where(row == 1, middle, jnp.where(row == 2, last, 0.0)))
    sums = jnp.dot(stack.astype(bf16), gather_ref[...], preferred_element_type=f32)
    sums = jnp.sum(sums, axis=0, keepdims=True)
    return [sums[:, at : at + LANES] for at in range(0, sums.shape[1], LANES)]


def total(field):
    value = jnp.sum(jnp.sum(field, axis=0, keepdims=True), axis=1, keepdims=True)
    return jnp.broadcast_to(value, (1, LANES))


def halves(first, second):
    return jnp.where(lax.broadcasted_iota(jnp.int32, (1, LANES), 1) < LANES // 2, first, second)


def turned(row):
    return pltpu.roll(jnp.broadcast_to(row, (8, LANES)), LANES // 2, 1)[0:1]


def to_all(ref, rows):
    ref[...] = jnp.broadcast_to(jnp.concatenate(rows, axis=0)[None], ref.shape)


def first_send(guess_hbm, prolong_hbm, agg_hbm, send_hbm, even_ref, odd_ref,
               guess_ref, prolong_ref, agg_ref, send_ref, sems):
    pairs = ((guess_hbm, guess_ref), (prolong_hbm, prolong_ref), (agg_hbm, agg_ref), (send_hbm, send_ref))
    copies = [pltpu.make_async_copy(*pair, sems.at[at]) for at, pair in enumerate(pairs)]
    for copy in copies:
        copy.start()
    for copy in copies:
        copy.wait()
    size = guess_ref.shape[0]
    agg = jnp.broadcast_to(agg_ref[...].astype(f32), (8, LANES))
    for side, ref in enumerate((even_ref, odd_ref)):
        places = row_of(send_ref, parity(side))
        ref[0:size, :] = pick(guess_ref[...], places)
        ref[size : 2 * size, :] = pick(prolong_ref[...], places)
        ref[2 * size : 2 * size + 8, :] = pick(agg, places)


def prepare(live_ref, guess_ref, rhs_ref, blocks_ref, valve_ref, agg_ref, recv_ref, cpd,
            local_ref, arrive_ref, gather_ref):
    local_ref[...] = rhs_ref[...] - local_product(blocks_ref, valve_ref, guess_ref[...])
    place = lax.axis_index("sub")
    count = arrive_ref.shape[1]
    slots = recv_ref.shape[1]
    row = lax.broadcasted_iota(jnp.int32, (count, slots), 0)
    slot = lax.broadcasted_iota(jnp.int32, (count, slots), 1)
    for side in (0, 1):
        other = place + 1 - 2 * parity(side)
        there = (other >= 0) & (other < lax.axis_size("sub"))
        which = 1 - parity(side)
        live = jnp.where(there, live_ref[0, which], 0)
        hit = (row_of(recv_ref, which) == row) & (slot < live)
        arrive_ref[side * slots : (side + 1) * slots, :] = jnp.where(hit, 1.0, 0.0).T.astype(bf16)
    period = gather_ref.shape[1]
    coarse = lax.rem(lax.broadcasted_iota(jnp.int32, (period, count), 0), cpd)
    gather_ref[...] = jnp.where(agg_ref[...] == coarse, 1.0, 0.0).T.astype(bf16)


def residual(local_ref, even_near_ref, odd_near_ref, arrive_ref, gather_ref, prolong_ref,
             jscale_ref, send_ref, cdiag_ref, first_ref, out_ref, even_ref, odd_ref):
    size = local_ref.shape[0]
    near = [even_near_ref[0:size, :], odd_near_ref[0:size, :]]
    first = local_ref[...] + coupling * received(near, arrive_ref)
    first_ref[...] = first
    weighted = jnp.sum(prolong_ref[...] * first, axis=0, keepdims=True)
    to_all(out_ref, restricted(weighted, gather_ref) + [total(first * first)])
    scaled = jscale_ref[...] * first
    cpd = cdiag_ref.shape[1]
    cdiag = jnp.concatenate([cdiag_ref[...], jnp.zeros((1, LANES - cpd), f32)], axis=1)
    for side, ref in enumerate((even_ref, odd_ref)):
        ref[0:size, :] = pick(scaled, row_of(send_ref, parity(side)))
        ref[size : size + 8, :] = jnp.broadcast_to(cdiag, (8, LANES))


def look_ahead(first_ref, jscale_ref, prolong_ref, blocks_ref, valve_ref, coff_ref, coff_even_ref,
               coff_odd_ref, lead_ref, pull_ref, matrix_ref):
    lead_ref[...] = local_product(blocks_ref, valve_ref, jscale_ref[...] * first_ref[...])
    pull_ref[...] = local_product(blocks_ref, valve_ref, prolong_ref[...])
    cpd = coff_ref.shape[0]
    for at, ref in enumerate((coff_ref, coff_even_ref, coff_odd_ref)):
        matrix_ref[at * SLOT : at * SLOT + cpd, :] = ref[...]
        matrix_ref[at * SLOT + cpd : (at + 1) * SLOT, :] = jnp.zeros((SLOT - cpd, ref.shape[1]), bf16)


def look_further(image_ref, jscale_ref, blocks_ref, valve_ref, lead_ref):
    lead_ref[...] = local_product(blocks_ref, valve_ref, jscale_ref[...] * image_ref[...])


def compact(got_ref, cpd):
    count, rows, _ = got_ref.shape
    shape = (rows, LANES)
    place = lax.broadcasted_iota(jnp.int32, shape, 0) * LANES + lax.broadcasted_iota(jnp.int32, shape, 1)
    owner = place // cpd
    group = (rows - 1) * LANES // cpd
    parts, sums = [], jnp.zeros(shape, f32)
    for at in range(0, count, group):
        part = jnp.zeros(shape, f32)
        for step in range(group):
            tile = got_ref[at + step]
            part = jnp.where(owner == step, tile, part)
            sums = sums + tile
        parts.append(part)
    return parts, sums


def solve_coarse(parts, matrix_ref, near_rows, cdiags):
    rows = parts[0].shape[0] - 1
    vector = jnp.concatenate([part[at : at + 1] for part in parts for at in range(rows)], axis=1)
    product = lax.dot_general(
        jnp.broadcast_to(vector, (8, vector.shape[1])).astype(bf16), matrix_ref[...],
        (((1,), (1,)), ((), ())), preferred_element_type=f32,
    )[0:1]
    low = product[:, :LANES]
    high = jnp.concatenate([product[:, LANES:], jnp.zeros((1, LANES - SLOT), f32)], axis=1)
    return [
        cdiag * row + share for cdiag, row, share in zip(cdiags, near_rows, (low, turned(low), high))
    ]


def rows_near(got_ref, grp_size):
    count = got_ref.shape[0]
    me = lax.axis_index("sub") * grp_size + lax.axis_index("grp")
    shifts = [0] + [grp_size * (1 - 2 * parity(side)) for side in (0, 1)]
    return [got_ref[lax.rem(me + shift + count, count)][0:1] for shift in shifts]


def spread_of(solution, agg):
    wide = jnp.broadcast_to(solution, (8, LANES))
    return jnp.take_along_axis(wide, jnp.broadcast_to(agg, (8, LANES)), axis=1)[0:1]


def cdiags_of(cdiag_ref, near_refs, size):
    cpd = cdiag_ref.shape[1]
    own = jnp.concatenate([cdiag_ref[...], jnp.zeros((1, LANES - cpd), f32)], axis=1)
    return [own] + [ref[size : size + 1, :] for ref in near_refs]


def near_spread(constants_ref, solution, size):
    agg = constants_ref[2 * size : 2 * size + 1, :].astype(jnp.int32)
    return constants_ref[size : 2 * size, :] * spread_of(solution, agg)


def first_step(got_ref, even_near_ref, odd_near_ref, even_const_ref, odd_const_ref, matrix_ref,
               cdiag_ref, first_ref, lead_ref, pull_ref, jscale_ref, prolong_ref, agg_ref,
               arrive_ref, gather_ref, send_ref, grp_size,
               basis_ref, direction_ref, image_ref, out_ref, even_ref, odd_ref):
    size = first_ref.shape[0]
    cpd = cdiag_ref.shape[1]
    parts, sums = compact(got_ref, cpd)
    rows = sums.shape[0]
    inverse = 1.0 / jnp.sqrt(sums[rows - 1 : rows])
    own_rows = [row * inverse for row in rows_near(got_ref, grp_size)]
    near_refs = (even_near_ref, odd_near_ref)
    solved = solve_coarse([part * inverse for part in parts], matrix_ref, own_rows,
                          cdiags_of(cdiag_ref, near_refs, size))
    basis = first_ref[...] * inverse
    basis_ref[...] = basis
    spread = spread_of(solved[0], agg_ref[...])
    jscale, prolong = jscale_ref[...], prolong_ref[...]
    direction_ref[...] = jscale * basis + prolong * spread
    near = [
        ref[0:size, :] * inverse + near_spread(const, part, size)
        for ref, const, part in zip(near_refs, (even_const_ref, odd_const_ref), solved[1:])
    ]
    image = lead_ref[...] * inverse + pull_ref[...] * spread - coupling * received(near, arrive_ref)
    image_ref[...] = image
    weighted = jnp.sum(prolong * image, axis=0, keepdims=True)
    dots = halves(total(basis * image), total(image * image))
    to_all(out_ref, restricted(weighted, gather_ref) + [dots])
    scaled = jscale * image
    for side, ref in enumerate((even_ref, odd_ref)):
        ref[...] = pick(scaled, row_of(send_ref, parity(side)))


def second_step(got_ref, first_got_ref, even_near_ref, odd_near_ref, even_first_ref, odd_first_ref,
                even_const_ref, odd_const_ref, matrix_ref, cdiag_ref, basis_ref, image_ref,
                lead_ref, lead_two_ref, pull_ref, jscale_ref, prolong_ref, agg_ref, arrive_ref,
                grp_size, basis_two_ref, direction_ref, image_two_ref, scalars_ref, out_ref):
    size = basis_ref.shape[0]
    cpd = cdiag_ref.shape[1]
    first_parts, first_sums = compact(first_got_ref, cpd)
    parts, sums = compact(got_ref, cpd)
    rows = sums.shape[0]
    beta = jnp.sqrt(first_sums[rows - 1 : rows])
    totals = sums[rows - 1 : rows]
    swapped = turned(totals)
    along, energy = halves(totals, swapped), halves(swapped, totals)
    height = jnp.sqrt(jnp.maximum(energy - along * along, 0.01 * energy))
    inverse = 1.0 / height
    slope = along / beta

    def mixed(new, old):
        return (new - slope * old) * inverse

    own_rows = [
        mixed(new, old)
        for new, old in zip(rows_near(got_ref, grp_size), rows_near(first_got_ref, grp_size))
    ]
    near_first = (even_first_ref, odd_first_ref)
    solved = solve_coarse([mixed(new, old) for new, old in zip(parts, first_parts)], matrix_ref,
                          own_rows, cdiags_of(cdiag_ref, near_first, size))
    basis = (image_ref[...] - along * basis_ref[...]) * inverse
    basis_two_ref[...] = basis
    spread = spread_of(solved[0], agg_ref[...])
    direction_ref[...] = jscale_ref[...] * basis + prolong_ref[...] * spread
    near = [
        mixed(ref[...], first[0:size, :]) + near_spread(const, part, size)
        for ref, first, const, part in zip(
            (even_near_ref, odd_near_ref), near_first, (even_const_ref, odd_const_ref), solved[1:]
        )
    ]
    image = mixed(lead_two_ref[...], lead_ref[...]) + pull_ref[...] * spread
    image = image - coupling * received(near, arrive_ref)
    image_two_ref[...] = image
    scalars_ref[...] = jnp.concatenate([beta, along, height, jnp.zeros((5, LANES), f32)], axis=0)
    to_all(out_ref, [total(basis_ref[...] * image), total(basis * image), total(image * image),
                     jnp.zeros((1, LANES), f32)])


def finish(got_ref, scalars_ref, guess_ref, basis_ref, basis_two_ref, direction_ref,
           direction_two_ref, image_ref, solution_ref, next_ref):
    beta, h11, h21 = scalars_ref[0:1, :], scalars_ref[1:2, :], scalars_ref[2:3, :]
    totals = jnp.sum(got_ref[...], axis=0)
    h12, h22, energy = totals[0:1], totals[1:2], totals[2:3]
    h32 = jnp.sqrt(jnp.maximum(energy - (h12 * h12 + h22 * h22), 0.01 * energy))
    g00 = h11 * h11 + h21 * h21
    g01 = h11 * h12 + h21 * h22
    g11 = h12 * h12 + h22 * h22 + h32 * h32
    t0, t1 = beta * h11, beta * h12
    factor = g01 / g00
    c1 = (t1 - factor * t0) / (g11 - factor * g01)
    c0 = (t0 - g01 * c1) / g00
    solution_ref[...] = guess_ref[...] + c0 * direction_ref[...] + c1 * direction_two_ref[...]
    next_ref[...] = (image_ref[...] - h12 * basis_ref[...] - h22 * basis_two_ref[...]) * (1.0 / h32)


def on_device(rhs, guess, blocks, valve, jscale, prolong, agg_map, cdiag, coff, send_rows,
              recv_rows, live_counts):
    rhs, guess, blocks, jscale, prolong = rhs[0, 0], guess[0, 0], blocks[0, 0], jscale[0, 0], prolong[0, 0]
    valve, agg, live = valve[0], agg_map[0], live_counts[0]
    send, recv = send_rows[0, 0], recv_rows[0, 0]
    size, count = guess.shape
    slots = send.shape[1]
    cpd = cdiag.shape[0]
    subs, grps = lax.axis_size("sub"), lax.axis_size("grp")
    devices = subs * grps
    period = math.lcm(cpd, LANES)
    cdiag = cdiag[None, :]
    moves = [pairing(subs, grps, side) for side in (0, 1)]

    def exchange(even, odd):
        odd = lax.ppermute(odd, AXES, moves[1])
        return lax.ppermute(even, AXES, moves[0]), odd

    def everyone(rows):
        return lax.all_to_all(rows, AXES, 0, 0, tiled=True)

    field = ((size, count), f32)
    near = ((size, slots), f32)
    rows_out = ((devices, period // LANES + 1, LANES), f32)
    packed = ((2 * size + 8, slots), f32)
    even, odd = call(
        first_send, [packed, packed], guess, prolong, agg, send, hbm=(0, 1, 2, 3), limit=56,
        scratch=[
            pltpu.VMEM(guess.shape, f32), pltpu.VMEM(prolong.shape, f32),
            pltpu.VMEM(agg.shape, jnp.int32), pltpu.VMEM(send.shape, jnp.int32),
            pltpu.SemaphoreType.DMA((4,)),
        ],
    )
    even_const, odd_const = exchange(even, odd)
    coff_even, coff_odd = exchange(coff, coff)
    local, arrive, gather = call(
        lambda *refs: prepare(*refs[:7], cpd, *refs[7:]),
        [field, ((2 * slots, count), bf16), ((count, period), bf16)],
        live, guess, rhs, blocks, valve, agg, recv, smem=(0,),
    )
    packed = ((size + 8, slots), f32)
    first, rows, even, odd = call(
        residual, [field, rows_out, packed, packed],
        local, even_const, odd_const, arrive, gather, prolong, jscale, send, cdiag,
    )
    even_first, odd_first = exchange(even, odd)
    first_got = everyone(rows)
    lead, pull, matrix = call(
        look_ahead, [field, field, ((3 * SLOT, coff.shape[1]), bf16)],
        first, jscale, prolong, blocks, valve, coff, coff_even, coff_odd,
    )
    basis, direction, image, rows, even, odd = call(
        lambda *refs: first_step(*refs[:16], grps, *refs[16:]),
        [field, field, field, rows_out, near, near],
        first_got, even_first, odd_first, even_const, odd_const, matrix, cdiag, first, lead, pull,
        jscale, prolong, agg, arrive, gather, send,
    )
    even_near, odd_near = exchange(even, odd)
    got = everyone(rows)
    (lead_two,) = call(look_further, [field], image, jscale, blocks, valve)
    basis_two, direction_two, image_two, scalars, rows = call(
        lambda *refs: second_step(*refs[:19], grps, *refs[19:]),
        [field, field, field, ((8, LANES), f32), ((devices, 4, LANES), f32)],
        got, first_got, even_near, odd_near, even_first, odd_first, even_const, odd_const, matrix,
        cdiag, basis, image, lead, lead_two, pull, jscale, prolong, agg, arrive,
    )
    got = everyone(rows)
    solution, next_basis = call(
        finish, [field, field],
        got, scalars, guess, basis, basis_two, direction, direction_two, image_two,
    )
    return solution[None, None], next_basis[None, None]


def solution(mesh):
    return jax.shard_map(
        on_device,
        mesh=mesh,
        in_specs=(
            P("sub", "grp", None, None),
            P("sub", "grp", None, None),
            P("sub", "grp", None, None, None),
            P("sub", "grp", None),
            P("sub", "grp", None, None),
            P("sub", "grp", None, None),
            P("sub", "grp", None),
            P(("sub", "grp")),
            P(("sub", "grp"), None),
            P("sub", "grp", None, None),
            P("sub", "grp", None, None),
            P("sub", "grp", None),
        ),
        out_specs=(P("sub", "grp", None, None), P("sub", "grp", None, None)),
        check_vma=False,
    )
```

time: 58.6 us -> 51.2 us (0.87)
  starting transfers between devices: 28.7 us -> 19 us
  waiting for transfers between devices: 6.58 us -> 10.3 us
  local copies, waits for them, and re-layouts: 5.59 us -> 2.56 us
  Pallas kernels: 4.26 us -> 7.13 us
  blocking collectives: 12.3 us -> 11.1 us
    ppermute x8, starting transfers between devices: 17.7 us -> 9.75 us  [the longest x4 9.74 us: exchange(): return (lax.ppermute(even, AXES, moves[0]), odd)]
    ppermute x8, waiting for transfers between devices: 0.67 us -> 3.65 us  [the longest x4 3.64 us: exchange(): return (lax.ppermute(even, AXES, moves[0]), odd)]
    pallas_call x6 -> x8, Pallas kernels: 4.26 us -> 7.13 us  [call(): pl.pallas_call(body, out_shape=[jax.ShapeDtypeStruct(shape, kind) for sha...]
    all_to_all x2, starting transfers between devices: 11 us -> 9.26 us  [everyone(): return lax.all_to_all(rows, AXES, 0, 0, tiled=True)]
    unnamed x31 -> x26, local copies, waits for them, and re-layouts: 4.11 us -> 2.56 us
    all_to_all x3 -> x0, local copies, waits for them, and re-layouts: 1.48 us -> none  [everyone(): return lax.all_to_all(rows, AXES, 0, 0, tiled=True)]
    all_to_all x1, blocking collectives: 12.3 us -> 11.1 us  [everyone(): return lax.all_to_all(rows, AXES, 0, 0, tiled=True)]
    all_to_all x2, waiting for transfers between devices: 5.91 us -> 6.63 us  [everyone(): return lax.all_to_all(rows, AXES, 0, 0, tiled=True)]
  transfers between devices with their start and end apart: 10 -> 10, of which waited for: 3 -> 4; matrix products, arithmetic and copies ran while one was open for 1% -> 0% of each run, Pallas kernels for 2% -> 5%
where the time goes in v2:
time: 51.2 us; the launch traced here: 50.9 us
  starting transfers between devices  19 us (37%)
  blocking collectives  11.1 us (22%)
  waiting for transfers between devices  10.3 us (20%)
  Pallas kernels  7.13 us (14%)
  local copies, waits for them, and re-layouts  2.56 us (5%)
  between operations  0.8 us (2%)
    all_to_all x1, blocking collectives, everyone(): return lax.all_to_all(rows, AXES, 0, 0, tiled=True)  11.1 us
    ppermute x4, starting transfers between devices, exchange(): return (lax.ppermute(even, AXES, moves[0]), odd)  9.74 us
    all_to_all x2, starting transfers between devices, everyone(): return lax.all_to_all(rows, AXES, 0, 0, tiled=True)  9.26 us
    pallas_call x8, Pallas kernels, call(): pl.pallas_call(body, out_shape=[jax.ShapeDtypeStruct(shape, kind) for sha...  7.13 us
    all_to_all x2, waiting for transfers between devices, everyone(): return lax.all_to_all(rows, AXES, 0, 0, tiled=True)  6.63 us
    ppermute x4, waiting for transfers between devices, exchange(): return (lax.ppermute(even, AXES, moves[0]), odd)  3.64 us
    unnamed x26, local copies, waits for them, and re-layouts  2.56 us
  transfers between devices with their start and end apart: 10, of which 4 were waited for; matrix products, arithmetic and copies ran while one was open for 0% of the time, Pallas kernels for 5%

profile of v2, /device:TPU:0, one launch (start us, length us, event | category | flops | bytes accessed | tf_op | source)
XLA Modules:
  0.0 50.9 jit_solution(978952668556726899)
XLA Ops:
  0.6 0.0 copy-start.4
  0.6 0.0 copy-start.6
  0.6 1.6 %shard_map.132 = (f32[136,128]{1,0:T(8,128)}, f32[136,128]{1,0:T(8,128)}) custom-call(f32[64,128]{1,0:T(8,128)} %bitcast.26, f32[64,128]{1,0:T(8,128)} %bitcast.16, s32[1,128]{1,0:T(1,128)} %bitcast.33, s32[2,128]{1,0:T(2,128)} %bitcast.30), custom_call_target="tpu_custom_call" | custom-call | tf_op jit(solution)/shard_map/pallas_call | solution.py:26
  2.3 3.0 %collective-permute-start = (f32[136,128]{1,0:T(8,128)}, f32[136,128]{1,0:T(8,128)S(1)}, u32[]{:S(2)}, u32[]{:S(2)}) collective-permute-start(f32[136,128]{1,0:T(8,128)} %get-tuple-element.28), channel_id=1, source_target_pairs={{0,4},{1,5},{2,6},{3,7},{4,0},{5,1},{6,2},{7,3},{8,12},{9,13},{10,... | collective-permute-start | bytes 208904 | tf_op jit(solution)/shard_map/ppermute | solution.py:347
  5.3 0.0 collective-permute-start.1
  5.3 3.0 %collective-permute-start.4 = (bf16[48,1536]{1,0:T(8,128)(2,1)}, bf16[48,1536]{1,0:T(8,128)(2,1)S(1)}, u32[]{:S(2)}, u32[]{:S(2)}) collective-permute-start(bf16[48,1536]{1,0:T(8,128)(2,1)} %coff_ref.1), channel_id=1, source_target_pairs={{0,4},{1,5},{2,6},{3,7},{4,0},{5,1},{6,2},{7,3},{8,12},{9,13},{10,... | collective-permute-start | bytes 442376 | tf_op jit(solution)/shard_map/ppermute | solution.py:347
  8.3 0.0 collective-permute-start.5
  8.3 0.0 copy-start.11
  8.4 0.0 copy-start.12
  8.4 0.0 copy-done.4
  8.4 0.0 copy-done.6
  8.4 0.6 %copy-done.11 = s32[1,1,2,128]{3,2,1,0:T(2,128)S(1)} copy-done((s32[1,1,2,128]{3,2,1,0:T(2,128)S(1)}, s32[1,1,2,128]{3,2,1,0:T(2,128)}, u32[]{:S(2)}) %copy-start.11) | copy-done | bytes 1048
  9.0 0.0 copy-done.8
  9.0 0.0 copy-done.9
  9.0 0.0 copy-done.12
  9.1 1.2 %copy-done = bf16[1,1,64,64,128]{4,3,2,1,0:T(8,128)(2,1)S(1)} copy-done((bf16[1,1,64,64,128]{4,3,2,1,0:T(8,128)(2,1)S(1)}, bf16[1,1,64,64,128]{4,3,2,1,0:T(8,128)(2,1)}, u32[]{:S(2)}) %copy-start) | copy-done | bytes 1048600
  10.3 0.9 %shard_map.131 = (f32[64,128]{1,0:T(8,128)S(1)}, bf16[256,128]{1,0:T(8,128)(2,1)S(1)}, bf16[128,384]{1,0:T(8,128)(2,1)S(1)}) custom-call(s32[1,2]{1,0:T(1,128)S(1)} %bitcast.44, f32[64,128]{1,0:T(8,128)S(1)} %bitcast.27, f32[64,128]{1,0:T(8,128)S(1)} %bitcast.29, bf16[64,64,128]{2,1,0:T(8,128)(2,1)S(1)} %bitcast.13, s32[1,128]{1,0:T(1,128)S(1)} %bitcast.37, ...), custom_call_target="tpu_custom_call" | custom-call | tf_op jit(solution)/shard_map/pallas_call | solution.py:26
  11.2 0.0 collective-permute-done.even_near_ref.refs_3_.refs_6_
  11.2 0.0 collective-permute-done.1.odd_near_ref.refs_4_.refs_7_
  11.2 0.0 copy-start.7
  11.2 0.0 copy-start.10
  11.2 0.0 copy-done.2
  11.3 0.0 copy-done.3
  11.3 0.6 %copy-done.7 = s32[1,1,2,128]{3,2,1,0:T(2,128)S(1)} copy-done((s32[1,1,2,128]{3,2,1,0:T(2,128)S(1)}, s32[1,1,2,128]{3,2,1,0:T(2,128)}, u32[]{:S(2)}) %copy-start.7) | copy-done | bytes 1048
  11.9 0.0 copy-done.10
  11.9 1.0 %shard_map.133 = (f32[64,128]{1,0:T(8,128)S(1)}, f32[32,4,128]{2,1,0:T(4,128)}, f32[72,128]{1,0:T(8,128)S(1)}, f32[72,128]{1,0:T(8,128)S(1)}) custom-call(f32[64,128]{1,0:T(8,128)S(1)} %get-tuple-element.27.local_ref, f32[136,128]{1,0:T(8,128)S(1)} %collective-permute-done.even_near_ref.refs_3_.refs_6_, ...), custom_call_target="tpu_custom_call" | custom-call | tf_op jit(solution)/shard_map/pallas_call | solution.py:26
  12.9 5.3 %all-to-all-start = ((f32[32,4,128]{2,1,0:T(4,128)}), f32[32,4,128]{2,1,0:T(4,128)S(1)}, u32[]{:S(2)}, u32[]{:S(2)}) async-start(f32[32,4,128]{2,1,0:T(4,128)} %get-tuple-element.32), calls=%async_computation | async-start | bytes 131072 | tf_op jit(solution)/shard_map/all_to_all | solution.py:350
  18.2 1.8 %collective-permute-start.2 = (f32[72,128]{1,0:T(8,128)S(1)}, f32[72,128]{1,0:T(8,128)S(1)}, u32[]{:S(2)}, u32[]{:S(2)}) collective-permute-start(f32[72,128]{1,0:T(8,128)S(1)} %get-tuple-element.33), channel_id=1, source_target_pairs={{0,4},{1,5},{2,6},{3,7},{4,0},{5,1},{6,2},{7,3},{8,12},{9,13},{10,... | collective-permute-start | bytes 110600 | tf_op jit(solution)/shard_map/ppermute | solution.py:347
  20.1 0.0 collective-permute-start.3
  20.1 0.0 collective-permute-done.4.coff_even_ref
  20.1 0.0 collective-permute-done.5.coff_odd_ref
  20.1 0.0 copy-done.1
  20.1 0.0 copy-done.5
  20.1 0.6 %shard_map.134 = (f32[64,128]{1,0:T(8,128)S(1)}, f32[64,128]{1,0:T(8,128)S(1)}, bf16[192,1536]{1,0:T(8,128)(2,1)S(1)}) custom-call(f32[64,128]{1,0:T(8,128)S(1)} %get-tuple-element.35.first_ref.refs_7_, f32[64,128]{1,0:T(8,128)S(1)} %bitcast.22, f32[64,128]{1,0:T(8,128)S(1)} %bitcast.18, bf16[64,64,128]{2,1,0:T(8,128)(2,1)S(1)} %bitcast.14, ...), custom_call_target="tpu_custom_call" | custom-call | tf_op jit(solution)/shard_map/pallas_call | solution.py:26
  20.6 1.7 %collective-permute-done.2.refs_1_.refs_4_ = f32[72,128]{1,0:T(8,128)S(1)} collective-permute-done((f32[72,128]{1,0:T(8,128)S(1)}, f32[72,128]{1,0:T(8,128)S(1)}, u32[]{:S(2)}, u32[]{:S(2)}) %collective-permute-start.2) | collective-permute-done | bytes 36896 | tf_op jit(solution)/shard_map/ppermute | solution.py:347
  22.3 0.0 collective-permute-done.3.refs_2_.refs_5_
  22.3 3.3 %all-to-all-done.refs_0_.refs_1_ = f32[32,4,128]{2,1,0:T(4,128)S(1)} async-done(((f32[32,4,128]{2,1,0:T(4,128)}), f32[32,4,128]{2,1,0:T(4,128)S(1)}, u32[]{:S(2)}, u32[]{:S(2)}) %all-to-all-start) | async-done | bytes 65568 | tf_op jit(solution)/shard_map/all_to_all | solution.py:350
  25.6 1.4 %shard_map.135 = (f32[64,128]{1,0:T(8,128)S(1)}, f32[64,128]{1,0:T(8,128)S(1)}, f32[64,128]{1,0:T(8,128)S(1)}, f32[32,4,128]{2,1,0:T(4,128)}, f32[64,128]{1,0:T(8,128)S(1)}, /*index=5*/f32[64,128]{1,0:T(8,128)S(1)}) custom-call(f32[32,4,128]{2,1,0:T(4,128)S(1)} %all-to-all-done.refs_0_.refs_1_, f32[72,128]{1,0:T(8,128)S(1)} %collective-permute-done.2.refs_1_.refs_4_, ...), custom_call_target="tpu_custom_call" | custom-call | tf_op jit(solution)/shard_map/pallas_call | solution.py:26
  27.0 3.9 %all-to-all-start.1 = ((f32[32,4,128]{2,1,0:T(4,128)}), f32[32,4,128]{2,1,0:T(4,128)S(1)}, u32[]{:S(2)}, u32[]{:S(2)}) async-start(f32[32,4,128]{2,1,0:T(4,128)} %get-tuple-element.39), calls=%async_computation.1 | async-start | bytes 131072 | tf_op jit(solution)/shard_map/all_to_all | solution.py:350
  31.0 1.8 %collective-permute-start.6 = (f32[64,128]{1,0:T(8,128)S(1)}, f32[64,128]{1,0:T(8,128)S(1)}, u32[]{:S(2)}, u32[]{:S(2)}) collective-permute-start(f32[64,128]{1,0:T(8,128)S(1)} %get-tuple-element.40), channel_id=1, source_target_pairs={{0,4},{1,5},{2,6},{3,7},{4,0},{5,1},{6,2},{7,3},{8,12},{9,13},{10,... | collective-permute-start | bytes 98312 | tf_op jit(solution)/shard_map/ppermute | solution.py:347
  32.8 0.0 collective-permute-start.7
  32.8 0.3 shard_map.136.refs_13_
  33.1 2.0 %collective-permute-done.6.refs_2_ = f32[64,128]{1,0:T(8,128)S(1)} collective-permute-done((f32[64,128]{1,0:T(8,128)S(1)}, f32[64,128]{1,0:T(8,128)S(1)}, u32[]{:S(2)}, u32[]{:S(2)}) %collective-permute-start.6) | collective-permute-done | bytes 32800 | tf_op jit(solution)/shard_map/ppermute | solution.py:347
  35.0 0.0 collective-permute-done.7.refs_3_
  35.0 3.3 %all-to-all-done.1.refs_0_ = f32[32,4,128]{2,1,0:T(4,128)S(1)} async-done(((f32[32,4,128]{2,1,0:T(4,128)}), f32[32,4,128]{2,1,0:T(4,128)S(1)}, u32[]{:S(2)}, u32[]{:S(2)}) %all-to-all-start.1) | async-done | bytes 65568 | tf_op jit(solution)/shard_map/all_to_all | solution.py:350
  38.4 0.7 %shard_map.137 = (f32[64,128]{1,0:T(8,128)S(1)}, f32[64,128]{1,0:T(8,128)S(1)}, f32[64,128]{1,0:T(8,128)S(1)}, f32[8,128]{1,0:T(8,128)S(1)}, f32[32,4,128]{2,1,0:T(4,128)S(1)}) custom-call(f32[32,4,128]{2,1,0:T(4,128)S(1)} %all-to-all-done.1.refs_0_, f32[32,4,128]{2,1,0:T(4,128)S(1)} %all-to-all-done.refs_0_.refs_1_, ...), custom_call_target="tpu_custom_call" | custom-call | tf_op jit(solution)/shard_map/pallas_call | solution.py:26
  39.1 11.1 %all_to_all.15.got_ref = f32[32,4,128]{2,1,0:T(4,128)S(1)} all-to-all(f32[32,4,128]{2,1,0:T(4,128)S(1)} %get-tuple-element.44), channel_id=1, replica_groups=mesh['sub'=8,'grp'=4] {'sub','grp'}, dimensions={0} | all-to-all | bytes 131072 | tf_op jit(solution)/shard_map/all_to_all | solution.py:350
  50.2 0.7 %shard_map.138 = (f32[64,128]{1,0:T(8,128)}, f32[64,128]{1,0:T(8,128)}) custom-call(f32[32,4,128]{2,1,0:T(4,128)S(1)} %all_to_all.15.got_ref, f32[8,128]{1,0:T(8,128)S(1)} %get-tuple-element.45.scalars_ref, f32[64,128]{1,0:T(8,128)S(1)} %bitcast.28, f32[64,128]{1,0:T(8,128)S(1)} %get-tuple-element.42.refs_10_.basis_ref, ...), custom_call_target="tpu_custom_call" | custom-call | tf_op jit(solution)/shard_map/pallas_call | solution.py:26
  (7 shorter events, 0.0 us)
Async XLA Ops:
  0.6 7.7 %copy-start.4 = (f32[1,1,64,128]{3,2,1,0:T(8,128)S(1)}, f32[1,1,64,128]{3,2,1,0:T(8,128)}, u32[]{:S(2)}) copy-start(f32[1,1,64,128]{3,2,1,0:T(8,128)} %param.13) | copy-start | bytes 98308
  0.6 7.7 %copy-start.6 = (f32[1,1,64,128]{3,2,1,0:T(8,128)S(1)}, f32[1,1,64,128]{3,2,1,0:T(8,128)}, u32[]{:S(2)}) copy-start(f32[1,1,64,128]{3,2,1,0:T(8,128)} %param.12) | copy-start | bytes 98308
  2.3 8.9 %collective-permute-start = (f32[136,128]{1,0:T(8,128)}, f32[136,128]{1,0:T(8,128)S(1)}, u32[]{:S(2)}, u32[]{:S(2)}) collective-permute-start(f32[136,128]{1,0:T(8,128)} %get-tuple-element.28), channel_id=1, source_target_pairs={{0,4},{1,5},{2,6},{3,7},{4,0},{5,1},{6,2},{7,3},{8,12},{9,13},{10,... | collective-permute-start | bytes 208904 | tf_op jit(solution)/shard_map/ppermute | solution.py:347
  5.3 5.9 %collective-permute-start.1 = (f32[136,128]{1,0:T(8,128)}, f32[136,128]{1,0:T(8,128)S(1)}, u32[]{:S(2)}, u32[]{:S(2)}) collective-permute-start(f32[136,128]{1,0:T(8,128)} %get-tuple-element.29), channel_id=1, source_target_pairs={{0,1},{1,0},{2,3},{3,2},{4,8},{5,9},{6,10},{7,11},{8,4},{9,5},{10,... | collective-permute-start | bytes 208904 | tf_op jit(solution)/shard_map/ppermute | solution.py:346
  5.3 14.7 %collective-permute-start.4 = (bf16[48,1536]{1,0:T(8,128)(2,1)}, bf16[48,1536]{1,0:T(8,128)(2,1)S(1)}, u32[]{:S(2)}, u32[]{:S(2)}) collective-permute-start(bf16[48,1536]{1,0:T(8,128)(2,1)} %coff_ref.1), channel_id=1, source_target_pairs={{0,4},{1,5},{2,6},{3,7},{4,0},{5,1},{6,2},{7,3},{8,12},{9,13},{10,... | collective-permute-start | bytes 442376 | tf_op jit(solution)/shard_map/ppermute | solution.py:347
  8.3 11.7 %collective-permute-start.5 = (bf16[48,1536]{1,0:T(8,128)(2,1)}, bf16[48,1536]{1,0:T(8,128)(2,1)S(1)}, u32[]{:S(2)}, u32[]{:S(2)}) collective-permute-start(bf16[48,1536]{1,0:T(8,128)(2,1)} %coff_ref.1), channel_id=1, source_target_pairs={{0,1},{1,0},{2,3},{3,2},{4,8},{5,9},{6,10},{7,11},{8,4},{9,5},{10,... | collective-permute-start | bytes 442376 | tf_op jit(solution)/shard_map/ppermute | solution.py:346
  8.3 0.7 %copy-start.11 = (s32[1,1,2,128]{3,2,1,0:T(2,128)S(1)}, s32[1,1,2,128]{3,2,1,0:T(2,128)}, u32[]{:S(2)}) copy-start(s32[1,1,2,128]{3,2,1,0:T(2,128)} %param.22) | copy-start | bytes 3076
  8.4 0.7 %copy-start.8 = (s32[1,1,128]{2,1,0:T(1,128)S(1)}, s32[1,1,128]{2,1,0:T(1,128)}, u32[]{:S(2)}) copy-start(s32[1,1,128]{2,1,0:T(1,128)} %param.18) | copy-start | bytes 1540
  8.4 0.7 %copy-start.9 = (s32[1,1,128]{2,1,0:T(1,128)S(1)}, s32[1,1,128]{2,1,0:T(1,128)}, u32[]{:S(2)}) copy-start(s32[1,1,128]{2,1,0:T(1,128)} %param.15) | copy-start | bytes 1540
  8.4 0.7 %copy-start.12 = (s32[1,1,2]{2,1,0:T(1,128)S(1)}, s32[1,1,2]{2,1,0:T(1,128)}, u32[]{:S(2)}) copy-start(s32[1,1,2]{2,1,0:T(1,128)} %param.23) | copy-start | bytes 28
  9.1 1.2 %copy-start = (bf16[1,1,64,64,128]{4,3,2,1,0:T(8,128)(2,1)S(1)}, bf16[1,1,64,64,128]{4,3,2,1,0:T(8,128)(2,1)}, u32[]{:S(2)}) copy-start(bf16[1,1,64,64,128]{4,3,2,1,0:T(8,128)(2,1)} %param.14) | copy-start | bytes 3145732
  10.3 1.0 %copy-start.2 = (f32[1,1,64,128]{3,2,1,0:T(8,128)S(1)}, f32[1,1,64,128]{3,2,1,0:T(8,128)}, u32[]{:S(2)}) copy-start(f32[1,1,64,128]{3,2,1,0:T(8,128)} %param.17) | copy-start | bytes 98308
  10.3 1.0 %copy-start.3 = (f32[1,1,64,128]{3,2,1,0:T(8,128)S(1)}, f32[1,1,64,128]{3,2,1,0:T(8,128)}, u32[]{:S(2)}) copy-start(f32[1,1,64,128]{3,2,1,0:T(8,128)} %param.16) | copy-start | bytes 98308
  10.3 9.8 %copy-start.1 = (bf16[1,1,64,64,128]{4,3,2,1,0:T(8,128)(2,1)S(1)}, bf16[1,1,64,64,128]{4,3,2,1,0:T(8,128)(2,1)}, u32[]{:S(2)}) copy-start(bf16[1,1,64,64,128]{4,3,2,1,0:T(8,128)(2,1)} %param.14) | copy-start | bytes 3145732
  11.2 0.7 %copy-start.7 = (s32[1,1,2,128]{3,2,1,0:T(2,128)S(1)}, s32[1,1,2,128]{3,2,1,0:T(2,128)}, u32[]{:S(2)}) copy-start(s32[1,1,2,128]{3,2,1,0:T(2,128)} %param.21) | copy-start | bytes 3076
  11.2 0.7 %copy-start.10 = (f32[48]{0:T(128)S(1)}, f32[48]{0:T(128)}, u32[]{:S(2)}) copy-start(f32[48]{0:T(128)} %param.19) | copy-start | bytes 580
  11.9 8.2 %copy-start.5 = (bf16[48,1536]{1,0:T(8,128)(2,1)S(1)}, bf16[48,1536]{1,0:T(8,128)(2,1)}, u32[]{:S(2)}) copy-start(bf16[48,1536]{1,0:T(8,128)(2,1)} %coff_ref.1) | copy-start | bytes 442372
  12.9 12.8 %all-to-all-start = ((f32[32,4,128]{2,1,0:T(4,128)}), f32[32,4,128]{2,1,0:T(4,128)S(1)}, u32[]{:S(2)}, u32[]{:S(2)}) async-start(f32[32,4,128]{2,1,0:T(4,128)} %get-tuple-element.32), calls=%async_computation | async-start | bytes 131072 | tf_op jit(solution)/shard_map/all_to_all | solution.py:350
  18.2 4.1 %collective-permute-start.2 = (f32[72,128]{1,0:T(8,128)S(1)}, f32[72,128]{1,0:T(8,128)S(1)}, u32[]{:S(2)}, u32[]{:S(2)}) collective-permute-start(f32[72,128]{1,0:T(8,128)S(1)} %get-tuple-element.33), channel_id=1, source_target_pairs={{0,4},{1,5},{2,6},{3,7},{4,0},{5,1},{6,2},{7,3},{8,12},{9,13},{10,... | collective-permute-start | bytes 110600 | tf_op jit(solution)/shard_map/ppermute | solution.py:347
  20.1 2.3 %collective-permute-start.3 = (f32[72,128]{1,0:T(8,128)S(1)}, f32[72,128]{1,0:T(8,128)S(1)}, u32[]{:S(2)}, u32[]{:S(2)}) collective-permute-start(f32[72,128]{1,0:T(8,128)S(1)} %get-tuple-element.34), channel_id=1, source_target_pairs={{0,1},{1,0},{2,3},{3,2},{4,8},{5,9},{6,10},{7,11},{8,4},{9,5},{10,... | collective-permute-start | bytes 110600 | tf_op jit(solution)/shard_map/ppermute | solution.py:346
  27.0 11.3 %all-to-all-start.1 = ((f32[32,4,128]{2,1,0:T(4,128)}), f32[32,4,128]{2,1,0:T(4,128)S(1)}, u32[]{:S(2)}, u32[]{:S(2)}) async-start(f32[32,4,128]{2,1,0:T(4,128)} %get-tuple-element.39), calls=%async_computation.1 | async-start | bytes 131072 | tf_op jit(solution)/shard_map/all_to_all | solution.py:350
  31.0 4.1 %collective-permute-start.6 = (f32[64,128]{1,0:T(8,128)S(1)}, f32[64,128]{1,0:T(8,128)S(1)}, u32[]{:S(2)}, u32[]{:S(2)}) collective-permute-start(f32[64,128]{1,0:T(8,128)S(1)} %get-tuple-element.40), channel_id=1, source_target_pairs={{0,4},{1,5},{2,6},{3,7},{4,0},{5,1},{6,2},{7,3},{8,12},{9,13},{10,... | collective-permute-start | bytes 98312 | tf_op jit(solution)/shard_map/ppermute | solution.py:347
  32.8 2.2 %collective-permute-start.7 = (f32[64,128]{1,0:T(8,128)S(1)}, f32[64,128]{1,0:T(8,128)S(1)}, u32[]{:S(2)}, u32[]{:S(2)}) collective-permute-start(f32[64,128]{1,0:T(8,128)S(1)} %get-tuple-element.41), channel_id=1, source_target_pairs={{0,1},{1,0},{2,3},{3,2},{4,8},{5,9},{6,10},{7,11},{8,4},{9,5},{10,... | collective-permute-start | bytes 98312 | tf_op jit(solution)/shard_map/ppermute | solution.py:346

commit v3 on v2

v3 whole, which is shorter than its diff:
```python
import math

import jax
import jax.numpy as jnp
from jax import lax
from jax.experimental import pallas as pl
from jax.experimental.pallas import tpu as pltpu
from jax.sharding import PartitionSpec as P

penalty_gain = 3.0
coupling = 0.5

LANES = 128
SLOT = 64
AXES = ("sub", "grp")
f32 = jnp.float32
bf16 = jnp.bfloat16

SEND, RECV, AGG, VALVE = slice(0, 2), slice(2, 4), slice(4, 5), slice(5, 6)


def call(body, outs, *args, smem=(), hbm=(), scratch=(), limit=32, final=False, aliases=None):
    def spec(at):
        if at in hbm:
            return pl.BlockSpec(memory_space=pltpu.HBM)
        return pl.BlockSpec(memory_space=pltpu.SMEM if at in smem else pltpu.VMEM)

    args = [
        pltpu.with_memory_space_constraint(arg, pltpu.HBM) if at in hbm else arg
        for at, arg in enumerate(args)
    ]
    return pl.pallas_call(
        body,
        out_shape=[
            jax.ShapeDtypeStruct(shape, kind) if final else pltpu.VMEM(shape, kind)
            for shape, kind in outs
        ],
        in_specs=[spec(at) for at in range(len(args))],
        out_specs=[pl.BlockSpec(memory_space=pltpu.VMEM)] * len(outs),
        scratch_shapes=list(scratch),
        input_output_aliases=aliases or {},
        compiler_params=pltpu.CompilerParams(vmem_limit_bytes=limit * 1024 * 1024),
    )(*args)


def partner(place, side):
    return place - 1 + 2 * ((place + side) % 2)


def pairing(subs, grps, side):
    moves = []
    for place in range(subs):
        other = partner(place, side)
        for group in range(grps):
            if 0 <= other < subs:
                target = other * grps + group
            else:
                target = place * grps + (group ^ 1 if group ^ 1 < grps else group)
            moves.append((place * grps + group, target))
    return moves


def row_of(ref, flipped):
    return jnp.where(flipped == 0, ref[0:1, :], ref[1:2, :])


def parity(side):
    return (lax.axis_index("sub") + side + 1) % 2


def pick(field, places):
    return jnp.take_along_axis(field, jnp.broadcast_to(places, field.shape), axis=1)


def pieces(field):
    high = field.astype(bf16)
    return high, (field - high.astype(f32)).astype(bf16)


def block_rows(blocks, field):
    return jnp.sum(blocks.astype(f32) * field[None], axis=1)


def local_product(blocks_ref, valve, field):
    rows = [block_rows(blocks_ref[at : at + 8], field) for at in range(0, blocks_ref.shape[0], 8)]
    return jnp.concatenate(rows, axis=0) + penalty_gain * valve.astype(f32) * field


def received(near, arrive_ref):
    high, low = pieces(jnp.concatenate(near, axis=1))
    both = jnp.dot(
        jnp.concatenate([high, low], axis=0), arrive_ref[...], preferred_element_type=f32
    )
    count = near[0].shape[0]
    return both[:count] + both[count:]


def restricted(weighted, gather_ref):
    high = weighted.astype(bf16).astype(f32)
    rest = weighted - high
    middle = rest.astype(bf16).astype(f32)
    last = rest - middle
    row = lax.broadcasted_iota(jnp.int32, (8, weighted.shape[1]), 0)
    stack = jnp.where(row == 0, high, jnp.where(row == 1, middle, jnp.where(row == 2, last, 0.0)))
    sums = jnp.dot(stack.astype(bf16), gather_ref[...], preferred_element_type=f32)
    sums = jnp.sum(sums, axis=0, keepdims=True)
    return [sums[:, at : at + LANES] for at in range(0, sums.shape[1], LANES)]


def total(field):
    value = jnp.sum(jnp.sum(field, axis=0, keepdims=True), axis=1, keepdims=True)
    return jnp.broadcast_to(value, (1, LANES))


def halves(first, second):
    return jnp.where(lax.broadcasted_iota(jnp.int32, (1, LANES), 1) < LANES // 2, first, second)


def turned(row):
    return pltpu.roll(jnp.broadcast_to(row, (8, LANES)), LANES // 2, 1)[0:1]


def to_all(ref, rows):
    ref[...] = jnp.broadcast_to(jnp.concatenate(rows, axis=0)[None], ref.shape)


def copy_all(pairs, sems):
    copies = [pltpu.make_async_copy(*pair, sems.at[at]) for at, pair in enumerate(pairs)]
    for copy in copies:
        copy.start()
    return copies


def first_send(guess_hbm, agg_hbm, send_hbm, recv_hbm, valve_hbm, odd_ref, even_ref, notes_ref,
               guess_ref, agg_ref, send_ref, recv_ref, valve_ref, sems):
    pairs = (
        (send_hbm, send_ref), (guess_hbm, guess_ref), (agg_hbm, agg_ref), (recv_hbm, recv_ref),
        (valve_hbm, valve_ref),
    )
    for copy in copy_all(pairs, sems):
        copy.wait()
    for side, ref in enumerate((odd_ref, even_ref)):
        ref[...] = pick(guess_ref[...], row_of(send_ref, parity(side)))
    notes_ref[...] = jnp.concatenate(
        [send_ref[...], recv_ref[...], agg_ref[...], valve_ref[...], jnp.zeros((2, LANES), jnp.int32)],
        axis=0,
    )


def wide(row):
    return jnp.concatenate([row, jnp.zeros((1, LANES - row.shape[1]), row.dtype)], axis=1)


def pack_constants(ref, coff_ref, prolong, agg, cdiag, places):
    cpd, width = coff_ref.shape
    for at in range(0, width, LANES):
        start = at // LANES * cpd
        ref[start : start + cpd, :] = coff_ref[:, at : at + LANES]
    base = cpd * (width // LANES)
    high, low = pieces(pick(prolong, places))
    size = high.shape[0]
    ref[base : base + size, :] = high
    ref[base + size : base + 2 * size, :] = low
    listed = pick(jnp.broadcast_to(agg.astype(f32), (8, LANES)), places)[0:1]
    one = cdiag.astype(bf16).astype(f32)
    two = (cdiag - one).astype(bf16).astype(f32)
    rows = [listed, one, two, cdiag - one - two, jnp.zeros((12, LANES), f32)]
    ref[base + 2 * size : base + 2 * size + 16, :] = jnp.concatenate(rows, axis=0).astype(bf16)


def prepare(live_hbm, guess_hbm, rhs_hbm, blocks_hbm, coff_hbm, prolong_hbm, cdiag_hbm, notes_ref,
            cpd, local_ref, arrive_ref, gather_ref, odd_ref, even_ref,
            live_ref, guess_ref, rhs_ref, blocks_ref, coff_ref, prolong_ref, cdiag_ref, sems):
    size = guess_ref.shape[0]
    chunk = size // 4
    pairs = [(coff_hbm, coff_ref), (prolong_hbm, prolong_ref), (cdiag_hbm, cdiag_ref),
             (live_hbm, live_ref), (guess_hbm, guess_ref)]
    for at in range(0, size, chunk):
        pairs.append((blocks_hbm.at[at : at + chunk], blocks_ref.at[at : at + chunk]))
    copies = copy_all(pairs + [(rhs_hbm, rhs_ref)], sems)
    for copy in copies[:4]:
        copy.wait()
    cdiag = wide(cdiag_ref[...])
    for side, ref in enumerate((odd_ref, even_ref)):
        places = row_of(notes_ref.at[SEND], parity(side))
        pack_constants(ref, coff_ref, prolong_ref[...], notes_ref[AGG], cdiag, places)
    count = arrive_ref.shape[1]
    slots = notes_ref.shape[1]
    period = gather_ref.shape[1]
    coarse = lax.rem(lax.broadcasted_iota(jnp.int32, (period, count), 0), cpd)
    gather_ref[...] = jnp.where(notes_ref[AGG] == coarse, 1.0, 0.0).T.astype(bf16)
    place = lax.axis_index("sub")
    row = lax.broadcasted_iota(jnp.int32, (count, slots), 0)
    slot = lax.broadcasted_iota(jnp.int32, (count, slots), 1)
    for side in (0, 1):
        other = place + 1 - 2 * parity(side)
        there = (other >= 0) & (other < lax.axis_size("sub"))
        which = 1 - parity(side)
        live = jnp.where(there, live_ref[0, which], 0)
        hit = (row_of(notes_ref.at[RECV], which) == row) & (slot < live)
        arrive_ref[side * slots : (side + 1) * slots, :] = jnp.where(hit, 1.0, 0.0).T.astype(bf16)
    copies[4].wait()
    guess = guess_ref[...]
    penalty = penalty_gain * notes_ref[VALVE].astype(f32)
    for at in range(0, size, 8):
        if at % chunk == 0:
            copies[5 + at // chunk].wait()
        part = slice(at, at + 8)
        local_ref[part, :] = block_rows(blocks_ref[part], guess) + penalty * guess[part]
    copies[-1].wait()
    local_ref[...] = rhs_ref[...] - local_ref[...]


def hand_on(odd_ref, even_ref, odd_after_ref, even_after_ref, odd_out_ref, even_out_ref):
    pass


def residual(local_ref, odd_near_ref, even_near_ref, arrive_ref, gather_ref, prolong_ref,
             jscale_ref, notes_ref, first_ref, out_ref, odd_ref, even_ref):
    near = [odd_near_ref[...], even_near_ref[...]]
    first = local_ref[...] + coupling * received(near, arrive_ref)
    first_ref[...] = first
    weighted = jnp.sum(prolong_ref[...] * first, axis=0, keepdims=True)
    to_all(out_ref, restricted(weighted, gather_ref) + [total(first * first)])
    scaled = jscale_ref[...] * first
    for side, ref in enumerate((odd_ref, even_ref)):
        ref[...] = pick(scaled, row_of(notes_ref.at[SEND], parity(side)))


def look_ahead(first_ref, jscale_ref, prolong_ref, blocks_ref, notes_ref, own_ref, odd_ref,
               even_ref, cpd, lead_ref, pull_ref, matrix_ref, odd_weights_ref, even_weights_ref,
               info_ref):
    lead_ref[...] = local_product(blocks_ref, notes_ref[VALVE], jscale_ref[...] * first_ref[...])
    pull_ref[...] = local_product(blocks_ref, notes_ref[VALVE], prolong_ref[...])
    width = matrix_ref.shape[1]
    size = first_ref.shape[0]
    base = cpd * (width // LANES)
    rows = []
    for slot, ref in enumerate((own_ref, odd_ref, even_ref)):
        for at in range(0, width, LANES):
            start = at // LANES * cpd
            matrix_ref[slot * SLOT : slot * SLOT + cpd, at : at + LANES] = ref[start : start + cpd, :]
        matrix_ref[slot * SLOT + cpd : (slot + 1) * SLOT, :] = jnp.zeros((SLOT - cpd, width), bf16)
        rows.append(ref[base + 2 * size : base + 2 * size + 16, :].astype(f32))
    for ref, weights_ref in ((odd_ref, odd_weights_ref), (even_ref, even_weights_ref)):
        weights_ref[...] = ref[base : base + size, :].astype(f32) + ref[
            base + size : base + 2 * size, :
        ].astype(f32)
    infos = [row[1:2] + row[2:3] + row[3:4] for row in rows] + [row[0:1] for row in rows[1:]]
    info_ref[...] = jnp.concatenate(infos + [jnp.zeros((3, LANES), f32)], axis=0)


def look_further(image_ref, jscale_ref, blocks_ref, notes_ref, lead_ref):
    lead_ref[...] = local_product(blocks_ref, notes_ref[VALVE], jscale_ref[...] * image_ref[...])


def compact(got_ref, cpd):
    count, rows, _ = got_ref.shape
    shape = (rows, LANES)
    place = lax.broadcasted_iota(jnp.int32, shape, 0) * LANES + lax.broadcasted_iota(jnp.int32, shape, 1)
    owner = place // cpd
    group = (rows - 1) * LANES // cpd
    parts, sums = [], jnp.zeros(shape, f32)
    for at in range(0, count, group):
        part = jnp.zeros(shape, f32)
        for step in range(group):
            tile = got_ref[at + step]
            part = jnp.where(owner == step, tile, part)
            sums = sums + tile
        parts.append(part)
    return parts, sums


def solve_coarse(parts, matrix_ref, near_rows, info_ref):
    rows = parts[0].shape[0] - 1
    vector = jnp.concatenate([part[at : at + 1] for part in parts for at in range(rows)], axis=1)
    product = lax.dot_general(
        jnp.broadcast_to(vector, (8, vector.shape[1])).astype(bf16), matrix_ref[...],
        (((1,), (1,)), ((), ())), preferred_element_type=f32,
    )[0:1]
    low = product[:, :LANES]
    high = jnp.concatenate([product[:, LANES:], jnp.zeros((1, LANES - SLOT), f32)], axis=1)
    shares = (low, turned(low), high)
    return [
        info_ref[at : at + 1, :] * row + share
        for at, (row, share) in enumerate(zip(near_rows, shares))
    ]


def rows_near(got_ref, grp_size):
    count = got_ref.shape[0]
    me = lax.axis_index("sub") * grp_size + lax.axis_index("grp")
    shifts = [0] + [grp_size * (1 - 2 * parity(side)) for side in (0, 1)]
    return [got_ref[lax.rem(me + shift + count, count)][0:1] for shift in shifts]


def spread_of(solution, agg):
    wide = jnp.broadcast_to(solution, (8, LANES))
    return jnp.take_along_axis(wide, jnp.broadcast_to(agg, (8, LANES)), axis=1)[0:1]


def near_spread(weights_ref, info_ref, side, solution):
    agg = info_ref[3 + side : 4 + side, :].astype(jnp.int32)
    return weights_ref[...] * spread_of(solution, agg)


def first_step(got_ref, odd_near_ref, even_near_ref, odd_weights_ref, even_weights_ref, matrix_ref,
               info_ref, first_ref, lead_ref, pull_ref, jscale_ref, prolong_ref, notes_ref,
               arrive_ref, gather_ref, grp_size, cpd,
               basis_ref, direction_ref, image_ref, out_ref, odd_ref, even_ref):
    parts, sums = compact(got_ref, cpd)
    rows = sums.shape[0]
    inverse = 1.0 / jnp.sqrt(sums[rows - 1 : rows])
    own_rows = [row * inverse for row in rows_near(got_ref, grp_size)]
    solved = solve_coarse([part * inverse for part in parts], matrix_ref, own_rows, info_ref)
    basis = first_ref[...] * inverse
    basis_ref[...] = basis
    spread = spread_of(solved[0], notes_ref[AGG])
    jscale, prolong = jscale_ref[...], prolong_ref[...]
    direction_ref[...] = jscale * basis + prolong * spread
    near = [
        odd_near_ref[...] * inverse + near_spread(odd_weights_ref, info_ref, 0, solved[1]),
        even_near_ref[...] * inverse + near_spread(even_weights_ref, info_ref, 1, solved[2]),
    ]
    image = lead_ref[...] * inverse + pull_ref[...] * spread - coupling * received(near, arrive_ref)
    image_ref[...] = image
    weighted = jnp.sum(prolong * image, axis=0, keepdims=True)
    dots = halves(total(basis * image), total(image * image))
    to_all(out_ref, restricted(weighted, gather_ref) + [dots])
    scaled = jscale * image
    for side, ref in enumerate((odd_ref, even_ref)):
        ref[...] = pick(scaled, row_of(notes_ref.at[SEND], parity(side)))


def second_step(got_ref, first_got_ref, odd_near_ref, even_near_ref, odd_first_ref, even_first_ref,
                odd_weights_ref, even_weights_ref, matrix_ref, info_ref, basis_ref, image_ref,
                lead_ref, lead_two_ref, pull_ref, jscale_ref, prolong_ref, notes_ref, arrive_ref,
                grp_size, cpd, basis_two_ref, direction_ref, image_two_ref, scalars_ref, out_ref):
    first_parts, first_sums = compact(first_got_ref, cpd)
    parts, sums = compact(got_ref, cpd)
    rows = sums.shape[0]
    beta = jnp.sqrt(first_sums[rows - 1 : rows])
    totals = sums[rows - 1 : rows]
    swapped = turned(totals)
    along, energy = halves(totals, swapped), halves(swapped, totals)
    height = jnp.sqrt(jnp.maximum(energy - along * along, 0.01 * energy))
    inverse = 1.0 / height
    slope = along / beta

    def mixed(new, old):
        return (new - slope * old) * inverse

    own_rows = [
        mixed(new, old)
        for new, old in zip(rows_near(got_ref, grp_size), rows_near(first_got_ref, grp_size))
    ]
    solved = solve_coarse(
        [mixed(new, old) for new, old in zip(parts, first_parts)], matrix_ref, own_rows, info_ref
    )
    basis = (image_ref[...] - along * basis_ref[...]) * inverse
    basis_two_ref[...] = basis
    spread = spread_of(solved[0], notes_ref[AGG])
    direction_ref[...] = jscale_ref[...] * basis + prolong_ref[...] * spread
    near = [
        mixed(odd_near_ref[...], odd_first_ref[...])
        + near_spread(odd_weights_ref, info_ref, 0, solved[1]),
        mixed(even_near_ref[...], even_first_ref[...])
        + near_spread(even_weights_ref, info_ref, 1, solved[2]),
    ]
    image = mixed(lead_two_ref[...], lead_ref[...]) + pull_ref[...] * spread
    image = image - coupling * received(near, arrive_ref)
    image_two_ref[...] = image
    scalars_ref[...] = jnp.concatenate([beta, along, height, jnp.zeros((5, LANES), f32)], axis=0)
    to_all(out_ref, [total(basis_ref[...] * image), total(basis * image), total(image * image),
                     jnp.zeros((1, LANES), f32)])


def finish(got_ref, scalars_ref, guess_ref, basis_ref, basis_two_ref, direction_ref,
           direction_two_ref, image_ref, solution_ref, next_ref):
    beta, h11, h21 = scalars_ref[0:1, :], scalars_ref[1:2, :], scalars_ref[2:3, :]
    totals = jnp.sum(got_ref[...], axis=0)
    h12, h22, energy = totals[0:1], totals[1:2], totals[2:3]
    h32 = jnp.sqrt(jnp.maximum(energy - (h12 * h12 + h22 * h22), 0.01 * energy))
    g00 = h11 * h11 + h21 * h21
    g01 = h11 * h12 + h21 * h22
    g11 = h12 * h12 + h22 * h22 + h32 * h32
    t0, t1 = beta * h11, beta * h12
    factor = g01 / g00
    c1 = (t1 - factor * t0) / (g11 - factor * g01)
    c0 = (t0 - g01 * c1) / g00
    solution_ref[...] = guess_ref[...] + c0 * direction_ref[...] + c1 * direction_two_ref[...]
    next_ref[...] = (image_ref[...] - h12 * basis_ref[...] - h22 * basis_two_ref[...]) * (1.0 / h32)


def on_device(rhs, guess, blocks, valve, jscale, prolong, agg_map, cdiag, coff, send_rows,
              recv_rows, live_counts):
    rhs, guess, blocks, jscale, prolong = rhs[0, 0], guess[0, 0], blocks[0, 0], jscale[0, 0], prolong[0, 0]
    valve, agg, live = valve[0], agg_map[0], live_counts[0]
    send, recv = send_rows[0, 0], recv_rows[0, 0]
    size, count = guess.shape
    slots = send.shape[1]
    cpd = cdiag.shape[0]
    subs, grps = lax.axis_size("sub"), lax.axis_size("grp")
    devices = subs * grps
    period = math.lcm(cpd, LANES)
    cdiag = cdiag[None, :]
    moves = [pairing(subs, grps, side) for side in (0, 1)]

    def exchange(odd, even):
        return lax.ppermute(odd, AXES, moves[0]), lax.ppermute(even, AXES, moves[1])

    def everyone(rows):
        return lax.all_to_all(rows, AXES, 0, 0, tiled=True)

    field = ((size, count), f32)
    near = ((size, slots), f32)
    rows_out = ((devices, period // LANES + 1, LANES), f32)
    small = ((8, LANES), f32)
    items = (guess, agg, send, recv, valve)
    odd, even, notes = call(
        first_send, [near, near, ((8, LANES), jnp.int32)], *items, hbm=range(5), limit=16,
        scratch=[pltpu.VMEM(item.shape, item.dtype) for item in items]
        + [pltpu.SemaphoreType.DMA((5,))],
    )
    odd_guess, even_guess = exchange(odd, even)
    packed = ((cpd * (coff.shape[1] // LANES) + 2 * size + 16, LANES), bf16)
    items = (guess, rhs, blocks, coff, prolong, cdiag)
    local, arrive, gather, odd, even = call(
        lambda *refs: prepare(*refs[:8], cpd, *refs[8:]),
        [field, ((2 * slots, count), bf16), ((count, period), bf16), packed, packed],
        live, *items, notes, hbm=range(7),
        scratch=[pltpu.SMEM(live.shape, live.dtype)]
        + [pltpu.VMEM(item.shape, item.dtype) for item in items]
        + [pltpu.SemaphoreType.DMA((10,))],
    )
    odd, even = call(
        hand_on, [packed, packed], odd, even, odd_guess, even_guess, aliases={0: 0, 1: 1}
    )
    odd_pack, even_pack = exchange(odd, even)
    own_pack = odd
    first, rows, odd, even = call(
        residual, [field, rows_out, near, near],
        local, odd_guess, even_guess, arrive, gather, prolong, jscale, notes,
    )
    odd_first, even_first = exchange(odd, even)
    first_got = everyone(rows)
    lead, pull, matrix, odd_weights, even_weights, info = call(
        lambda *refs: look_ahead(*refs[:8], cpd, *refs[8:]), [field, field, ((3 * SLOT, coff.shape[1]), bf16), near, near, small],
        first, jscale, prolong, blocks, notes, own_pack, odd_pack, even_pack,
    )
    basis, direction, image, rows, odd, even = call(
        lambda *refs: first_step(*refs[:15], grps, cpd, *refs[15:]),
        [field, field, field, rows_out, near, near],
        first_got, odd_first, even_first, odd_weights, even_weights, matrix, info, first, lead, pull,
        jscale, prolong, notes, arrive, gather,
    )
    odd_near, even_near = exchange(odd, even)
    got = everyone(rows)
    (lead_two,) = call(look_further, [field], image, jscale, blocks, notes)
    basis_two, direction_two, image_two, scalars, rows = call(
        lambda *refs: second_step(*refs[:19], grps, cpd, *refs[19:]),
        [field, field, field, ((8, LANES), f32), ((devices, 4, LANES), f32)],
        got, first_got, odd_near, even_near, odd_first, even_first, odd_weights, even_weights, matrix,
        info, basis, image, lead, lead_two, pull, jscale, prolong, notes, arrive,
    )
    got = everyone(rows)
    solution, next_basis = call(
        finish, [field, field],
        got, scalars, guess, basis, basis_two, direction, direction_two, image_two, final=True,
    )
    return solution[None, None], next_basis[None, None]


def solution(mesh):
    return jax.shard_map(
        on_device,
        mesh=mesh,
        in_specs=(
            P("sub", "grp", None, None),
            P("sub", "grp", None, None),
            P("sub", "grp", None, None, None),
            P("sub", "grp", None),
            P("sub", "grp", None, None),
            P("sub", "grp", None, None),
            P("sub", "grp", None),
            P(("sub", "grp")),
            P(("sub", "grp"), None),
            P("sub", "grp", None, None),
            P("sub", "grp", None, None),
            P("sub", "grp", None),
        ),
        out_specs=(P("sub", "grp", None, None), P("sub", "grp", None, None)),
        check_vma=False,
    )
```

time: 51.2 us -> 47.5 us (0.928)
  waiting for transfers between devices: 10.3 us -> 7.58 us
  local copies, waits for them, and re-layouts: 2.56 us -> 0.02 us
  starting transfers between devices: 19 us -> 21.4 us
  blocking collectives: 11.1 us -> 10.2 us
    ppermute x8, starting transfers between devices: 9.75 us -> 13.2 us  [the longest x4 12 us: exchange(): lax.ppermute(even, AXES, moves[1])]
    unnamed x26 -> x8, local copies, waits for them, and re-layouts: 2.56 us -> 0.02 us
    all_to_all x2, waiting for transfers between devices: 6.63 us -> 4.43 us  [everyone(): return lax.all_to_all(rows, AXES, 0, 0, tiled=True)]
    all_to_all x2, starting transfers between devices: 9.26 us -> 8.27 us  [everyone(): return lax.all_to_all(rows, AXES, 0, 0, tiled=True)]
    all_to_all x1, blocking collectives: 11.1 us -> 10.2 us  [everyone(): return lax.all_to_all(rows, AXES, 0, 0, tiled=True)]
    pallas_call x8 -> x9, Pallas kernels: 7.13 us -> 7.16 us  [call(): pl.pallas_call(body, out_shape=[jax.ShapeDtypeStruct(shape, kind) if fina...]
  transfers between devices with their start and end apart: 10 -> 10, of which waited for: 4 -> 5; matrix products, arithmetic and copies ran while one was open for 0% -> 0% of each run, Pallas kernels for 5% -> 7%
where the time goes in v3:
time: 47.5 us; the launch traced here: 47.1 us
  starting transfers between devices  21.4 us (45%)
  blocking collectives  10.2 us (21%)
  waiting for transfers between devices  7.58 us (16%)
  Pallas kernels  7.16 us (15%)
  between operations  0.73 us (2%)
    ppermute x4, starting transfers between devices, exchange(): lax.ppermute(even, AXES, moves[1])  12 us
    all_to_all x1, blocking collectives, everyone(): return lax.all_to_all(rows, AXES, 0, 0, tiled=True)  10.2 us
    all_to_all x2, starting transfers between devices, everyone(): return lax.all_to_all(rows, AXES, 0, 0, tiled=True)  8.27 us
    pallas_call x9, Pallas kernels, call(): pl.pallas_call(body, out_shape=[jax.ShapeDtypeStruct(shape, kind) if fina...  7.16 us
    all_to_all x2, waiting for transfers between devices, everyone(): return lax.all_to_all(rows, AXES, 0, 0, tiled=True)  4.43 us
    ppermute x4, waiting for transfers between devices, exchange(): lax.ppermute(even, AXES, moves[1])  3.14 us
    ppermute x4, starting transfers between devices, exchange(): lax.ppermute(odd, AXES, moves[0])  1.15 us
  transfers between devices with their start and end apart: 10, of which 5 were waited for; matrix products, arithmetic and copies ran while one was open for 0% of the time, Pallas kernels for 7%

profile of v3, /device:TPU:0, one launch (start us, length us, event | category | flops | bytes accessed | tf_op | source)
XLA Modules:
  0.0 47.1 jit_solution(14986964452595300520)
XLA Ops:
  0.6 0.9 %shard_map.131 = (f32[64,128]{1,0:T(8,128)S(1)}, f32[64,128]{1,0:T(8,128)S(1)}, s32[8,128]{1,0:T(8,128)S(1)}) custom-call(f32[64,128]{1,0:T(8,128)} %bitcast.26, s32[1,128]{1,0:T(1,128)} %bitcast.32, s32[2,128]{1,0:T(2,128)} %bitcast.30, s32[2,128]{1,0:T(2,128)} %bitcast.31, s32[1,128]{1,0:T(1,128)} %bitcast.33), custom_call_target="tpu_custom_call" | custom-call | tf_op jit(solution)/shard_map/pallas_call | solution.py:32
  1.6 0.5 %collective-permute-start = (f32[64,128]{1,0:T(8,128)S(1)}, f32[64,128]{1,0:T(8,128)S(1)}, u32[]{:S(2)}, u32[]{:S(2)}) collective-permute-start(f32[64,128]{1,0:T(8,128)S(1)} %get-tuple-element.37), channel_id=1, source_target_pairs={{0,1},{1,0},{2,3},{3,2},{4,8},{5,9},{6,10},{7,11},{8,4},{9,5},{10,... | collective-permute-start | bytes 98312 | tf_op jit(solution)/shard_map/ppermute | solution.py:410
  2.1 4.0 %collective-permute-start.1 = (f32[64,128]{1,0:T(8,128)S(1)}, f32[64,128]{1,0:T(8,128)S(1)}, u32[]{:S(2)}, u32[]{:S(2)}) collective-permute-start(f32[64,128]{1,0:T(8,128)S(1)} %get-tuple-element.38), channel_id=1, source_target_pairs={{0,4},{1,5},{2,6},{3,7},{4,0},{5,1},{6,2},{7,3},{8,12},{9,13},{10,... | collective-permute-start | bytes 98312 | tf_op jit(solution)/shard_map/ppermute | solution.py:410
  6.1 0.0 copy-start
  6.1 1.6 %shard_map.132 = (f32[64,128]{1,0:T(8,128)S(1)}, bf16[256,128]{1,0:T(8,128)(2,1)S(1)}, bf16[128,384]{1,0:T(8,128)(2,1)S(1)}, bf16[720,128]{1,0:T(8,128)(2,1)S(1)}, bf16[720,128]{1,0:T(8,128)(2,1)S(1)}) custom-call(s32[1,2]{1,0:T(1,128)} %bitcast.34, f32[64,128]{1,0:T(8,128)} %bitcast.27, f32[64,128]{1,0:T(8,128)} %bitcast.29, bf16[64,64,128]{2,1,0:T(8,128)(2,1)} %bitcast.13, ...), custom_call_target="tpu_custom_call" | custom-call | tf_op jit(solution)/shard_map/pallas_call | solution.py:32
  7.7 0.0 collective-permute-done.odd_near_ref.odd_after_ref
  7.7 0.3 collective-permute-done.1.even_near_ref.even_after_ref
  8.0 0.0 copy-start.1
  8.0 0.0 copy-start.2
  8.0 2.0 %collective-permute-start.5 = (bf16[720,128]{1,0:T(8,128)(2,1)S(1)}, bf16[720,128]{1,0:T(8,128)(2,1)S(1)}, u32[]{:S(2)}, u32[]{:S(2)}) collective-permute-start(bf16[720,128]{1,0:T(8,128)(2,1)S(1)} %get-tuple-element.48), channel_id=1, source_target_pairs={{0,4},{1,5},{2,6},{3,7},{4,0},{5,1},{6,2},{7,3},{8,12},{9,13},{10,... | collective-permute-start | bytes 552968 | tf_op jit(solution)/shard_map/ppermute | solution.py:410
  10.0 0.0 collective-permute-start.4
  10.0 0.0 copy-done.1
  10.0 0.0 copy-done.2
  10.0 1.0 %shard_map.133 = (f32[64,128]{1,0:T(8,128)S(1)}, f32[32,4,128]{2,1,0:T(4,128)}, f32[64,128]{1,0:T(8,128)S(1)}, f32[64,128]{1,0:T(8,128)S(1)}) custom-call(f32[64,128]{1,0:T(8,128)S(1)} %get-tuple-element.36.local_ref, f32[64,128]{1,0:T(8,128)S(1)} %collective-permute-done.odd_near_ref.odd_after_ref, ...), custom_call_target="tpu_custom_call" | custom-call | tf_op jit(solution)/shard_map/pallas_call | solution.py:32
  11.0 5.3 %all-to-all-start = ((f32[32,4,128]{2,1,0:T(4,128)}), f32[32,4,128]{2,1,0:T(4,128)S(1)}, u32[]{:S(2)}, u32[]{:S(2)}) async-start(f32[32,4,128]{2,1,0:T(4,128)} %get-tuple-element.41), calls=%async_computation | async-start | bytes 131072 | tf_op jit(solution)/shard_map/all_to_all | solution.py:413
  16.3 0.3 collective-permute-start.2
  16.7 3.0 %collective-permute-start.3 = (f32[64,128]{1,0:T(8,128)S(1)}, f32[64,128]{1,0:T(8,128)S(1)}, u32[]{:S(2)}, u32[]{:S(2)}) collective-permute-start(f32[64,128]{1,0:T(8,128)S(1)} %get-tuple-element.43), channel_id=1, source_target_pairs={{0,4},{1,5},{2,6},{3,7},{4,0},{5,1},{6,2},{7,3},{8,12},{9,13},{10,... | collective-permute-start | bytes 98312 | tf_op jit(solution)/shard_map/ppermute | solution.py:410
  19.6 0.0 collective-permute-done.5.refs_7_
  19.6 0.0 collective-permute-done.4.refs_6_
  19.6 0.0 copy-done
  19.7 0.6 %shard_map.135 = (f32[64,128]{1,0:T(8,128)S(1)}, f32[64,128]{1,0:T(8,128)S(1)}, bf16[192,1536]{1,0:T(8,128)(2,1)S(1)}, f32[64,128]{1,0:T(8,128)S(1)}, f32[64,128]{1,0:T(8,128)S(1)}, /*index=5*/f32[8,128]{1,0:T(8,128)S(1)}) custom-call(f32[64,128]{1,0:T(8,128)S(1)} %get-tuple-element.44.refs_0_.refs_7_, f32[64,128]{1,0:T(8,128)S(1)} %bitcast.22, ...), custom_call_target="tpu_custom_call" | custom-call | tf_op jit(solution)/shard_map/pallas_call | solution.py:32
  20.3 0.0 collective-permute-done.2.refs_1_.refs_4_
  20.3 1.3 %collective-permute-done.3.refs_2_.refs_5_ = f32[64,128]{1,0:T(8,128)S(1)} collective-permute-done((f32[64,128]{1,0:T(8,128)S(1)}, f32[64,128]{1,0:T(8,128)S(1)}, u32[]{:S(2)}, u32[]{:S(2)}) %collective-permute-start.3) | collective-permute-done | bytes 32800 | tf_op jit(solution)/shard_map/ppermute | solution.py:410
  21.5 2.2 %all-to-all-done.refs_0_.refs_1_ = f32[32,4,128]{2,1,0:T(4,128)S(1)} async-done(((f32[32,4,128]{2,1,0:T(4,128)}), f32[32,4,128]{2,1,0:T(4,128)S(1)}, u32[]{:S(2)}, u32[]{:S(2)}) %all-to-all-start) | async-done | bytes 65568 | tf_op jit(solution)/shard_map/all_to_all | solution.py:413
  23.8 1.4 %shard_map.136 = (f32[64,128]{1,0:T(8,128)S(1)}, f32[64,128]{1,0:T(8,128)S(1)}, f32[64,128]{1,0:T(8,128)S(1)}, f32[32,4,128]{2,1,0:T(4,128)}, f32[64,128]{1,0:T(8,128)S(1)}, /*index=5*/f32[64,128]{1,0:T(8,128)S(1)}) custom-call(f32[32,4,128]{2,1,0:T(4,128)S(1)} %all-to-all-done.refs_0_.refs_1_, f32[64,128]{1,0:T(8,128)S(1)} %collective-permute-done.2.refs_1_.refs_4_, ...), custom_call_target="tpu_custom_call" | custom-call | tf_op jit(solution)/shard_map/pallas_call | solution.py:32
  25.1 2.9 %all-to-all-start.1 = ((f32[32,4,128]{2,1,0:T(4,128)}), f32[32,4,128]{2,1,0:T(4,128)S(1)}, u32[]{:S(2)}, u32[]{:S(2)}) async-start(f32[32,4,128]{2,1,0:T(4,128)} %get-tuple-element.55), calls=%async_computation.1 | async-start | bytes 131072 | tf_op jit(solution)/shard_map/all_to_all | solution.py:413
  28.1 0.3 collective-permute-start.6
  28.4 3.0 %collective-permute-start.7 = (f32[64,128]{1,0:T(8,128)S(1)}, f32[64,128]{1,0:T(8,128)S(1)}, u32[]{:S(2)}, u32[]{:S(2)}) collective-permute-start(f32[64,128]{1,0:T(8,128)S(1)} %get-tuple-element.57), channel_id=1, source_target_pairs={{0,4},{1,5},{2,6},{3,7},{4,0},{5,1},{6,2},{7,3},{8,12},{9,13},{10,... | collective-permute-start | bytes 98312 | tf_op jit(solution)/shard_map/ppermute | solution.py:410
  31.4 0.3 shard_map.137.refs_13_
  31.7 0.0 collective-permute-done.6.refs_2_
  31.7 1.6 %collective-permute-done.7.refs_3_ = f32[64,128]{1,0:T(8,128)S(1)} collective-permute-done((f32[64,128]{1,0:T(8,128)S(1)}, f32[64,128]{1,0:T(8,128)S(1)}, u32[]{:S(2)}, u32[]{:S(2)}) %collective-permute-start.7) | collective-permute-done | bytes 32800 | tf_op jit(solution)/shard_map/ppermute | solution.py:410
  33.3 2.2 %all-to-all-done.1.refs_0_ = f32[32,4,128]{2,1,0:T(4,128)S(1)} async-done(((f32[32,4,128]{2,1,0:T(4,128)}), f32[32,4,128]{2,1,0:T(4,128)S(1)}, u32[]{:S(2)}, u32[]{:S(2)}) %all-to-all-start.1) | async-done | bytes 65568 | tf_op jit(solution)/shard_map/all_to_all | solution.py:413
  35.5 0.7 %shard_map.138 = (f32[64,128]{1,0:T(8,128)S(1)}, f32[64,128]{1,0:T(8,128)S(1)}, f32[64,128]{1,0:T(8,128)S(1)}, f32[8,128]{1,0:T(8,128)S(1)}, f32[32,4,128]{2,1,0:T(4,128)S(1)}) custom-call(f32[32,4,128]{2,1,0:T(4,128)S(1)} %all-to-all-done.1.refs_0_, f32[32,4,128]{2,1,0:T(4,128)S(1)} %all-to-all-done.refs_0_.refs_1_, ...), custom_call_target="tpu_custom_call" | custom-call | tf_op jit(solution)/shard_map/pallas_call | solution.py:32
  36.2 0.0 copy-start.3
  36.2 10.2 %all_to_all.15.got_ref = f32[32,4,128]{2,1,0:T(4,128)S(1)} all-to-all(f32[32,4,128]{2,1,0:T(4,128)S(1)} %get-tuple-element.60), channel_id=1, replica_groups=mesh['sub'=8,'grp'=4] {'sub','grp'}, dimensions={0} | all-to-all | bytes 131072 | tf_op jit(solution)/shard_map/all_to_all | solution.py:413
  46.4 0.0 copy-done.3
  46.4 0.7 %shard_map.139 = (f32[64,128]{1,0:T(8,128)}, f32[64,128]{1,0:T(8,128)}) custom-call(f32[32,4,128]{2,1,0:T(4,128)S(1)} %all_to_all.15.got_ref, f32[8,128]{1,0:T(8,128)S(1)} %get-tuple-element.61.scalars_ref, f32[64,128]{1,0:T(8,128)S(1)} %bitcast.28, f32[64,128]{1,0:T(8,128)S(1)} %get-tuple-element.58.refs_10_.basis_ref, ...), custom_call_target="tpu_custom_call" | custom-call | tf_op jit(solution)/shard_map/pallas_call | solution.py:32
  (1 shorter events, 0.0 us)
Async XLA Ops:
  1.6 6.2 %collective-permute-start = (f32[64,128]{1,0:T(8,128)S(1)}, f32[64,128]{1,0:T(8,128)S(1)}, u32[]{:S(2)}, u32[]{:S(2)}) collective-permute-start(f32[64,128]{1,0:T(8,128)S(1)} %get-tuple-element.37), channel_id=1, source_target_pairs={{0,1},{1,0},{2,3},{3,2},{4,8},{5,9},{6,10},{7,11},{8,4},{9,5},{10,... | collective-permute-start | bytes 98312 | tf_op jit(solution)/shard_map/ppermute | solution.py:410
  2.1 5.9 %collective-permute-start.1 = (f32[64,128]{1,0:T(8,128)S(1)}, f32[64,128]{1,0:T(8,128)S(1)}, u32[]{:S(2)}, u32[]{:S(2)}) collective-permute-start(f32[64,128]{1,0:T(8,128)S(1)} %get-tuple-element.38), channel_id=1, source_target_pairs={{0,4},{1,5},{2,6},{3,7},{4,0},{5,1},{6,2},{7,3},{8,12},{9,13},{10,... | collective-permute-start | bytes 98312 | tf_op jit(solution)/shard_map/ppermute | solution.py:410
  6.1 13.5 %copy-start = (bf16[1,1,64,64,128]{4,3,2,1,0:T(8,128)(2,1)S(1)}, bf16[1,1,64,64,128]{4,3,2,1,0:T(8,128)(2,1)}, u32[]{:S(2)}) copy-start(bf16[1,1,64,64,128]{4,3,2,1,0:T(8,128)(2,1)} %param.14) | copy-start | bytes 3145732
  8.0 2.0 %copy-start.1 = (f32[1,1,64,128]{3,2,1,0:T(8,128)S(1)}, f32[1,1,64,128]{3,2,1,0:T(8,128)}, u32[]{:S(2)}) copy-start(f32[1,1,64,128]{3,2,1,0:T(8,128)} %param.17) | copy-start | bytes 98308
  8.0 2.0 %copy-start.2 = (f32[1,1,64,128]{3,2,1,0:T(8,128)S(1)}, f32[1,1,64,128]{3,2,1,0:T(8,128)}, u32[]{:S(2)}) copy-start(f32[1,1,64,128]{3,2,1,0:T(8,128)} %param.16) | copy-start | bytes 98308
  8.0 11.6 %collective-permute-start.5 = (bf16[720,128]{1,0:T(8,128)(2,1)S(1)}, bf16[720,128]{1,0:T(8,128)(2,1)S(1)}, u32[]{:S(2)}, u32[]{:S(2)}) collective-permute-start(bf16[720,128]{1,0:T(8,128)(2,1)S(1)} %get-tuple-element.48), channel_id=1, source_target_pairs={{0,4},{1,5},{2,6},{3,7},{4,0},{5,1},{6,2},{7,3},{8,12},{9,13},{10,... | collective-permute-start | bytes 552968 | tf_op jit(solution)/shard_map/ppermute | solution.py:410
  10.0 9.6 %collective-permute-start.4 = (bf16[720,128]{1,0:T(8,128)(2,1)S(1)}, bf16[720,128]{1,0:T(8,128)(2,1)S(1)}, u32[]{:S(2)}, u32[]{:S(2)}) collective-permute-start(bf16[720,128]{1,0:T(8,128)(2,1)S(1)} %get-tuple-element.47.refs_5_), channel_id=1, source_target_pairs={{0,1},{1,0},{2,3},{3,2},{4,8},{5,9},{6,10},{7,11},{8,4},{9,5},{10,... | collective-permute-start | bytes 552968 | tf_op jit(solution)/shard_map/ppermute | solution.py:410
  11.0 12.8 %all-to-all-start = ((f32[32,4,128]{2,1,0:T(4,128)}), f32[32,4,128]{2,1,0:T(4,128)S(1)}, u32[]{:S(2)}, u32[]{:S(2)}) async-start(f32[32,4,128]{2,1,0:T(4,128)} %get-tuple-element.41), calls=%async_computation | async-start | bytes 131072 | tf_op jit(solution)/shard_map/all_to_all | solution.py:413
  16.3 3.9 %collective-permute-start.2 = (f32[64,128]{1,0:T(8,128)S(1)}, f32[64,128]{1,0:T(8,128)S(1)}, u32[]{:S(2)}, u32[]{:S(2)}) collective-permute-start(f32[64,128]{1,0:T(8,128)S(1)} %get-tuple-element.42), channel_id=1, source_target_pairs={{0,1},{1,0},{2,3},{3,2},{4,8},{5,9},{6,10},{7,11},{8,4},{9,5},{10,... | collective-permute-start | bytes 98312 | tf_op jit(solution)/shard_map/ppermute | solution.py:410
  16.7 4.9 %collective-permute-start.3 = (f32[64,128]{1,0:T(8,128)S(1)}, f32[64,128]{1,0:T(8,128)S(1)}, u32[]{:S(2)}, u32[]{:S(2)}) collective-permute-start(f32[64,128]{1,0:T(8,128)S(1)} %get-tuple-element.43), channel_id=1, source_target_pairs={{0,4},{1,5},{2,6},{3,7},{4,0},{5,1},{6,2},{7,3},{8,12},{9,13},{10,... | collective-permute-start | bytes 98312 | tf_op jit(solution)/shard_map/ppermute | solution.py:410
  25.1 10.4 %all-to-all-start.1 = ((f32[32,4,128]{2,1,0:T(4,128)}), f32[32,4,128]{2,1,0:T(4,128)S(1)}, u32[]{:S(2)}, u32[]{:S(2)}) async-start(f32[32,4,128]{2,1,0:T(4,128)} %get-tuple-element.55), calls=%async_computation.1 | async-start | bytes 131072 | tf_op jit(solution)/shard_map/all_to_all | solution.py:413
  28.1 3.6 %collective-permute-start.6 = (f32[64,128]{1,0:T(8,128)S(1)}, f32[64,128]{1,0:T(8,128)S(1)}, u32[]{:S(2)}, u32[]{:S(2)}) collective-permute-start(f32[64,128]{1,0:T(8,128)S(1)} %get-tuple-element.56), channel_id=1, source_target_pairs={{0,1},{1,0},{2,3},{3,2},{4,8},{5,9},{6,10},{7,11},{8,4},{9,5},{10,... | collective-permute-start | bytes 98312 | tf_op jit(solution)/shard_map/ppermute | solution.py:410
  28.4 4.9 %collective-permute-start.7 = (f32[64,128]{1,0:T(8,128)S(1)}, f32[64,128]{1,0:T(8,128)S(1)}, u32[]{:S(2)}, u32[]{:S(2)}) collective-permute-start(f32[64,128]{1,0:T(8,128)S(1)} %get-tuple-element.57), channel_id=1, source_target_pairs={{0,4},{1,5},{2,6},{3,7},{4,0},{5,1},{6,2},{7,3},{8,12},{9,13},{10,... | collective-permute-start | bytes 98312 | tf_op jit(solution)/shard_map/ppermute | solution.py:410
  36.2 10.2 %copy-start.3 = (f32[1,1,64,128]{3,2,1,0:T(8,128)S(1)}, f32[1,1,64,128]{3,2,1,0:T(8,128)}, u32[]{:S(2)}) copy-start(f32[1,1,64,128]{3,2,1,0:T(8,128)} %param.13) | copy-start | bytes 98308

commit v4 on v3

--- a/solution.py
+++ b/solution.py
@@ -103,25 +103,30 @@
     row = lax.broadcasted_iota(jnp.int32, (8, weighted.shape[1]), 0)
     stack = jnp.where(row == 0, high, jnp.where(row == 1, middle, jnp.where(row == 2, last, 0.0)))
     sums = jnp.dot(stack.astype(bf16), gather_ref[...], preferred_element_type=f32)
-    sums = jnp.sum(sums, axis=0, keepdims=True)
-    return [sums[:, at : at + LANES] for at in range(0, sums.shape[1], LANES)]
+    return jnp.sum(sums, axis=0, keepdims=True)
 
 
 def total(field):
-    value = jnp.sum(jnp.sum(field, axis=0, keepdims=True), axis=1, keepdims=True)
-    return jnp.broadcast_to(value, (1, LANES))
-
-
-def halves(first, second):
-    return jnp.where(lax.broadcasted_iota(jnp.int32, (1, LANES), 1) < LANES // 2, first, second)
-
-
-def turned(row):
-    return pltpu.roll(jnp.broadcast_to(row, (8, LANES)), LANES // 2, 1)[0:1]
-
-
-def to_all(ref, rows):
-    ref[...] = jnp.broadcast_to(jnp.concatenate(rows, axis=0)[None], ref.shape)
+    return jnp.sum(jnp.sum(field, axis=0, keepdims=True), axis=1, keepdims=True)
+
+
+def to_all(ref, row, first_lane, totals):
+    lane = lax.broadcasted_iota(jnp.int32, (1, LANES), 1)
+    for at, value in enumerate(totals):
+        row = jnp.where(lane == first_lane + at, value, row)
+    ref[...] = jnp.broadcast_to(row, ref.shape)
+
+
+def flat(ref):
+    return ref[...] if len(ref.shape) == 2 else ref[:, 0, :]
+
+
+def summed(ref, first_lane, count):
+    rows = jnp.broadcast_to(jnp.sum(flat(ref), axis=0, keepdims=True), (8, LANES))
+    return [
+        jnp.take_along_axis(rows, jnp.full((8, LANES), first_lane + at, jnp.int32), axis=1)[0:1]
+        for at in range(count)
+    ]
 
 
 def copy_all(pairs, sems):
@@ -169,7 +174,7 @@
 
 
 def prepare(live_hbm, guess_hbm, rhs_hbm, blocks_hbm, coff_hbm, prolong_hbm, cdiag_hbm, notes_ref,
-            cpd, local_ref, arrive_ref, gather_ref, odd_ref, even_ref,
+            local_ref, arrive_ref, gather_ref, odd_ref, even_ref,
             live_ref, guess_ref, rhs_ref, blocks_ref, coff_ref, prolong_ref, cdiag_ref, sems):
     size = guess_ref.shape[0]
     chunk = size // 4
@@ -186,8 +191,7 @@
         pack_constants(ref, coff_ref, prolong_ref[...], notes_ref[AGG], cdiag, places)
     count = arrive_ref.shape[1]
     slots = notes_ref.shape[1]
-    period = gather_ref.shape[1]
-    coarse = lax.rem(lax.broadcasted_iota(jnp.int32, (period, count), 0), cpd)
+    coarse = lax.broadcasted_iota(jnp.int32, (LANES, count), 0)
     gather_ref[...] = jnp.where(notes_ref[AGG] == coarse, 1.0, 0.0).T.astype(bf16)
     place = lax.axis_index("sub")
     row = lax.broadcasted_iota(jnp.int32, (count, slots), 0)
@@ -211,29 +215,27 @@
     local_ref[...] = rhs_ref[...] - local_ref[...]
 
 
-def hand_on(odd_ref, even_ref, odd_after_ref, even_after_ref, odd_out_ref, even_out_ref):
-    pass
-
-
 def residual(local_ref, odd_near_ref, even_near_ref, arrive_ref, gather_ref, prolong_ref,
-             jscale_ref, notes_ref, first_ref, out_ref, odd_ref, even_ref):
+             jscale_ref, notes_ref, odd_pack_ref, even_pack_ref, cpd, first_ref, out_ref, odd_ref,
+             even_ref):
     near = [odd_near_ref[...], even_near_ref[...]]
     first = local_ref[...] + coupling * received(near, arrive_ref)
     first_ref[...] = first
     weighted = jnp.sum(prolong_ref[...] * first, axis=0, keepdims=True)
-    to_all(out_ref, restricted(weighted, gather_ref) + [total(first * first)])
+    to_all(out_ref, restricted(weighted, gather_ref), cpd, [total(first * first)])
     scaled = jscale_ref[...] * first
+    size = first.shape[0]
+    tail = odd_ref.shape[0] - 2 * size
     for side, ref in enumerate((odd_ref, even_ref)):
-        ref[...] = pick(scaled, row_of(notes_ref.at[SEND], parity(side)))
-
-
-def look_ahead(first_ref, jscale_ref, prolong_ref, blocks_ref, notes_ref, own_ref, odd_ref,
-               even_ref, cpd, lead_ref, pull_ref, matrix_ref, odd_weights_ref, even_weights_ref,
-               info_ref):
-    lead_ref[...] = local_product(blocks_ref, notes_ref[VALVE], jscale_ref[...] * first_ref[...])
-    pull_ref[...] = local_product(blocks_ref, notes_ref[VALVE], prolong_ref[...])
+        high, low = pieces(pick(scaled, row_of(notes_ref.at[SEND], parity(side))))
+        ref[tail : tail + size, :] = high
+        ref[tail + size :, :] = low
+
+
+def unpack(own_ref, even_ref, odd_ref, cpd, matrix_ref, odd_weights_ref, even_weights_ref,
+           odd_first_ref, even_first_ref, info_ref):
     width = matrix_ref.shape[1]
-    size = first_ref.shape[0]
+    size = odd_first_ref.shape[0]
     base = cpd * (width // LANES)
     rows = []
     for slot, ref in enumerate((own_ref, odd_ref, even_ref)):
@@ -242,56 +244,66 @@
             matrix_ref[slot * SLOT : slot * SLOT + cpd, at : at + LANES] = ref[start : start + cpd, :]
         matrix_ref[slot * SLOT + cpd : (slot + 1) * SLOT, :] = jnp.zeros((SLOT - cpd, width), bf16)
         rows.append(ref[base + 2 * size : base + 2 * size + 16, :].astype(f32))
-    for ref, weights_ref in ((odd_ref, odd_weights_ref), (even_ref, even_weights_ref)):
-        weights_ref[...] = ref[base : base + size, :].astype(f32) + ref[
-            base + size : base + 2 * size, :
-        ].astype(f32)
+    for ref, weights_ref, near_ref in (
+        (odd_ref, odd_weights_ref, odd_first_ref), (even_ref, even_weights_ref, even_first_ref)
+    ):
+        for start, to_ref in ((base, weights_ref), (base + 2 * size + 16, near_ref)):
+            high, low = ref[start : start + size, :], ref[start + size : start + 2 * size, :]
+            to_ref[...] = high.astype(f32) + low.astype(f32)
     infos = [row[1:2] + row[2:3] + row[3:4] for row in rows] + [row[0:1] for row in rows[1:]]
     info_ref[...] = jnp.concatenate(infos + [jnp.zeros((3, LANES), f32)], axis=0)
 
 
-def look_further(image_ref, jscale_ref, blocks_ref, notes_ref, lead_ref):
-    lead_ref[...] = local_product(blocks_ref, notes_ref[VALVE], jscale_ref[...] * image_ref[...])
-
-
-def compact(got_ref, cpd):
-    count, rows, _ = got_ref.shape
-    shape = (rows, LANES)
-    place = lax.broadcasted_iota(jnp.int32, shape, 0) * LANES + lax.broadcasted_iota(jnp.int32, shape, 1)
-    owner = place // cpd
-    group = (rows - 1) * LANES // cpd
-    parts, sums = [], jnp.zeros(shape, f32)
-    for at in range(0, count, group):
-        part = jnp.zeros(shape, f32)
-        for step in range(group):
-            tile = got_ref[at + step]
-            part = jnp.where(owner == step, tile, part)
-            sums = sums + tile
-        parts.append(part)
-    return parts, sums
-
-
-def solve_coarse(parts, matrix_ref, near_rows, info_ref):
-    rows = parts[0].shape[0] - 1
-    vector = jnp.concatenate([part[at : at + 1] for part in parts for at in range(rows)], axis=1)
+def look_ahead(image_ref, first_ref, jscale_ref, prolong_ref, blocks_ref, notes_ref,
+               lead_two_ref, lead_ref, pull_ref):
+    valve, jscale = notes_ref[VALVE], jscale_ref[...]
+    lead_two_ref[...] = local_product(blocks_ref, valve, jscale * image_ref[...])
+    lead_ref[...] = local_product(blocks_ref, valve, jscale * first_ref[...])
+    pull_ref[...] = local_product(blocks_ref, valve, prolong_ref[...])
+
+
+def solve_coarse(parts, matrix_ref, near_rows, cdiags, cpd):
+    group = parts[0].shape[0]
+    shape = (group, LANES)
+    row = lax.broadcasted_iota(jnp.int32, shape, 0)
+    lane = lax.broadcasted_iota(jnp.int32, shape, 1)
+    masks = [(at + lane) // cpd == row for at in range(0, group * cpd, LANES)]
+    source = lax.rem(lane - cpd * row + cpd * group, LANES)
+    tiles = []
+    for part in parts:
+        shifted = jnp.take_along_axis(part, source, axis=1)
+        tiles.extend(jnp.where(mask, shifted, 0.0) for mask in masks)
     product = lax.dot_general(
-        jnp.broadcast_to(vector, (8, vector.shape[1])).astype(bf16), matrix_ref[...],
-        (((1,), (1,)), ((), ())), preferred_element_type=f32,
-    )[0:1]
+        jnp.concatenate(tiles, axis=1).astype(bf16), matrix_ref[...], (((1,), (1,)), ((), ())),
+        preferred_element_type=f32,
+    )
+    product = jnp.sum(product, axis=0, keepdims=True)
     low = product[:, :LANES]
     high = jnp.concatenate([product[:, LANES:], jnp.zeros((1, LANES - SLOT), f32)], axis=1)
-    shares = (low, turned(low), high)
-    return [
-        info_ref[at : at + 1, :] * row + share
-        for at, (row, share) in enumerate(zip(near_rows, shares))
-    ]
-
-
-def rows_near(got_ref, grp_size):
-    count = got_ref.shape[0]
+    turned = pltpu.roll(jnp.broadcast_to(low, (8, LANES)), LANES - SLOT, 1)[0:1]
+    shares = (low, turned, high)
+    return [cdiag * row + share for cdiag, row, share in zip(cdiags, near_rows, shares)]
+
+
+def parts_of(ref, cpd):
+    group = math.lcm(cpd, LANES) // cpd
+    rows = flat(ref)
+    return [rows[at : at + group, :] for at in range(0, rows.shape[0], group)]
+
+
+def rows_near(parts, grp_size):
+    group = parts[0].shape[0]
+    count = group * len(parts)
     me = lax.axis_index("sub") * grp_size + lax.axis_index("grp")
-    shifts = [0] + [grp_size * (1 - 2 * parity(side)) for side in (0, 1)]
-    return [got_ref[lax.rem(me + shift + count, count)][0:1] for shift in shifts]
+    place = lax.broadcasted_iota(jnp.int32, parts[0].shape, 0)
+    rows = []
+    for shift in [0] + [grp_size * (1 - 2 * parity(side)) for side in (0, 1)]:
+        wanted = lax.rem(me + shift + count, count)
+        found = jnp.where(place == wanted, parts[0], 0.0)
+        for at, part in enumerate(parts[1:], 1):
+            found = jnp.where(place + at * group == wanted, part, found)
+        rows.append(jnp.sum(found, axis=0, keepdims=True))
+    return rows
 
 
 def spread_of(solution, agg):
@@ -304,29 +316,32 @@
     return weights_ref[...] * spread_of(solution, agg)
 
 
-def first_step(got_ref, odd_near_ref, even_near_ref, odd_weights_ref, even_weights_ref, matrix_ref,
-               info_ref, first_ref, lead_ref, pull_ref, jscale_ref, prolong_ref, notes_ref,
-               arrive_ref, gather_ref, grp_size, cpd,
-               basis_ref, direction_ref, image_ref, out_ref, odd_ref, even_ref):
-    parts, sums = compact(got_ref, cpd)
-    rows = sums.shape[0]
-    inverse = 1.0 / jnp.sqrt(sums[rows - 1 : rows])
-    own_rows = [row * inverse for row in rows_near(got_ref, grp_size)]
-    solved = solve_coarse([part * inverse for part in parts], matrix_ref, own_rows, info_ref)
+def first_step(got_ref, own_pack_ref, even_pack_ref, odd_pack_ref, first_ref, jscale_ref,
+               prolong_ref, blocks_ref, notes_ref, arrive_ref, gather_ref, grp_size, cpd,
+               basis_ref, direction_ref, image_ref, out_ref, odd_ref, even_ref, matrix_ref,
+               odd_weights_ref, even_weights_ref, odd_near_ref, even_near_ref, info_ref):
+    unpack(own_pack_ref, even_pack_ref, odd_pack_ref, cpd, matrix_ref, odd_weights_ref,
+           even_weights_ref, odd_near_ref, even_near_ref, info_ref)
+    inverse = 1.0 / jnp.sqrt(summed(got_ref, cpd, 1)[0])
+    parts = [part * inverse for part in parts_of(got_ref, cpd)]
+    cdiags = [info_ref[at : at + 1, :] for at in range(3)]
+    solved = solve_coarse(parts, matrix_ref, rows_near(parts, grp_size), cdiags, cpd)
     basis = first_ref[...] * inverse
     basis_ref[...] = basis
     spread = spread_of(solved[0], notes_ref[AGG])
     jscale, prolong = jscale_ref[...], prolong_ref[...]
-    direction_ref[...] = jscale * basis + prolong * spread
+    direction = jscale * basis + prolong * spread
+    direction_ref[...] = direction
     near = [
         odd_near_ref[...] * inverse + near_spread(odd_weights_ref, info_ref, 0, solved[1]),
         even_near_ref[...] * inverse + near_spread(even_weights_ref, info_ref, 1, solved[2]),
     ]
-    image = lead_ref[...] * inverse + pull_ref[...] * spread - coupling * received(near, arrive_ref)
+    image = local_product(blocks_ref, notes_ref[VALVE], direction)
+    image = image - coupling * received(near, arrive_ref)
     image_ref[...] = image
     weighted = jnp.sum(prolong * image, axis=0, keepdims=True)
-    dots = halves(total(basis * image), total(image * image))
-    to_all(out_ref, restricted(weighted, gather_ref) + [dots])
+    dots = [total(basis * image), total(image * image)]
+    to_all(out_ref, restricted(weighted, gather_ref), cpd, dots)
     scaled = jscale * image
     for side, ref in enumerate((odd_ref, even_ref)):
         ref[...] = pick(scaled, row_of(notes_ref.at[SEND], parity(side)))
@@ -336,13 +351,8 @@
                 odd_weights_ref, even_weights_ref, matrix_ref, info_ref, basis_ref, image_ref,
                 lead_ref, lead_two_ref, pull_ref, jscale_ref, prolong_ref, notes_ref, arrive_ref,
                 grp_size, cpd, basis_two_ref, direction_ref, image_two_ref, scalars_ref, out_ref):
-    first_parts, first_sums = compact(first_got_ref, cpd)
-    parts, sums = compact(got_ref, cpd)
-    rows = sums.shape[0]
-    beta = jnp.sqrt(first_sums[rows - 1 : rows])
-    totals = sums[rows - 1 : rows]
-    swapped = turned(totals)
-    along, energy = halves(totals, swapped), halves(swapped, totals)
+    beta = jnp.sqrt(summed(first_got_ref, cpd, 1)[0])
+    along, energy = summed(got_ref, cpd, 2)
     height = jnp.sqrt(jnp.maximum(energy - along * along, 0.01 * energy))
     inverse = 1.0 / height
     slope = along / beta
@@ -350,13 +360,11 @@
     def mixed(new, old):
         return (new - slope * old) * inverse
 
-    own_rows = [
-        mixed(new, old)
-        for new, old in zip(rows_near(got_ref, grp_size), rows_near(first_got_ref, grp_size))
+    parts = [
+        mixed(new, old) for new, old in zip(parts_of(got_ref, cpd), parts_of(first_got_ref, cpd))
     ]
-    solved = solve_coarse(
-        [mixed(new, old) for new, old in zip(parts, first_parts)], matrix_ref, own_rows, info_ref
-    )
+    cdiags = [info_ref[at : at + 1, :] for at in range(3)]
+    solved = solve_coarse(parts, matrix_ref, rows_near(parts, grp_size), cdiags, cpd)
     basis = (image_ref[...] - along * basis_ref[...]) * inverse
     basis_two_ref[...] = basis
     spread = spread_of(solved[0], notes_ref[AGG])
@@ -371,15 +379,14 @@
     image = image - coupling * received(near, arrive_ref)
     image_two_ref[...] = image
     scalars_ref[...] = jnp.concatenate([beta, along, height, jnp.zeros((5, LANES), f32)], axis=0)
-    to_all(out_ref, [total(basis_ref[...] * image), total(basis * image), total(image * image),
-                     jnp.zeros((1, LANES), f32)])
+    dots = [total(basis_ref[...] * image), total(basis * image), total(image * image)]
+    to_all(out_ref, jnp.zeros((1, LANES), f32), 0, dots)
 
 
 def finish(got_ref, scalars_ref, guess_ref, basis_ref, basis_two_ref, direction_ref,
            direction_two_ref, image_ref, solution_ref, next_ref):
     beta, h11, h21 = scalars_ref[0:1, :], scalars_ref[1:2, :], scalars_ref[2:3, :]
-    totals = jnp.sum(got_ref[...], axis=0)
-    h12, h22, energy = totals[0:1], totals[1:2], totals[2:3]
+    h12, h22, energy = summed(got_ref, 0, 3)
     h32 = jnp.sqrt(jnp.maximum(energy - (h12 * h12 + h22 * h22), 0.01 * energy))
     g00 = h11 * h11 + h21 * h21
     g01 = h11 * h12 + h21 * h22
@@ -402,7 +409,6 @@
     cpd = cdiag.shape[0]
     subs, grps = lax.axis_size("sub"), lax.axis_size("grp")
     devices = subs * grps
-    period = math.lcm(cpd, LANES)
     cdiag = cdiag[None, :]
     moves = [pairing(subs, grps, side) for side in (0, 1)]
 
@@ -414,7 +420,7 @@
 
     field = ((size, count), f32)
     near = ((size, slots), f32)
-    rows_out = ((devices, period // LANES + 1, LANES), f32)
+    rows_out = ((devices, LANES), f32)
     small = ((8, LANES), f32)
     items = (guess, agg, send, recv, valve)
     odd, even, notes = call(
@@ -423,43 +429,41 @@
         + [pltpu.SemaphoreType.DMA((5,))],
     )
     odd_guess, even_guess = exchange(odd, even)
-    packed = ((cpd * (coff.shape[1] // LANES) + 2 * size + 16, LANES), bf16)
+    packed = ((cpd * (coff.shape[1] // LANES) + 4 * size + 16, LANES), bf16)
     items = (guess, rhs, blocks, coff, prolong, cdiag)
     local, arrive, gather, odd, even = call(
-        lambda *refs: prepare(*refs[:8], cpd, *refs[8:]),
-        [field, ((2 * slots, count), bf16), ((count, period), bf16), packed, packed],
+        prepare,
+        [field, ((2 * slots, count), bf16), ((count, LANES), bf16), packed, packed],
         live, *items, notes, hbm=range(7),
         scratch=[pltpu.SMEM(live.shape, live.dtype)]
         + [pltpu.VMEM(item.shape, item.dtype) for item in items]
         + [pltpu.SemaphoreType.DMA((10,))],
     )
-    odd, even = call(
-        hand_on, [packed, packed], odd, even, odd_guess, even_guess, aliases={0: 0, 1: 1}
-    )
-    odd_pack, even_pack = exchange(odd, even)
+    first, rows, odd, even = call(
+        lambda *refs: residual(*refs[:10], cpd, *refs[10:]), [field, rows_out, packed, packed],
+        local, odd_guess, even_guess, arrive, gather, prolong, jscale, notes, odd, even,
+        aliases={8: 2, 9: 3},
+    )
+    even_pack = lax.ppermute(even, AXES, moves[1])
+    odd_pack = lax.ppermute(odd, AXES, moves[0])
     own_pack = odd
-    first, rows, odd, even = call(
-        residual, [field, rows_out, near, near],
-        local, odd_guess, even_guess, arrive, gather, prolong, jscale, notes,
-    )
-    odd_first, even_first = exchange(odd, even)
     first_got = everyone(rows)
-    lead, pull, matrix, odd_weights, even_weights, info = call(
-        lambda *refs: look_ahead(*refs[:8], cpd, *refs[8:]), [field, field, ((3 * SLOT, coff.shape[1]), bf16), near, near, small],
-        first, jscale, prolong, blocks, notes, own_pack, odd_pack, even_pack,
-    )
-    basis, direction, image, rows, odd, even = call(
-        lambda *refs: first_step(*refs[:15], grps, cpd, *refs[15:]),
-        [field, field, field, rows_out, near, near],
-        first_got, odd_first, even_first, odd_weights, even_weights, matrix, info, first, lead, pull,
-        jscale, prolong, notes, arrive, gather,
+    (basis, direction, image, rows, odd, even, matrix, odd_weights, even_weights, odd_first,
+     even_first, info) = call(
+        lambda *refs: first_step(*refs[:11], grps, cpd, *refs[11:]),
+        [field, field, field, ((devices, 2, LANES), f32), near, near,
+         ((3 * SLOT, coff.shape[1]), bf16)] + [near] * 4 + [small],
+        first_got, own_pack, even_pack, odd_pack, first, jscale, prolong, blocks, notes, arrive,
+        gather,
     )
     odd_near, even_near = exchange(odd, even)
     got = everyone(rows)
-    (lead_two,) = call(look_further, [field], image, jscale, blocks, notes)
+    lead_two, lead, pull = call(
+        look_ahead, [field, field, field], image, first, jscale, prolong, blocks, notes
+    )
     basis_two, direction_two, image_two, scalars, rows = call(
         lambda *refs: second_step(*refs[:19], grps, cpd, *refs[19:]),
-        [field, field, field, ((8, LANES), f32), ((devices, 4, LANES), f32)],
+        [field, field, field, ((8, LANES), f32), rows_out],
         got, first_got, odd_near, even_near, odd_first, even_first, odd_weights, even_weights, matrix,
         info, basis, image, lead, lead_two, pull, jscale, prolong, notes, arrive,
     )

time: 47.5 us -> 46.1 us (0.971)
  blocking collectives: 10.2 us -> 22.3 us
  starting transfers between devices: 21.4 us -> 12.4 us
  waiting for transfers between devices: 7.58 us -> 3.61 us
    all_to_all x1 -> x2, blocking collectives: 10.2 us -> 22.3 us  [everyone(): return lax.all_to_all(rows, AXES, 0, 0, tiled=True)]
    all_to_all x2 -> x1, starting transfers between devices: 8.27 us -> 2.57 us  [everyone(): return lax.all_to_all(rows, AXES, 0, 0, tiled=True)]
    ppermute x4 -> x2, starting transfers between devices: 12 us -> 7.07 us  [exchange(): lax.ppermute(even, AXES, moves[1])]
    all_to_all x2 -> x1, waiting for transfers between devices: 4.43 us -> 2.14 us  [everyone(): return lax.all_to_all(rows, AXES, 0, 0, tiled=True)]
    ppermute x0 -> x2, starting transfers between devices: none -> 2.08 us  [the longest x1 2.07 us: on_device(): even_pack = lax.ppermute(even, AXES, moves[1])]
    ppermute x4 -> x2, waiting for transfers between devices: 3.14 us -> 1.45 us  [exchange(): lax.ppermute(even, AXES, moves[1])]
    ppermute x4 -> x2, starting transfers between devices: 1.15 us -> 0.7 us  [exchange(): lax.ppermute(odd, AXES, moves[0])]
    pallas_call x9 -> x7, Pallas kernels: 7.16 us -> 6.75 us  [call(): pl.pallas_call(body, out_shape=[jax.ShapeDtypeStruct(shape, kind) if fina...]
  transfers between devices with their start and end apart: 10 -> 7, of which waited for: 5 -> 3; matrix products, arithmetic and copies ran while one was open for 0% -> 0% of each run, Pallas kernels for 7% -> 5%
where the time goes in v4:
time: 46.1 us; the launch traced here: 45.8 us
  blocking collectives  22.3 us (48%)
  starting transfers between devices  12.4 us (27%)
  Pallas kernels  6.75 us (15%)
  waiting for transfers between devices  3.61 us (8%)
  between operations  0.7 us (2%)
    all_to_all x2, blocking collectives, everyone(): return lax.all_to_all(rows, AXES, 0, 0, tiled=True)  22.3 us
    ppermute x2, starting transfers between devices, exchange(): lax.ppermute(even, AXES, moves[1])  7.07 us
    pallas_call x7, Pallas kernels, call(): pl.pallas_call(body, out_shape=[jax.ShapeDtypeStruct(shape, kind) if fina...  6.75 us
    all_to_all x1, starting transfers between devices, everyone(): return lax.all_to_all(rows, AXES, 0, 0, tiled=True)  2.57 us
    all_to_all x1, waiting for transfers between devices, everyone(): return lax.all_to_all(rows, AXES, 0, 0, tiled=True)  2.14 us
    ppermute x1, starting transfers between devices, on_device(): even_pack = lax.ppermute(even, AXES, moves[1])  2.07 us
    ppermute x2, waiting for transfers between devices, exchange(): lax.ppermute(even, AXES, moves[1])  1.45 us
  transfers between devices with their start and end apart: 7, of which 3 were waited for; matrix products, arithmetic and copies ran while one was open for 0% of the time, Pallas kernels for 5%

profile of v4, /device:TPU:0, one launch (start us, length us, event | category | flops | bytes accessed | tf_op | source)
XLA Modules:
  0.0 45.8 jit_solution(10125822656215707749)
XLA Ops:
  0.6 0.0 copy-start
  0.6 1.0 %shard_map.131 = (f32[64,128]{1,0:T(8,128)S(1)}, f32[64,128]{1,0:T(8,128)S(1)}, s32[8,128]{1,0:T(8,128)S(1)}) custom-call(f32[64,128]{1,0:T(8,128)} %bitcast.33, s32[1,128]{1,0:T(1,128)} %bitcast.44, s32[2,128]{1,0:T(2,128)} %bitcast.42, s32[2,128]{1,0:T(2,128)} %bitcast.43, s32[1,128]{1,0:T(1,128)} %bitcast.45), custom_call_target="tpu_custom_call" | custom-call | tf_op jit(solution)/shard_map/pallas_call | solution.py:32
  1.7 0.5 %collective-permute-start = (f32[64,128]{1,0:T(8,128)S(1)}, f32[64,128]{1,0:T(8,128)S(1)}, u32[]{:S(2)}, u32[]{:S(2)}) collective-permute-start(f32[64,128]{1,0:T(8,128)S(1)} %get-tuple-element.38), channel_id=1, source_target_pairs={{0,1},{1,0},{2,3},{3,2},{4,8},{5,9},{6,10},{7,11},{8,4},{9,5},{10,... | collective-permute-start | bytes 98312 | tf_op jit(solution)/shard_map/ppermute | solution.py:416
  2.2 4.0 %collective-permute-start.1 = (f32[64,128]{1,0:T(8,128)S(1)}, f32[64,128]{1,0:T(8,128)S(1)}, u32[]{:S(2)}, u32[]{:S(2)}) collective-permute-start(f32[64,128]{1,0:T(8,128)S(1)} %get-tuple-element.39), channel_id=1, source_target_pairs={{0,4},{1,5},{2,6},{3,7},{4,0},{5,1},{6,2},{7,3},{8,12},{9,13},{10,... | collective-permute-start | bytes 98312 | tf_op jit(solution)/shard_map/ppermute | solution.py:416
  6.2 0.0 copy-start.1
  6.2 0.0 copy-start.2
  6.2 1.5 %shard_map.132 = (f32[64,128]{1,0:T(8,128)S(1)}, bf16[256,128]{1,0:T(8,128)(2,1)S(1)}, bf16[128,128]{1,0:T(8,128)(2,1)S(1)}, bf16[848,128]{1,0:T(8,128)(2,1)S(1)}, bf16[848,128]{1,0:T(8,128)(2,1)S(1)}) custom-call(s32[1,2]{1,0:T(1,128)} %bitcast.46, f32[64,128]{1,0:T(8,128)} %bitcast.34, f32[64,128]{1,0:T(8,128)} %bitcast.41, bf16[64,64,128]{2,1,0:T(8,128)(2,1)} %bitcast.21, ...), custom_call_target="tpu_custom_call" | custom-call | tf_op jit(solution)/shard_map/pallas_call | solution.py:32
  7.7 0.0 collective-permute-done.refs_1_
  7.7 0.4 collective-permute-done.1.refs_2_
  8.1 0.0 copy-done.1
  8.1 0.0 copy-done.2
  8.1 0.3 shard_map.133
  8.4 2.1 %collective-permute-start.2 = (bf16[848,128]{1,0:T(8,128)(2,1)S(1)}, bf16[848,128]{1,0:T(8,128)(2,1)S(1)}, u32[]{:S(2)}, u32[]{:S(2)}) collective-permute-start(bf16[848,128]{1,0:T(8,128)(2,1)S(1)} %get-tuple-element.46), channel_id=1, source_target_pairs={{0,4},{1,5},{2,6},{3,7},{4,0},{5,1},{6,2},{7,3},{8,12},{9,13},{10,... | collective-permute-start | bytes 651272 | tf_op jit(solution)/shard_map/ppermute | solution.py:447
  10.5 0.0 collective-permute-start.3
  10.5 12.3 %all_to_all.27 = f32[32,1,128]{2,1,0:T(1,128)S(1)} all-to-all(f32[32,1,128]{2,1,0:T(1,128)S(1)} %bitcast.40), channel_id=1, replica_groups=mesh['sub'=8,'grp'=4] {'sub','grp'}, dimensions={0} | all-to-all | bytes 32768 | tf_op jit(solution)/shard_map/all_to_all | solution.py:419
  22.8 0.0 collective-permute-done.2.refs_2_
  22.8 0.0 collective-permute-done.3.refs_3_
  22.8 0.0 copy-done
  22.8 1.7 %shard_map.134 = (f32[64,128]{1,0:T(8,128)S(1)}, f32[64,128]{1,0:T(8,128)S(1)}, f32[64,128]{1,0:T(8,128)S(1)}, f32[32,2,128]{2,1,0:T(2,128)}, f32[64,128]{1,0:T(...) custom-call(f32[32,128]{1,0:T(8,128)S(1)} %bitcast.36, ...), custom_call_target="tpu_custom_call" | custom-call | tf_op jit(solution)/shard_map/pallas_call | solution.py:32
  24.5 2.6 %all-to-all-start.1 = ((f32[32,2,128]{2,1,0:T(2,128)}), f32[32,2,128]{2,1,0:T(2,128)S(1)}, u32[]{:S(2)}, u32[]{:S(2)}) async-start(f32[32,2,128]{2,1,0:T(2,128)} %get-tuple-element.48), calls=%async_computation.1 | async-start | bytes 65536 | tf_op jit(solution)/shard_map/all_to_all | solution.py:419
  27.0 0.2 collective-permute-start.4
  27.2 3.0 %collective-permute-start.5 = (f32[64,128]{1,0:T(8,128)S(1)}, f32[64,128]{1,0:T(8,128)S(1)}, u32[]{:S(2)}, u32[]{:S(2)}) collective-permute-start(f32[64,128]{1,0:T(8,128)S(1)} %get-tuple-element.50), channel_id=1, source_target_pairs={{0,4},{1,5},{2,6},{3,7},{4,0},{5,1},{6,2},{7,3},{8,12},{9,13},{10,... | collective-permute-start | bytes 98312 | tf_op jit(solution)/shard_map/ppermute | solution.py:416
  30.2 0.8 %shard_map.135 = (f32[64,128]{1,0:T(8,128)S(1)}, f32[64,128]{1,0:T(8,128)S(1)}, f32[64,128]{1,0:T(8,128)S(1)}) custom-call(f32[64,128]{1,0:T(8,128)S(1)} %get-tuple-element.58.image_ref.refs_11_, f32[64,128]{1,0:T(8,128)S(1)} %get-tuple-element.47.refs_4_.first_ref, f32[64,128]{1,0:T(8,128)S(1)} %bitcast.31, f32[64,128]{1,0:T(8,128)S(1)} %bitcast.27, ...), custom_call_target="tpu_custom_call" | custom-call | tf_op jit(solution)/shard_map/pallas_call | solution.py:32
  31.0 0.0 collective-permute-done.4.refs_2_
  31.1 1.1 %collective-permute-done.5.refs_3_ = f32[64,128]{1,0:T(8,128)S(1)} collective-permute-done((f32[64,128]{1,0:T(8,128)S(1)}, f32[64,128]{1,0:T(8,128)S(1)}, u32[]{:S(2)}, u32[]{:S(2)}) %collective-permute-start.5) | collective-permute-done | bytes 32800 | tf_op jit(solution)/shard_map/ppermute | solution.py:416
  32.1 2.1 %all-to-all-done.1.refs_0_ = f32[32,2,128]{2,1,0:T(2,128)S(1)} async-done(((f32[32,2,128]{2,1,0:T(2,128)}), f32[32,2,128]{2,1,0:T(2,128)S(1)}, u32[]{:S(2)}, u32[]{:S(2)}) %all-to-all-start.1) | async-done | bytes 32800 | tf_op jit(solution)/shard_map/all_to_all | solution.py:419
  34.3 0.8 %shard_map.136 = (f32[64,128]{1,0:T(8,128)S(1)}, f32[64,128]{1,0:T(8,128)S(1)}, f32[64,128]{1,0:T(8,128)S(1)}, f32[8,128]{1,0:T(8,128)S(1)}, f32[32,128]{1,0:T(8,128)S(1)}) custom-call(f32[32,2,128]{2,1,0:T(2,128)S(1)} %all-to-all-done.1.refs_0_, f32[32,128]{1,0:T(8,128)S(1)} %bitcast.37, f32[64,128]{1,0:T(8,128)S(1)} %collective-permute-done.4.refs_2_, ...), custom_call_target="tpu_custom_call" | custom-call | tf_op jit(solution)/shard_map/pallas_call | solution.py:32
  35.0 0.0 copy-start.3
  35.0 10.1 %all_to_all.28 = f32[32,1,128]{2,1,0:T(1,128)S(1)} all-to-all(f32[32,1,128]{2,1,0:T(1,128)S(1)} %bitcast.39), channel_id=1, replica_groups=mesh['sub'=8,'grp'=4] {'sub','grp'}, dimensions={0} | all-to-all | bytes 32768 | tf_op jit(solution)/shard_map/all_to_all | solution.py:419
  45.1 0.0 copy-done.3
  45.1 0.7 %shard_map.137 = (f32[64,128]{1,0:T(8,128)}, f32[64,128]{1,0:T(8,128)}) custom-call(f32[32,128]{1,0:T(8,128)S(1)} %bitcast.38, f32[8,128]{1,0:T(8,128)S(1)} %get-tuple-element.63.scalars_ref, f32[64,128]{1,0:T(8,128)S(1)} %bitcast.35, f32[64,128]{1,0:T(8,128)S(1)} %get-tuple-element.57.refs_10_.basis_ref, f32[64,128]{1,0:T(8,128)S(1)} %get-tuple-element.64.basis_two_ref, ...), custom_call_target="tpu_custom_call" | custom-call | tf_op jit(solution)/shard_map/pallas_call | solution.py:32
Async XLA Ops:
  0.6 22.2 %copy-start = (bf16[1,1,64,64,128]{4,3,2,1,0:T(8,128)(2,1)S(1)}, bf16[1,1,64,64,128]{4,3,2,1,0:T(8,128)(2,1)}, u32[]{:S(2)}) copy-start(bf16[1,1,64,64,128]{4,3,2,1,0:T(8,128)(2,1)} %param.14) | copy-start | bytes 3145732
  1.7 6.1 %collective-permute-start = (f32[64,128]{1,0:T(8,128)S(1)}, f32[64,128]{1,0:T(8,128)S(1)}, u32[]{:S(2)}, u32[]{:S(2)}) collective-permute-start(f32[64,128]{1,0:T(8,128)S(1)} %get-tuple-element.38), channel_id=1, source_target_pairs={{0,1},{1,0},{2,3},{3,2},{4,8},{5,9},{6,10},{7,11},{8,4},{9,5},{10,... | collective-permute-start | bytes 98312 | tf_op jit(solution)/shard_map/ppermute | solution.py:416
  2.2 5.9 %collective-permute-start.1 = (f32[64,128]{1,0:T(8,128)S(1)}, f32[64,128]{1,0:T(8,128)S(1)}, u32[]{:S(2)}, u32[]{:S(2)}) collective-permute-start(f32[64,128]{1,0:T(8,128)S(1)} %get-tuple-element.39), channel_id=1, source_target_pairs={{0,4},{1,5},{2,6},{3,7},{4,0},{5,1},{6,2},{7,3},{8,12},{9,13},{10,... | collective-permute-start | bytes 98312 | tf_op jit(solution)/shard_map/ppermute | solution.py:416
  6.2 1.9 %copy-start.1 = (f32[1,1,64,128]{3,2,1,0:T(8,128)S(1)}, f32[1,1,64,128]{3,2,1,0:T(8,128)}, u32[]{:S(2)}) copy-start(f32[1,1,64,128]{3,2,1,0:T(8,128)} %param.17) | copy-start | bytes 98308
  6.2 1.9 %copy-start.2 = (f32[1,1,64,128]{3,2,1,0:T(8,128)S(1)}, f32[1,1,64,128]{3,2,1,0:T(8,128)}, u32[]{:S(2)}) copy-start(f32[1,1,64,128]{3,2,1,0:T(8,128)} %param.16) | copy-start | bytes 98308
  8.4 14.4 %collective-permute-start.2 = (bf16[848,128]{1,0:T(8,128)(2,1)S(1)}, bf16[848,128]{1,0:T(8,128)(2,1)S(1)}, u32[]{:S(2)}, u32[]{:S(2)}) collective-permute-start(bf16[848,128]{1,0:T(8,128)(2,1)S(1)} %get-tuple-element.46), channel_id=1, source_target_pairs={{0,4},{1,5},{2,6},{3,7},{4,0},{5,1},{6,2},{7,3},{8,12},{9,13},{10,... | collective-permute-start | bytes 651272 | tf_op jit(solution)/shard_map/ppermute | solution.py:447
  10.5 12.3 %collective-permute-start.3 = (bf16[848,128]{1,0:T(8,128)(2,1)S(1)}, bf16[848,128]{1,0:T(8,128)(2,1)S(1)}, u32[]{:S(2)}, u32[]{:S(2)}) collective-permute-start(bf16[848,128]{1,0:T(8,128)(2,1)S(1)} %get-tuple-element.45.refs_1_), channel_id=1, source_target_pairs={{0,1},{1,0},{2,3},{3,2},{4,8},{5,9},{6,10},{7,11},{8,4},{9,5},{10,... | collective-permute-start | bytes 651272 | tf_op jit(solution)/shard_map/ppermute | solution.py:448
  24.5 9.8 %all-to-all-start.1 = ((f32[32,2,128]{2,1,0:T(2,128)}), f32[32,2,128]{2,1,0:T(2,128)S(1)}, u32[]{:S(2)}, u32[]{:S(2)}) async-start(f32[32,2,128]{2,1,0:T(2,128)} %get-tuple-element.48), calls=%async_computation.1 | async-start | bytes 65536 | tf_op jit(solution)/shard_map/all_to_all | solution.py:419
  27.0 4.0 %collective-permute-start.4 = (f32[64,128]{1,0:T(8,128)S(1)}, f32[64,128]{1,0:T(8,128)S(1)}, u32[]{:S(2)}, u32[]{:S(2)}) collective-permute-start(f32[64,128]{1,0:T(8,128)S(1)} %get-tuple-element.49), channel_id=1, source_target_pairs={{0,1},{1,0},{2,3},{3,2},{4,8},{5,9},{6,10},{7,11},{8,4},{9,5},{10,... | collective-permute-start | bytes 98312 | tf_op jit(solution)/shard_map/ppermute | solution.py:416
  27.2 4.9 %collective-permute-start.5 = (f32[64,128]{1,0:T(8,128)S(1)}, f32[64,128]{1,0:T(8,128)S(1)}, u32[]{:S(2)}, u32[]{:S(2)}) collective-permute-start(f32[64,128]{1,0:T(8,128)S(1)} %get-tuple-element.50), channel_id=1, source_target_pairs={{0,4},{1,5},{2,6},{3,7},{4,0},{5,1},{6,2},{7,3},{8,12},{9,13},{10,... | collective-permute-start | bytes 98312 | tf_op jit(solution)/shard_map/ppermute | solution.py:416
  35.0 10.1 %copy-start.3 = (f32[1,1,64,128]{3,2,1,0:T(8,128)S(1)}, f32[1,1,64,128]{3,2,1,0:T(8,128)}, u32[]{:S(2)}) copy-start(f32[1,1,64,128]{3,2,1,0:T(8,128)} %param.13) | copy-start | bytes 98308

commit v5 on v4

--- a/solution.py
+++ b/solution.py
@@ -254,6 +254,28 @@
     info_ref[...] = jnp.concatenate(infos + [jnp.zeros((3, LANES), f32)], axis=0)
 
 
+def unpack(own_ref, even_ref, odd_ref, cpd, matrix_ref, odd_weights_ref, even_weights_ref,
+           odd_first_ref, even_first_ref, info_ref):
+    width = matrix_ref.shape[1]
+    size = odd_first_ref.shape[0]
+    base = cpd * (width // LANES)
+    rows = []
+    for slot, ref in enumerate((own_ref, odd_ref, even_ref)):
+        for at in range(0, width, LANES):
+            start = at // LANES * cpd
+            matrix_ref[slot * SLOT : slot * SLOT + cpd, at : at + LANES] = ref[start : start + cpd, :]
+        matrix_ref[slot * SLOT + cpd : (slot + 1) * SLOT, :] = jnp.zeros((SLOT - cpd, width), bf16)
+        rows.append(ref[base + 2 * size : base + 2 * size + 16, :].astype(f32))
+    for ref, weights_ref, near_ref in (
+        (odd_ref, odd_weights_ref, odd_first_ref), (even_ref, even_weights_ref, even_first_ref)
+    ):
+        for start, to_ref in ((base, weights_ref), (base + 2 * size + 16, near_ref)):
+            high, low = ref[start : start + size, :], ref[start + size : start + 2 * size, :]
+            to_ref[...] = high.astype(f32) + low.astype(f32)
+    infos = [row[1:2] + row[2:3] + row[3:4] for row in rows] + [row[0:1] for row in rows[1:]]
+    info_ref[...] = jnp.concatenate(infos + [jnp.zeros((3, LANES), f32)], axis=0)
+
+
 def look_ahead(image_ref, first_ref, jscale_ref, prolong_ref, blocks_ref, notes_ref,
                lead_two_ref, lead_ref, pull_ref):
     valve, jscale = notes_ref[VALVE], jscale_ref[...]
@@ -347,9 +369,9 @@
         ref[...] = pick(scaled, row_of(notes_ref.at[SEND], parity(side)))
 
 
-def second_step(got_ref, first_got_ref, odd_near_ref, even_near_ref, odd_first_ref, even_first_ref,
+def second_step(got_ref, first_got_ref, even_near_ref, odd_near_ref, odd_first_ref, even_first_ref,
                 odd_weights_ref, even_weights_ref, matrix_ref, info_ref, basis_ref, image_ref,
-                lead_ref, lead_two_ref, pull_ref, jscale_ref, prolong_ref, notes_ref, arrive_ref,
+                jscale_ref, prolong_ref, blocks_ref, notes_ref, arrive_ref,
                 grp_size, cpd, basis_two_ref, direction_ref, image_two_ref, scalars_ref, out_ref):
     beta = jnp.sqrt(summed(first_got_ref, cpd, 1)[0])
     along, energy = summed(got_ref, cpd, 2)
@@ -368,14 +390,15 @@
     basis = (image_ref[...] - along * basis_ref[...]) * inverse
     basis_two_ref[...] = basis
     spread = spread_of(solved[0], notes_ref[AGG])
-    direction_ref[...] = jscale_ref[...] * basis + prolong_ref[...] * spread
+    direction = jscale_ref[...] * basis + prolong_ref[...] * spread
+    direction_ref[...] = direction
     near = [
         mixed(odd_near_ref[...], odd_first_ref[...])
         + near_spread(odd_weights_ref, info_ref, 0, solved[1]),
         mixed(even_near_ref[...], even_first_ref[...])
         + near_spread(even_weights_ref, info_ref, 1, solved[2]),
     ]
-    image = mixed(lead_two_ref[...], lead_ref[...]) + pull_ref[...] * spread
+    image = local_product(blocks_ref, notes_ref[VALVE], direction)
     image = image - coupling * received(near, arrive_ref)
     image_two_ref[...] = image
     scalars_ref[...] = jnp.concatenate([beta, along, height, jnp.zeros((5, LANES), f32)], axis=0)
@@ -451,21 +474,18 @@
     (basis, direction, image, rows, odd, even, matrix, odd_weights, even_weights, odd_first,
      even_first, info) = call(
         lambda *refs: first_step(*refs[:11], grps, cpd, *refs[11:]),
-        [field, field, field, ((devices, 2, LANES), f32), near, near,
+        [field, field, field, rows_out, near, near,
          ((3 * SLOT, coff.shape[1]), bf16)] + [near] * 4 + [small],
         first_got, own_pack, even_pack, odd_pack, first, jscale, prolong, blocks, notes, arrive,
         gather,
     )
     odd_near, even_near = exchange(odd, even)
     got = everyone(rows)
-    lead_two, lead, pull = call(
-        look_ahead, [field, field, field], image, first, jscale, prolong, blocks, notes
-    )
     basis_two, direction_two, image_two, scalars, rows = call(
-        lambda *refs: second_step(*refs[:19], grps, cpd, *refs[19:]),
+        lambda *refs: second_step(*refs[:17], grps, cpd, *refs[17:]),
         [field, field, field, ((8, LANES), f32), rows_out],
-        got, first_got, odd_near, even_near, odd_first, even_first, odd_weights, even_weights, matrix,
-        info, basis, image, lead, lead_two, pull, jscale, prolong, notes, arrive,
+        got, first_got, even_near, odd_near, odd_first, even_first, odd_weights, even_weights, matrix,
+        info, basis, image, jscale, prolong, blocks, notes, arrive,
     )
     got = everyone(rows)
     solution, next_basis = call(

time: 46.1 us -> 45.5 us (0.987)
  blocking collectives: 22.3 us -> 31.5 us
  starting transfers between devices: 12.4 us -> 7.25 us
  waiting for transfers between devices: 3.61 us -> 0.39 us
  Pallas kernels: 6.75 us -> 5.4 us
    all_to_all x2 -> x3, blocking collectives: 22.3 us -> 31.5 us  [everyone(): return lax.all_to_all(rows, AXES, 0, 0, tiled=True)]
    all_to_all x1 -> x0, starting transfers between devices: 2.57 us -> none  [everyone(): return lax.all_to_all(rows, AXES, 0, 0, tiled=True)]
    ppermute x2, starting transfers between devices: 7.07 us -> 4.65 us  [exchange(): lax.ppermute(even, AXES, moves[1])]
    all_to_all x1 -> x0, waiting for transfers between devices: 2.14 us -> none  [everyone(): return lax.all_to_all(rows, AXES, 0, 0, tiled=True)]
    pallas_call x7 -> x6, Pallas kernels: 6.75 us -> 5.4 us  [call(): pl.pallas_call(body, out_shape=[jax.ShapeDtypeStruct(shape, kind) if fina...]
    ppermute x2, waiting for transfers between devices: 1.45 us -> 0.38 us  [exchange(): lax.ppermute(even, AXES, moves[1])]
  transfers between devices with their start and end apart: 7 -> 6, of which waited for: 3 -> 1; matrix products, arithmetic and copies ran while one was open for 0% -> 0% of each run, Pallas kernels for 5% -> 3%
where the time goes in v5:
time: 45.5 us; the launch traced here: 45.3 us
  blocking collectives  31.5 us (69%)
  starting transfers between devices  7.25 us (16%)
  Pallas kernels  5.4 us (12%)
  between operations  0.68 us (1%)
    all_to_all x3, blocking collectives, everyone(): return lax.all_to_all(rows, AXES, 0, 0, tiled=True)  31.5 us
    pallas_call x6, Pallas kernels, call(): pl.pallas_call(body, out_shape=[jax.ShapeDtypeStruct(shape, kind) if fina...  5.4 us
    ppermute x2, starting transfers between devices, exchange(): lax.ppermute(even, AXES, moves[1])  4.65 us
    ppermute x1, starting transfers between devices, on_device(): even_pack = lax.ppermute(even, AXES, moves[1])  2.07 us
  transfers between devices with their start and end apart: 6, of which 1 were waited for; matrix products, arithmetic and copies ran while one was open for 0% of the time, Pallas kernels for 3%

profile of v5, /device:TPU:0, one launch (start us, length us, event | category | flops | bytes accessed | tf_op | source)
XLA Modules:
  0.0 45.3 jit_solution(14069347826030720385)
XLA Ops:
  0.6 0.0 copy-start
  0.6 1.0 %shard_map.131 = (f32[64,128]{1,0:T(8,128)S(1)}, f32[64,128]{1,0:T(8,128)S(1)}, s32[8,128]{1,0:T(8,128)S(1)}) custom-call(f32[64,128]{1,0:T(8,128)} %bitcast.35, s32[1,128]{1,0:T(1,128)} %bitcast.48, s32[2,128]{1,0:T(2,128)} %bitcast.46, s32[2,128]{1,0:T(2,128)} %bitcast.47, s32[1,128]{1,0:T(1,128)} %bitcast.49), custom_call_target="tpu_custom_call" | custom-call | tf_op jit(solution)/shard_map/pallas_call | solution.py:32
  1.7 0.5 %collective-permute-start = (f32[64,128]{1,0:T(8,128)S(1)}, f32[64,128]{1,0:T(8,128)S(1)}, u32[]{:S(2)}, u32[]{:S(2)}) collective-permute-start(f32[64,128]{1,0:T(8,128)S(1)} %get-tuple-element.35), channel_id=1, source_target_pairs={{0,1},{1,0},{2,3},{3,2},{4,8},{5,9},{6,10},{7,11},{8,4},{9,5},{10,... | collective-permute-start | bytes 98312 | tf_op jit(solution)/shard_map/ppermute | solution.py:439
  2.2 4.0 %collective-permute-start.1 = (f32[64,128]{1,0:T(8,128)S(1)}, f32[64,128]{1,0:T(8,128)S(1)}, u32[]{:S(2)}, u32[]{:S(2)}) collective-permute-start(f32[64,128]{1,0:T(8,128)S(1)} %get-tuple-element.36), channel_id=1, source_target_pairs={{0,4},{1,5},{2,6},{3,7},{4,0},{5,1},{6,2},{7,3},{8,12},{9,13},{10,... | collective-permute-start | bytes 98312 | tf_op jit(solution)/shard_map/ppermute | solution.py:439
  6.2 0.0 copy-start.1
  6.2 0.0 copy-start.2
  6.2 1.5 %shard_map.132 = (f32[64,128]{1,0:T(8,128)S(1)}, bf16[256,128]{1,0:T(8,128)(2,1)S(1)}, bf16[128,128]{1,0:T(8,128)(2,1)S(1)}, bf16[848,128]{1,0:T(8,128)(2,1)S(1)}, bf16[848,128]{1,0:T(8,128)(2,1)S(1)}) custom-call(s32[1,2]{1,0:T(1,128)} %bitcast.50, f32[64,128]{1,0:T(8,128)} %bitcast.36, f32[64,128]{1,0:T(8,128)} %bitcast.45, bf16[64,64,128]{2,1,0:T(8,128)(2,1)} %bitcast.25, ...), custom_call_target="tpu_custom_call" | custom-call | tf_op jit(solution)/shard_map/pallas_call | solution.py:32
  7.7 0.0 collective-permute-done.refs_1_
  7.7 0.4 collective-permute-done.1.refs_2_
  8.1 0.0 copy-done.1
  8.1 0.0 copy-done.2
  8.1 0.3 shard_map.133
  8.4 2.1 %collective-permute-start.2 = (bf16[848,128]{1,0:T(8,128)(2,1)S(1)}, bf16[848,128]{1,0:T(8,128)(2,1)S(1)}, u32[]{:S(2)}, u32[]{:S(2)}) collective-permute-start(bf16[848,128]{1,0:T(8,128)(2,1)S(1)} %get-tuple-element.43), channel_id=1, source_target_pairs={{0,4},{1,5},{2,6},{3,7},{4,0},{5,1},{6,2},{7,3},{8,12},{9,13},{10,... | collective-permute-start | bytes 651272 | tf_op jit(solution)/shard_map/ppermute | solution.py:470
  10.5 0.0 collective-permute-start.3
  10.5 12.3 %all_to_all.33 = f32[32,1,128]{2,1,0:T(1,128)S(1)} all-to-all(f32[32,1,128]{2,1,0:T(1,128)S(1)} %bitcast.44), channel_id=1, replica_groups=mesh['sub'=8,'grp'=4] {'sub','grp'}, dimensions={0} | all-to-all | bytes 32768 | tf_op jit(solution)/shard_map/all_to_all | solution.py:442
  22.8 0.0 collective-permute-done.2.refs_2_
  22.8 0.0 collective-permute-done.3.refs_3_
  22.8 0.0 copy-done
  22.8 1.0 %shard_map.134 = (f32[64,128]{1,0:T(8,128)S(1)}, f32[64,128]{1,0:T(8,128)S(1)}, f32[64,128]{1,0:T(8,128)S(1)}, f32[32,128]{1,0:T(8,128)S(1)}, f32[64,128]{1,0:T(...) custom-call(f32[32,128]{1,0:T(8,128)S(1)} %bitcast.38, ...), custom_call_target="tpu_custom_call" | custom-call | tf_op jit(solution)/shard_map/pallas_call | solution.py:32
  23.8 0.6 %collective-permute-start.4 = (f32[64,128]{1,0:T(8,128)S(1)}, f32[64,128]{1,0:T(8,128)S(1)}, u32[]{:S(2)}, u32[]{:S(2)}) collective-permute-start(f32[64,128]{1,0:T(8,128)S(1)} %get-tuple-element.46), channel_id=1, source_target_pairs={{0,4},{1,5},{2,6},{3,7},{4,0},{5,1},{6,2},{7,3},{8,12},{9,13},{10,... | collective-permute-start | bytes 98312 | tf_op jit(solution)/shard_map/ppermute | solution.py:439
  24.4 0.0 collective-permute-start.5
  24.4 10.3 %all_to_all.34 = f32[32,1,128]{2,1,0:T(1,128)S(1)} all-to-all(f32[32,1,128]{2,1,0:T(1,128)S(1)} %bitcast.42), channel_id=1, replica_groups=mesh['sub'=8,'grp'=4] {'sub','grp'}, dimensions={0} | all-to-all | bytes 32768 | tf_op jit(solution)/shard_map/all_to_all | solution.py:442
  34.7 0.0 collective-permute-done.4.refs_2_
  34.7 0.0 collective-permute-done.5.refs_3_
  34.7 0.9 %shard_map.135 = (f32[64,128]{1,0:T(8,128)S(1)}, f32[64,128]{1,0:T(8,128)S(1)}, f32[64,128]{1,0:T(8,128)S(1)}, f32[8,128]{1,0:T(8,128)S(1)}, f32[32,128]{1,0:T(8,128)S(1)}) custom-call(f32[32,128]{1,0:T(8,128)S(1)} %bitcast.40, f32[32,128]{1,0:T(8,128)S(1)} %bitcast.39, f32[64,128]{1,0:T(8,128)S(1)} %collective-permute-done.4.refs_2_, ...), custom_call_target="tpu_custom_call" | custom-call | tf_op jit(solution)/shard_map/pallas_call | solution.py:32
  35.6 0.0 copy-start.3
  35.6 9.0 %all_to_all.35 = f32[32,1,128]{2,1,0:T(1,128)S(1)} all-to-all(f32[32,1,128]{2,1,0:T(1,128)S(1)} %bitcast.43), channel_id=1, replica_groups=mesh['sub'=8,'grp'=4] {'sub','grp'}, dimensions={0} | all-to-all | bytes 32768 | tf_op jit(solution)/shard_map/all_to_all | solution.py:442
  44.5 0.0 copy-done.3
  44.5 0.7 %shard_map.136 = (f32[64,128]{1,0:T(8,128)}, f32[64,128]{1,0:T(8,128)}) custom-call(f32[32,128]{1,0:T(8,128)S(1)} %bitcast.41, f32[8,128]{1,0:T(8,128)S(1)} %get-tuple-element.57.scalars_ref, f32[64,128]{1,0:T(8,128)S(1)} %bitcast.37, f32[64,128]{1,0:T(8,128)S(1)} %get-tuple-element.54.refs_10_.basis_ref, f32[64,128]{1,0:T(8,128)S(1)} %get-tuple-element.58.basis_two_ref, ...), custom_call_target="tpu_custom_call" | custom-call | tf_op jit(solution)/shard_map/pallas_call | solution.py:32
Async XLA Ops:
  0.6 22.2 %copy-start = (bf16[1,1,64,64,128]{4,3,2,1,0:T(8,128)(2,1)S(1)}, bf16[1,1,64,64,128]{4,3,2,1,0:T(8,128)(2,1)}, u32[]{:S(2)}) copy-start(bf16[1,1,64,64,128]{4,3,2,1,0:T(8,128)(2,1)} %param.14) | copy-start | bytes 3145732
  1.7 6.1 %collective-permute-start = (f32[64,128]{1,0:T(8,128)S(1)}, f32[64,128]{1,0:T(8,128)S(1)}, u32[]{:S(2)}, u32[]{:S(2)}) collective-permute-start(f32[64,128]{1,0:T(8,128)S(1)} %get-tuple-element.35), channel_id=1, source_target_pairs={{0,1},{1,0},{2,3},{3,2},{4,8},{5,9},{6,10},{7,11},{8,4},{9,5},{10,... | collective-permute-start | bytes 98312 | tf_op jit(solution)/shard_map/ppermute | solution.py:439
  2.2 5.9 %collective-permute-start.1 = (f32[64,128]{1,0:T(8,128)S(1)}, f32[64,128]{1,0:T(8,128)S(1)}, u32[]{:S(2)}, u32[]{:S(2)}) collective-permute-start(f32[64,128]{1,0:T(8,128)S(1)} %get-tuple-element.36), channel_id=1, source_target_pairs={{0,4},{1,5},{2,6},{3,7},{4,0},{5,1},{6,2},{7,3},{8,12},{9,13},{10,... | collective-permute-start | bytes 98312 | tf_op jit(solution)/shard_map/ppermute | solution.py:439
  6.2 1.9 %copy-start.1 = (f32[1,1,64,128]{3,2,1,0:T(8,128)S(1)}, f32[1,1,64,128]{3,2,1,0:T(8,128)}, u32[]{:S(2)}) copy-start(f32[1,1,64,128]{3,2,1,0:T(8,128)} %param.17) | copy-start | bytes 98308
  6.2 1.9 %copy-start.2 = (f32[1,1,64,128]{3,2,1,0:T(8,128)S(1)}, f32[1,1,64,128]{3,2,1,0:T(8,128)}, u32[]{:S(2)}) copy-start(f32[1,1,64,128]{3,2,1,0:T(8,128)} %param.16) | copy-start | bytes 98308
  8.4 14.4 %collective-permute-start.2 = (bf16[848,128]{1,0:T(8,128)(2,1)S(1)}, bf16[848,128]{1,0:T(8,128)(2,1)S(1)}, u32[]{:S(2)}, u32[]{:S(2)}) collective-permute-start(bf16[848,128]{1,0:T(8,128)(2,1)S(1)} %get-tuple-element.43), channel_id=1, source_target_pairs={{0,4},{1,5},{2,6},{3,7},{4,0},{5,1},{6,2},{7,3},{8,12},{9,13},{10,... | collective-permute-start | bytes 651272 | tf_op jit(solution)/shard_map/ppermute | solution.py:470
  10.5 12.3 %collective-permute-start.3 = (bf16[848,128]{1,0:T(8,128)(2,1)S(1)}, bf16[848,128]{1,0:T(8,128)(2,1)S(1)}, u32[]{:S(2)}, u32[]{:S(2)}) collective-permute-start(bf16[848,128]{1,0:T(8,128)(2,1)S(1)} %get-tuple-element.42.refs_1_), channel_id=1, source_target_pairs={{0,1},{1,0},{2,3},{3,2},{4,8},{5,9},{6,10},{7,11},{8,4},{9,5},{10,... | collective-permute-start | bytes 651272 | tf_op jit(solution)/shard_map/ppermute | solution.py:471
  23.8 10.9 %collective-permute-start.4 = (f32[64,128]{1,0:T(8,128)S(1)}, f32[64,128]{1,0:T(8,128)S(1)}, u32[]{:S(2)}, u32[]{:S(2)}) collective-permute-start(f32[64,128]{1,0:T(8,128)S(1)} %get-tuple-element.46), channel_id=1, source_target_pairs={{0,4},{1,5},{2,6},{3,7},{4,0},{5,1},{6,2},{7,3},{8,12},{9,13},{10,... | collective-permute-start | bytes 98312 | tf_op jit(solution)/shard_map/ppermute | solution.py:439
  24.4 10.3 %collective-permute-start.5 = (f32[64,128]{1,0:T(8,128)S(1)}, f32[64,128]{1,0:T(8,128)S(1)}, u32[]{:S(2)}, u32[]{:S(2)}) collective-permute-start(f32[64,128]{1,0:T(8,128)S(1)} %get-tuple-element.47), channel_id=1, source_target_pairs={{0,1},{1,0},{2,3},{3,2},{4,8},{5,9},{6,10},{7,11},{8,4},{9,5},{10,... | collective-permute-start | bytes 98312 | tf_op jit(solution)/shard_map/ppermute | solution.py:439
  35.6 9.0 %copy-start.3 = (f32[1,1,64,128]{3,2,1,0:T(8,128)S(1)}, f32[1,1,64,128]{3,2,1,0:T(8,128)}, u32[]{:S(2)}) copy-start(f32[1,1,64,128]{3,2,1,0:T(8,128)} %param.13) | copy-start | bytes 98308

commit v6 on v5

--- a/solution.py
+++ b/solution.py
@@ -68,13 +68,20 @@
     return (lax.axis_index("sub") + side + 1) % 2
 
 
+def along_lanes(field, places, axis):
+    return jnp.take_along_axis(field, places, axis=axis, mode="promise_in_bounds")
+
+
 def pick(field, places):
-    return jnp.take_along_axis(field, jnp.broadcast_to(places, field.shape), axis=1)
-
-
-def pieces(field):
-    high = field.astype(bf16)
-    return high, (field - high.astype(f32)).astype(bf16)
+    return along_lanes(field, jnp.broadcast_to(places, field.shape), axis=1)
+
+
+def pieces(field, count=2):
+    result = []
+    for _ in range(count):
+        result.append(field.astype(bf16))
+        field = field - result[-1].astype(f32)
+    return result
 
 
 def block_rows(blocks, field):
@@ -86,13 +93,14 @@
     return jnp.concatenate(rows, axis=0) + penalty_gain * valve.astype(f32) * field
 
 
-def received(near, arrive_ref):
-    high, low = pieces(jnp.concatenate(near, axis=1))
-    both = jnp.dot(
-        jnp.concatenate([high, low], axis=0), arrive_ref[...], preferred_element_type=f32
-    )
-    count = near[0].shape[0]
-    return both[:count] + both[count:]
+def received(near, arrive_ref, count=2):
+    parts = pieces(jnp.concatenate(near, axis=1), count)
+    sums = jnp.dot(jnp.concatenate(parts, axis=0), arrive_ref[...], preferred_element_type=f32)
+    size = near[0].shape[0]
+    result = sums[:size]
+    for at in range(size, count * size, size):
+        result = result + sums[at : at + size]
+    return result
 
 
 def restricted(weighted, gather_ref):
@@ -124,7 +132,7 @@
 def summed(ref, first_lane, count):
     rows = jnp.broadcast_to(jnp.sum(flat(ref), axis=0, keepdims=True), (8, LANES))
     return [
-        jnp.take_along_axis(rows, jnp.full((8, LANES), first_lane + at, jnp.int32), axis=1)[0:1]
+        along_lanes(rows, jnp.full((8, LANES), first_lane + at, jnp.int32), axis=1)[0:1]
         for at in range(count)
     ]
 
@@ -219,7 +227,7 @@
              jscale_ref, notes_ref, odd_pack_ref, even_pack_ref, cpd, first_ref, out_ref, odd_ref,
              even_ref):
     near = [odd_near_ref[...], even_near_ref[...]]
-    first = local_ref[...] + coupling * received(near, arrive_ref)
+    first = local_ref[...] + coupling * received(near, arrive_ref, 3)
     first_ref[...] = first
     weighted = jnp.sum(prolong_ref[...] * first, axis=0, keepdims=True)
     to_all(out_ref, restricted(weighted, gather_ref), cpd, [total(first * first)])
@@ -293,7 +301,7 @@
     source = lax.rem(lane - cpd * row + cpd * group, LANES)
     tiles = []
     for part in parts:
-        shifted = jnp.take_along_axis(part, source, axis=1)
+        shifted = along_lanes(part, source, axis=1)
         tiles.extend(jnp.where(mask, shifted, 0.0) for mask in masks)
     product = lax.dot_general(
         jnp.concatenate(tiles, axis=1).astype(bf16), matrix_ref[...], (((1,), (1,)), ((), ())),
@@ -330,7 +338,7 @@
 
 def spread_of(solution, agg):
     wide = jnp.broadcast_to(solution, (8, LANES))
-    return jnp.take_along_axis(wide, jnp.broadcast_to(agg, (8, LANES)), axis=1)[0:1]
+    return along_lanes(wide, jnp.broadcast_to(agg, (8, LANES)), axis=1)[0:1]
 
 
 def near_spread(weights_ref, info_ref, side, solution):

time: 45.5 us -> 45.6 us (level)
  no operation moved by 1% of the time
where the time goes in v6:
time: 45.6 us; the launch traced here: 45.3 us
  blocking collectives  31.5 us (69%)
  starting transfers between devices  7.25 us (16%)
  Pallas kernels  5.4 us (12%)
  between operations  0.68 us (1%)
    all_to_all x3, blocking collectives, everyone(): return lax.all_to_all(rows, AXES, 0, 0, tiled=True)  31.5 us
    pallas_call x6, Pallas kernels, call(): pl.pallas_call(body, out_shape=[jax.ShapeDtypeStruct(shape, kind) if fina...  5.4 us
    ppermute x2, starting transfers between devices, exchange(): lax.ppermute(even, AXES, moves[1])  4.65 us
    ppermute x1, starting transfers between devices, on_device(): even_pack = lax.ppermute(even, AXES, moves[1])  2.08 us
  transfers between devices with their start and end apart: 6, of which 1 were waited for; matrix products, arithmetic and copies ran while one was open for 0% of the time, Pallas kernels for 3%

profile of v6, /device:TPU:0, one launch (start us, length us, event | category | flops | bytes accessed | tf_op | source)
XLA Modules:
  0.0 45.3 jit_solution(2596537903817153757)
XLA Ops:
  0.6 0.0 copy-start
  0.6 1.0 %shard_map.131 = (f32[64,128]{1,0:T(8,128)S(1)}, f32[64,128]{1,0:T(8,128)S(1)}, s32[8,128]{1,0:T(8,128)S(1)}) custom-call(f32[64,128]{1,0:T(8,128)} %bitcast.35, s32[1,128]{1,0:T(1,128)} %bitcast.48, s32[2,128]{1,0:T(2,128)} %bitcast.46, s32[2,128]{1,0:T(2,128)} %bitcast.47, s32[1,128]{1,0:T(1,128)} %bitcast.49), custom_call_target="tpu_custom_call" | custom-call | tf_op jit(solution)/shard_map/pallas_call | solution.py:32
  1.7 0.5 %collective-permute-start = (f32[64,128]{1,0:T(8,128)S(1)}, f32[64,128]{1,0:T(8,128)S(1)}, u32[]{:S(2)}, u32[]{:S(2)}) collective-permute-start(f32[64,128]{1,0:T(8,128)S(1)} %get-tuple-element.35), channel_id=1, source_target_pairs={{0,1},{1,0},{2,3},{3,2},{4,8},{5,9},{6,10},{7,11},{8,4},{9,5},{10,... | collective-permute-start | bytes 98312 | tf_op jit(solution)/shard_map/ppermute | solution.py:447
  2.2 4.0 %collective-permute-start.1 = (f32[64,128]{1,0:T(8,128)S(1)}, f32[64,128]{1,0:T(8,128)S(1)}, u32[]{:S(2)}, u32[]{:S(2)}) collective-permute-start(f32[64,128]{1,0:T(8,128)S(1)} %get-tuple-element.36), channel_id=1, source_target_pairs={{0,4},{1,5},{2,6},{3,7},{4,0},{5,1},{6,2},{7,3},{8,12},{9,13},{10,... | collective-permute-start | bytes 98312 | tf_op jit(solution)/shard_map/ppermute | solution.py:447
  6.2 0.0 copy-start.1
  6.2 0.0 copy-start.2
  6.2 1.5 %shard_map.132 = (f32[64,128]{1,0:T(8,128)S(1)}, bf16[256,128]{1,0:T(8,128)(2,1)S(1)}, bf16[128,128]{1,0:T(8,128)(2,1)S(1)}, bf16[848,128]{1,0:T(8,128)(2,1)S(1)}, bf16[848,128]{1,0:T(8,128)(2,1)S(1)}) custom-call(s32[1,2]{1,0:T(1,128)} %bitcast.50, f32[64,128]{1,0:T(8,128)} %bitcast.36, f32[64,128]{1,0:T(8,128)} %bitcast.45, bf16[64,64,128]{2,1,0:T(8,128)(2,1)} %bitcast.25, ...), custom_call_target="tpu_custom_call" | custom-call | tf_op jit(solution)/shard_map/pallas_call | solution.py:32
  7.7 0.0 collective-permute-done.refs_1_
  7.7 0.4 collective-permute-done.1.refs_2_
  8.1 0.0 copy-done.1
  8.1 0.0 copy-done.2
  8.1 0.3 shard_map.133
  8.4 2.1 %collective-permute-start.2 = (bf16[848,128]{1,0:T(8,128)(2,1)S(1)}, bf16[848,128]{1,0:T(8,128)(2,1)S(1)}, u32[]{:S(2)}, u32[]{:S(2)}) collective-permute-start(bf16[848,128]{1,0:T(8,128)(2,1)S(1)} %get-tuple-element.43), channel_id=1, source_target_pairs={{0,4},{1,5},{2,6},{3,7},{4,0},{5,1},{6,2},{7,3},{8,12},{9,13},{10,... | collective-permute-start | bytes 651272 | tf_op jit(solution)/shard_map/ppermute | solution.py:478
  10.5 0.0 collective-permute-start.3
  10.5 12.3 %all_to_all.33 = f32[32,1,128]{2,1,0:T(1,128)S(1)} all-to-all(f32[32,1,128]{2,1,0:T(1,128)S(1)} %bitcast.44), channel_id=1, replica_groups=mesh['sub'=8,'grp'=4] {'sub','grp'}, dimensions={0} | all-to-all | bytes 32768 | tf_op jit(solution)/shard_map/all_to_all | solution.py:450
  22.8 0.0 collective-permute-done.2.refs_2_
  22.8 0.0 collective-permute-done.3.refs_3_
  22.8 0.0 copy-done
  22.8 1.0 %shard_map.134 = (f32[64,128]{1,0:T(8,128)S(1)}, f32[64,128]{1,0:T(8,128)S(1)}, f32[64,128]{1,0:T(8,128)S(1)}, f32[32,128]{1,0:T(8,128)S(1)}, f32[64,128]{1,0:T(...) custom-call(f32[32,128]{1,0:T(8,128)S(1)} %bitcast.38, ...), custom_call_target="tpu_custom_call" | custom-call | tf_op jit(solution)/shard_map/pallas_call | solution.py:32
  23.8 0.6 %collective-permute-start.4 = (f32[64,128]{1,0:T(8,128)S(1)}, f32[64,128]{1,0:T(8,128)S(1)}, u32[]{:S(2)}, u32[]{:S(2)}) collective-permute-start(f32[64,128]{1,0:T(8,128)S(1)} %get-tuple-element.46), channel_id=1, source_target_pairs={{0,4},{1,5},{2,6},{3,7},{4,0},{5,1},{6,2},{7,3},{8,12},{9,13},{10,... | collective-permute-start | bytes 98312 | tf_op jit(solution)/shard_map/ppermute | solution.py:447
  24.4 0.0 collective-permute-start.5
  24.4 10.3 %all_to_all.34 = f32[32,1,128]{2,1,0:T(1,128)S(1)} all-to-all(f32[32,1,128]{2,1,0:T(1,128)S(1)} %bitcast.42), channel_id=1, replica_groups=mesh['sub'=8,'grp'=4] {'sub','grp'}, dimensions={0} | all-to-all | bytes 32768 | tf_op jit(solution)/shard_map/all_to_all | solution.py:450
  34.7 0.0 collective-permute-done.4.refs_2_
  34.7 0.0 collective-permute-done.5.refs_3_
  34.7 0.9 %shard_map.135 = (f32[64,128]{1,0:T(8,128)S(1)}, f32[64,128]{1,0:T(8,128)S(1)}, f32[64,128]{1,0:T(8,128)S(1)}, f32[8,128]{1,0:T(8,128)S(1)}, f32[32,128]{1,0:T(8,128)S(1)}) custom-call(f32[32,128]{1,0:T(8,128)S(1)} %bitcast.40, f32[32,128]{1,0:T(8,128)S(1)} %bitcast.39, f32[64,128]{1,0:T(8,128)S(1)} %collective-permute-done.4.refs_2_, ...), custom_call_target="tpu_custom_call" | custom-call | tf_op jit(solution)/shard_map/pallas_call | solution.py:32
  35.6 0.0 copy-start.3
  35.6 9.0 %all_to_all.35 = f32[32,1,128]{2,1,0:T(1,128)S(1)} all-to-all(f32[32,1,128]{2,1,0:T(1,128)S(1)} %bitcast.43), channel_id=1, replica_groups=mesh['sub'=8,'grp'=4] {'sub','grp'}, dimensions={0} | all-to-all | bytes 32768 | tf_op jit(solution)/shard_map/all_to_all | solution.py:450
  44.5 0.0 copy-done.3
  44.5 0.7 %shard_map.136 = (f32[64,128]{1,0:T(8,128)}, f32[64,128]{1,0:T(8,128)}) custom-call(f32[32,128]{1,0:T(8,128)S(1)} %bitcast.41, f32[8,128]{1,0:T(8,128)S(1)} %get-tuple-element.57.scalars_ref, f32[64,128]{1,0:T(8,128)S(1)} %bitcast.37, f32[64,128]{1,0:T(8,128)S(1)} %get-tuple-element.54.refs_10_.basis_ref, f32[64,128]{1,0:T(8,128)S(1)} %get-tuple-element.58.basis_two_ref, ...), custom_call_target="tpu_custom_call" | custom-call | tf_op jit(solution)/shard_map/pallas_call | solution.py:32
Async XLA Ops:
  0.6 22.2 %copy-start = (bf16[1,1,64,64,128]{4,3,2,1,0:T(8,128)(2,1)S(1)}, bf16[1,1,64,64,128]{4,3,2,1,0:T(8,128)(2,1)}, u32[]{:S(2)}) copy-start(bf16[1,1,64,64,128]{4,3,2,1,0:T(8,128)(2,1)} %param.14) | copy-start | bytes 3145732
  1.7 6.1 %collective-permute-start = (f32[64,128]{1,0:T(8,128)S(1)}, f32[64,128]{1,0:T(8,128)S(1)}, u32[]{:S(2)}, u32[]{:S(2)}) collective-permute-start(f32[64,128]{1,0:T(8,128)S(1)} %get-tuple-element.35), channel_id=1, source_target_pairs={{0,1},{1,0},{2,3},{3,2},{4,8},{5,9},{6,10},{7,11},{8,4},{9,5},{10,... | collective-permute-start | bytes 98312 | tf_op jit(solution)/shard_map/ppermute | solution.py:447
  2.2 5.9 %collective-permute-start.1 = (f32[64,128]{1,0:T(8,128)S(1)}, f32[64,128]{1,0:T(8,128)S(1)}, u32[]{:S(2)}, u32[]{:S(2)}) collective-permute-start(f32[64,128]{1,0:T(8,128)S(1)} %get-tuple-element.36), channel_id=1, source_target_pairs={{0,4},{1,5},{2,6},{3,7},{4,0},{5,1},{6,2},{7,3},{8,12},{9,13},{10,... | collective-permute-start | bytes 98312 | tf_op jit(solution)/shard_map/ppermute | solution.py:447
  6.2 1.9 %copy-start.1 = (f32[1,1,64,128]{3,2,1,0:T(8,128)S(1)}, f32[1,1,64,128]{3,2,1,0:T(8,128)}, u32[]{:S(2)}) copy-start(f32[1,1,64,128]{3,2,1,0:T(8,128)} %param.17) | copy-start | bytes 98308
  6.2 1.9 %copy-start.2 = (f32[1,1,64,128]{3,2,1,0:T(8,128)S(1)}, f32[1,1,64,128]{3,2,1,0:T(8,128)}, u32[]{:S(2)}) copy-start(f32[1,1,64,128]{3,2,1,0:T(8,128)} %param.16) | copy-start | bytes 98308
  8.4 14.4 %collective-permute-start.2 = (bf16[848,128]{1,0:T(8,128)(2,1)S(1)}, bf16[848,128]{1,0:T(8,128)(2,1)S(1)}, u32[]{:S(2)}, u32[]{:S(2)}) collective-permute-start(bf16[848,128]{1,0:T(8,128)(2,1)S(1)} %get-tuple-element.43), channel_id=1, source_target_pairs={{0,4},{1,5},{2,6},{3,7},{4,0},{5,1},{6,2},{7,3},{8,12},{9,13},{10,... | collective-permute-start | bytes 651272 | tf_op jit(solution)/shard_map/ppermute | solution.py:478
  10.5 12.3 %collective-permute-start.3 = (bf16[848,128]{1,0:T(8,128)(2,1)S(1)}, bf16[848,128]{1,0:T(8,128)(2,1)S(1)}, u32[]{:S(2)}, u32[]{:S(2)}) collective-permute-start(bf16[848,128]{1,0:T(8,128)(2,1)S(1)} %get-tuple-element.42.refs_1_), channel_id=1, source_target_pairs={{0,1},{1,0},{2,3},{3,2},{4,8},{5,9},{6,10},{7,11},{8,4},{9,5},{10,... | collective-permute-start | bytes 651272 | tf_op jit(solution)/shard_map/ppermute | solution.py:479
  23.8 10.9 %collective-permute-start.4 = (f32[64,128]{1,0:T(8,128)S(1)}, f32[64,128]{1,0:T(8,128)S(1)}, u32[]{:S(2)}, u32[]{:S(2)}) collective-permute-start(f32[64,128]{1,0:T(8,128)S(1)} %get-tuple-element.46), channel_id=1, source_target_pairs={{0,4},{1,5},{2,6},{3,7},{4,0},{5,1},{6,2},{7,3},{8,12},{9,13},{10,... | collective-permute-start | bytes 98312 | tf_op jit(solution)/shard_map/ppermute | solution.py:447
  24.4 10.3 %collective-permute-start.5 = (f32[64,128]{1,0:T(8,128)S(1)}, f32[64,128]{1,0:T(8,128)S(1)}, u32[]{:S(2)}, u32[]{:S(2)}) collective-permute-start(f32[64,128]{1,0:T(8,128)S(1)} %get-tuple-element.47), channel_id=1, source_target_pairs={{0,1},{1,0},{2,3},{3,2},{4,8},{5,9},{6,10},{7,11},{8,4},{9,5},{10,... | collective-permute-start | bytes 98312 | tf_op jit(solution)/shard_map/ppermute | solution.py:447
  35.6 9.0 %copy-start.3 = (f32[1,1,64,128]{3,2,1,0:T(8,128)S(1)}, f32[1,1,64,128]{3,2,1,0:T(8,128)}, u32[]{:S(2)}) copy-start(f32[1,1,64,128]{3,2,1,0:T(8,128)} %param.13) | copy-start | bytes 98308

commit v7 on v6

--- a/solution.py
+++ b/solution.py
@@ -182,8 +182,8 @@
 
 
 def prepare(live_hbm, guess_hbm, rhs_hbm, blocks_hbm, coff_hbm, prolong_hbm, cdiag_hbm, notes_ref,
-            local_ref, arrive_ref, gather_ref, odd_ref, even_ref,
-            live_ref, guess_ref, rhs_ref, blocks_ref, coff_ref, prolong_ref, cdiag_ref, sems):
+            local_ref, arrive_ref, gather_ref, odd_ref, even_ref, blocks_ref,
+            live_ref, guess_ref, rhs_ref, coff_ref, prolong_ref, cdiag_ref, sems):
     size = guess_ref.shape[0]
     chunk = size // 4
     pairs = [(coff_hbm, coff_ref), (prolong_hbm, prolong_ref), (cdiag_hbm, cdiag_ref),
@@ -461,11 +461,12 @@
     )
     odd_guess, even_guess = exchange(odd, even)
     packed = ((cpd * (coff.shape[1] // LANES) + 4 * size + 16, LANES), bf16)
-    items = (guess, rhs, blocks, coff, prolong, cdiag)
-    local, arrive, gather, odd, even = call(
+    items = (guess, rhs, coff, prolong, cdiag)
+    local, arrive, gather, odd, even, blocks = call(
         prepare,
-        [field, ((2 * slots, count), bf16), ((count, LANES), bf16), packed, packed],
-        live, *items, notes, hbm=range(7),
+        [field, ((2 * slots, count), bf16), ((count, LANES), bf16), packed, packed,
+         (blocks.shape, bf16)],
+        live, guess, rhs, blocks, coff, prolong, cdiag, notes, hbm=range(7),
         scratch=[pltpu.SMEM(live.shape, live.dtype)]
         + [pltpu.VMEM(item.shape, item.dtype) for item in items]
         + [pltpu.SemaphoreType.DMA((10,))],

time: 45.6 us -> 45.5 us (level)
  no operation moved by 1% of the time
where the time goes in v7:
time: 45.5 us; the launch traced here: 45.2 us
  blocking collectives  31.5 us (69%)
  starting transfers between devices  7.25 us (16%)
  Pallas kernels  5.32 us (12%)
  between operations  0.67 us (1%)
    all_to_all x3, blocking collectives, everyone(): return lax.all_to_all(rows, AXES, 0, 0, tiled=True)  31.5 us
    pallas_call x6, Pallas kernels, call(): pl.pallas_call(body, out_shape=[jax.ShapeDtypeStruct(shape, kind) if fina...  5.32 us
    ppermute x2, starting transfers between devices, exchange(): lax.ppermute(even, AXES, moves[1])  4.65 us
    ppermute x1, starting transfers between devices, on_device(): even_pack = lax.ppermute(even, AXES, moves[1])  2.08 us
  transfers between devices with their start and end apart: 6, of which 1 were waited for; matrix products, arithmetic and copies ran while one was open for 0% of the time, Pallas kernels for 3%

profile of v7, /device:TPU:0, one launch (start us, length us, event | category | flops | bytes accessed | tf_op | source)
XLA Modules:
  0.0 45.2 jit_solution(10674346583128283535)
XLA Ops:
  0.6 0.9 %shard_map.131 = (f32[64,128]{1,0:T(8,128)S(1)}, f32[64,128]{1,0:T(8,128)S(1)}, s32[8,128]{1,0:T(8,128)S(1)}) custom-call(f32[64,128]{1,0:T(8,128)} %bitcast.32, s32[1,128]{1,0:T(1,128)} %bitcast.46, s32[2,128]{1,0:T(2,128)} %bitcast.44, s32[2,128]{1,0:T(2,128)} %bitcast.45, s32[1,128]{1,0:T(1,128)} %bitcast.47), custom_call_target="tpu_custom_call" | custom-call | tf_op jit(solution)/shard_map/pallas_call | solution.py:32
  1.6 0.5 %collective-permute-start = (f32[64,128]{1,0:T(8,128)S(1)}, f32[64,128]{1,0:T(8,128)S(1)}, u32[]{:S(2)}, u32[]{:S(2)}) collective-permute-start(f32[64,128]{1,0:T(8,128)S(1)} %get-tuple-element.36), channel_id=1, source_target_pairs={{0,1},{1,0},{2,3},{3,2},{4,8},{5,9},{6,10},{7,11},{8,4},{9,5},{10,... | collective-permute-start | bytes 98312 | tf_op jit(solution)/shard_map/ppermute | solution.py:447
  2.1 4.0 %collective-permute-start.1 = (f32[64,128]{1,0:T(8,128)S(1)}, f32[64,128]{1,0:T(8,128)S(1)}, u32[]{:S(2)}, u32[]{:S(2)}) collective-permute-start(f32[64,128]{1,0:T(8,128)S(1)} %get-tuple-element.37), channel_id=1, source_target_pairs={{0,4},{1,5},{2,6},{3,7},{4,0},{5,1},{6,2},{7,3},{8,12},{9,13},{10,... | collective-permute-start | bytes 98312 | tf_op jit(solution)/shard_map/ppermute | solution.py:447
  6.1 0.0 copy-start
  6.1 0.0 copy-start.1
  6.1 1.5 %shard_map.132 = (f32[64,128]{1,0:T(8,128)S(1)}, bf16[256,128]{1,0:T(8,128)(2,1)S(1)}, bf16[128,128]{1,0:T(8,128)(2,1)S(1)}, bf16[848,128]{1,0:T(8,128)(2,1)S(1)...) custom-call(s32[1,2]{1,0:T(1,128)} %bitcast.48, f32[64,128]{1,0:T(8,128)} %bitcast.33, ...), custom_call_target="tpu_custom_call" | custom-call | tf_op jit(solution)/shard_map/pallas_call | solution.py:32
  7.6 0.0 collective-permute-done.refs_1_
  7.6 0.4 collective-permute-done.1.refs_2_
  8.0 0.0 copy-done
  8.0 0.0 copy-done.1
  8.0 0.3 shard_map.133
  8.3 2.1 %collective-permute-start.2 = (bf16[848,128]{1,0:T(8,128)(2,1)S(1)}, bf16[848,128]{1,0:T(8,128)(2,1)S(1)}, u32[]{:S(2)}, u32[]{:S(2)}) collective-permute-start(bf16[848,128]{1,0:T(8,128)(2,1)S(1)} %get-tuple-element.44), channel_id=1, source_target_pairs={{0,4},{1,5},{2,6},{3,7},{4,0},{5,1},{6,2},{7,3},{8,12},{9,13},{10,... | collective-permute-start | bytes 651272 | tf_op jit(solution)/shard_map/ppermute | solution.py:479
  10.4 0.0 collective-permute-start.3
  10.4 12.3 %all_to_all.33 = f32[32,1,128]{2,1,0:T(1,128)S(1)} all-to-all(f32[32,1,128]{2,1,0:T(1,128)S(1)} %bitcast.41), channel_id=1, replica_groups=mesh['sub'=8,'grp'=4] {'sub','grp'}, dimensions={0} | all-to-all | bytes 32768 | tf_op jit(solution)/shard_map/all_to_all | solution.py:450
  22.7 0.0 collective-permute-done.2.refs_2_
  22.7 0.0 collective-permute-done.3.refs_3_
  22.7 1.0 %shard_map.134 = (f32[64,128]{1,0:T(8,128)S(1)}, f32[64,128]{1,0:T(8,128)S(1)}, f32[64,128]{1,0:T(8,128)S(1)}, f32[32,128]{1,0:T(8,128)S(1)}, f32[64,128]{1,0:T(...) custom-call(f32[32,128]{1,0:T(8,128)S(1)} %bitcast.35, ...), custom_call_target="tpu_custom_call" | custom-call | tf_op jit(solution)/shard_map/pallas_call | solution.py:32
  23.7 0.6 %collective-permute-start.4 = (f32[64,128]{1,0:T(8,128)S(1)}, f32[64,128]{1,0:T(8,128)S(1)}, u32[]{:S(2)}, u32[]{:S(2)}) collective-permute-start(f32[64,128]{1,0:T(8,128)S(1)} %get-tuple-element.48), channel_id=1, source_target_pairs={{0,4},{1,5},{2,6},{3,7},{4,0},{5,1},{6,2},{7,3},{8,12},{9,13},{10,... | collective-permute-start | bytes 98312 | tf_op jit(solution)/shard_map/ppermute | solution.py:447
  24.3 0.0 collective-permute-start.5
  24.3 10.3 %all_to_all.34 = f32[32,1,128]{2,1,0:T(1,128)S(1)} all-to-all(f32[32,1,128]{2,1,0:T(1,128)S(1)} %bitcast.39), channel_id=1, replica_groups=mesh['sub'=8,'grp'=4] {'sub','grp'}, dimensions={0} | all-to-all | bytes 32768 | tf_op jit(solution)/shard_map/all_to_all | solution.py:450
  34.6 0.0 collective-permute-done.4.refs_2_
  34.6 0.0 collective-permute-done.5.refs_3_
  34.6 0.9 %shard_map.135 = (f32[64,128]{1,0:T(8,128)S(1)}, f32[64,128]{1,0:T(8,128)S(1)}, f32[64,128]{1,0:T(8,128)S(1)}, f32[8,128]{1,0:T(8,128)S(1)}, f32[32,128]{1,0:T(8,128)S(1)}) custom-call(f32[32,128]{1,0:T(8,128)S(1)} %bitcast.37, f32[32,128]{1,0:T(8,128)S(1)} %bitcast.36, f32[64,128]{1,0:T(8,128)S(1)} %collective-permute-done.4.refs_2_, ...), custom_call_target="tpu_custom_call" | custom-call | tf_op jit(solution)/shard_map/pallas_call | solution.py:32
  35.5 0.0 copy-start.2
  35.5 9.0 %all_to_all.35 = f32[32,1,128]{2,1,0:T(1,128)S(1)} all-to-all(f32[32,1,128]{2,1,0:T(1,128)S(1)} %bitcast.40), channel_id=1, replica_groups=mesh['sub'=8,'grp'=4] {'sub','grp'}, dimensions={0} | all-to-all | bytes 32768 | tf_op jit(solution)/shard_map/all_to_all | solution.py:450
  44.4 0.0 copy-done.2
  44.4 0.7 %shard_map.136 = (f32[64,128]{1,0:T(8,128)}, f32[64,128]{1,0:T(8,128)}) custom-call(f32[32,128]{1,0:T(8,128)S(1)} %bitcast.38, f32[8,128]{1,0:T(8,128)S(1)} %get-tuple-element.59.scalars_ref, f32[64,128]{1,0:T(8,128)S(1)} %bitcast.34, f32[64,128]{1,0:T(8,128)S(1)} %get-tuple-element.56.refs_10_.basis_ref, f32[64,128]{1,0:T(8,128)S(1)} %get-tuple-element.60.basis_two_ref, ...), custom_call_target="tpu_custom_call" | custom-call | tf_op jit(solution)/shard_map/pallas_call | solution.py:32
Async XLA Ops:
  1.6 6.1 %collective-permute-start = (f32[64,128]{1,0:T(8,128)S(1)}, f32[64,128]{1,0:T(8,128)S(1)}, u32[]{:S(2)}, u32[]{:S(2)}) collective-permute-start(f32[64,128]{1,0:T(8,128)S(1)} %get-tuple-element.36), channel_id=1, source_target_pairs={{0,1},{1,0},{2,3},{3,2},{4,8},{5,9},{6,10},{7,11},{8,4},{9,5},{10,... | collective-permute-start | bytes 98312 | tf_op jit(solution)/shard_map/ppermute | solution.py:447
  2.1 5.9 %collective-permute-start.1 = (f32[64,128]{1,0:T(8,128)S(1)}, f32[64,128]{1,0:T(8,128)S(1)}, u32[]{:S(2)}, u32[]{:S(2)}) collective-permute-start(f32[64,128]{1,0:T(8,128)S(1)} %get-tuple-element.37), channel_id=1, source_target_pairs={{0,4},{1,5},{2,6},{3,7},{4,0},{5,1},{6,2},{7,3},{8,12},{9,13},{10,... | collective-permute-start | bytes 98312 | tf_op jit(solution)/shard_map/ppermute | solution.py:447
  6.1 1.9 %copy-start = (f32[1,1,64,128]{3,2,1,0:T(8,128)S(1)}, f32[1,1,64,128]{3,2,1,0:T(8,128)}, u32[]{:S(2)}) copy-start(f32[1,1,64,128]{3,2,1,0:T(8,128)} %param.17) | copy-start | bytes 98308
  6.1 1.9 %copy-start.1 = (f32[1,1,64,128]{3,2,1,0:T(8,128)S(1)}, f32[1,1,64,128]{3,2,1,0:T(8,128)}, u32[]{:S(2)}) copy-start(f32[1,1,64,128]{3,2,1,0:T(8,128)} %param.16) | copy-start | bytes 98308
  8.3 14.4 %collective-permute-start.2 = (bf16[848,128]{1,0:T(8,128)(2,1)S(1)}, bf16[848,128]{1,0:T(8,128)(2,1)S(1)}, u32[]{:S(2)}, u32[]{:S(2)}) collective-permute-start(bf16[848,128]{1,0:T(8,128)(2,1)S(1)} %get-tuple-element.44), channel_id=1, source_target_pairs={{0,4},{1,5},{2,6},{3,7},{4,0},{5,1},{6,2},{7,3},{8,12},{9,13},{10,... | collective-permute-start | bytes 651272 | tf_op jit(solution)/shard_map/ppermute | solution.py:479
  10.4 12.3 %collective-permute-start.3 = (bf16[848,128]{1,0:T(8,128)(2,1)S(1)}, bf16[848,128]{1,0:T(8,128)(2,1)S(1)}, u32[]{:S(2)}, u32[]{:S(2)}) collective-permute-start(bf16[848,128]{1,0:T(8,128)(2,1)S(1)} %get-tuple-element.43.refs_1_), channel_id=1, source_target_pairs={{0,1},{1,0},{2,3},{3,2},{4,8},{5,9},{6,10},{7,11},{8,4},{9,5},{10,... | collective-permute-start | bytes 651272 | tf_op jit(solution)/shard_map/ppermute | solution.py:480
  23.7 10.9 %collective-permute-start.4 = (f32[64,128]{1,0:T(8,128)S(1)}, f32[64,128]{1,0:T(8,128)S(1)}, u32[]{:S(2)}, u32[]{:S(2)}) collective-permute-start(f32[64,128]{1,0:T(8,128)S(1)} %get-tuple-element.48), channel_id=1, source_target_pairs={{0,4},{1,5},{2,6},{3,7},{4,0},{5,1},{6,2},{7,3},{8,12},{9,13},{10,... | collective-permute-start | bytes 98312 | tf_op jit(solution)/shard_map/ppermute | solution.py:447
  24.3 10.3 %collective-permute-start.5 = (f32[64,128]{1,0:T(8,128)S(1)}, f32[64,128]{1,0:T(8,128)S(1)}, u32[]{:S(2)}, u32[]{:S(2)}) collective-permute-start(f32[64,128]{1,0:T(8,128)S(1)} %get-tuple-element.49), channel_id=1, source_target_pairs={{0,1},{1,0},{2,3},{3,2},{4,8},{5,9},{6,10},{7,11},{8,4},{9,5},{10,... | collective-permute-start | bytes 98312 | tf_op jit(solution)/shard_map/ppermute | solution.py:447
  35.5 9.0 %copy-start.2 = (f32[1,1,64,128]{3,2,1,0:T(8,128)S(1)}, f32[1,1,64,128]{3,2,1,0:T(8,128)}, u32[]{:S(2)}) copy-start(f32[1,1,64,128]{3,2,1,0:T(8,128)} %param.13) | copy-start | bytes 98308

commit v8 on v7

--- a/solution.py
+++ b/solution.py
@@ -68,12 +68,12 @@
     return (lax.axis_index("sub") + side + 1) % 2
 
 
-def along_lanes(field, places, axis):
-    return jnp.take_along_axis(field, places, axis=axis, mode="promise_in_bounds")
+def along_lanes(field, places):
+    return jnp.take_along_axis(field, places, axis=1, mode="promise_in_bounds")
 
 
 def pick(field, places):
-    return along_lanes(field, jnp.broadcast_to(places, field.shape), axis=1)
+    return along_lanes(field, jnp.broadcast_to(places, field.shape))
 
 
 def pieces(field, count=2):
@@ -125,14 +125,10 @@
     ref[...] = jnp.broadcast_to(row, ref.shape)
 
 
-def flat(ref):
-    return ref[...] if len(ref.shape) == 2 else ref[:, 0, :]
-
-
 def summed(ref, first_lane, count):
-    rows = jnp.broadcast_to(jnp.sum(flat(ref), axis=0, keepdims=True), (8, LANES))
+    rows = jnp.broadcast_to(jnp.sum(ref[...], axis=0, keepdims=True), (8, LANES))
     return [
-        along_lanes(rows, jnp.full((8, LANES), first_lane + at, jnp.int32), axis=1)[0:1]
+        along_lanes(rows, jnp.full((8, LANES), first_lane + at, jnp.int32))[0:1]
         for at in range(count)
     ]
 
@@ -262,36 +258,6 @@
     info_ref[...] = jnp.concatenate(infos + [jnp.zeros((3, LANES), f32)], axis=0)
 
 
-def unpack(own_ref, even_ref, odd_ref, cpd, matrix_ref, odd_weights_ref, even_weights_ref,
-           odd_first_ref, even_first_ref, info_ref):
-    width = matrix_ref.shape[1]
-    size = odd_first_ref.shape[0]
-    base = cpd * (width // LANES)
-    rows = []
-    for slot, ref in enumerate((own_ref, odd_ref, even_ref)):
-        for at in range(0, width, LANES):
-            start = at // LANES * cpd
-            matrix_ref[slot * SLOT : slot * SLOT + cpd, at : at + LANES] = ref[start : start + cpd, :]
-        matrix_ref[slot * SLOT + cpd : (slot + 1) * SLOT, :] = jnp.zeros((SLOT - cpd, width), bf16)
-        rows.append(ref[base + 2 * size : base + 2 * size + 16, :].astype(f32))
-    for ref, weights_ref, near_ref in (
-        (odd_ref, odd_weights_ref, odd_first_ref), (even_ref, even_weights_ref, even_first_ref)
-    ):
-        for start, to_ref in ((base, weights_ref), (base + 2 * size + 16, near_ref)):
-            high, low = ref[start : start + size, :], ref[start + size : start + 2 * size, :]
-            to_ref[...] = high.astype(f32) + low.astype(f32)
-    infos = [row[1:2] + row[2:3] + row[3:4] for row in rows] + [row[0:1] for row in rows[1:]]
-    info_ref[...] = jnp.concatenate(infos + [jnp.zeros((3, LANES), f32)], axis=0)
-
-
-def look_ahead(image_ref, first_ref, jscale_ref, prolong_ref, blocks_ref, notes_ref,
-               lead_two_ref, lead_ref, pull_ref):
-    valve, jscale = notes_ref[VALVE], jscale_ref[...]
-    lead_two_ref[...] = local_product(blocks_ref, valve, jscale * image_ref[...])
-    lead_ref[...] = local_product(blocks_ref, valve, jscale * first_ref[...])
-    pull_ref[...] = local_product(blocks_ref, valve, prolong_ref[...])
-
-
 def solve_coarse(parts, matrix_ref, near_rows, cdiags, cpd):
     group = parts[0].shape[0]
     shape = (group, LANES)
@@ -301,7 +267,7 @@
     source = lax.rem(lane - cpd * row + cpd * group, LANES)
     tiles = []
     for part in parts:
-        shifted = along_lanes(part, source, axis=1)
+        shifted = along_lanes(part, source)
         tiles.extend(jnp.where(mask, shifted, 0.0) for mask in masks)
     product = lax.dot_general(
         jnp.concatenate(tiles, axis=1).astype(bf16), matrix_ref[...], (((1,), (1,)), ((), ())),
@@ -317,7 +283,7 @@
 
 def parts_of(ref, cpd):
     group = math.lcm(cpd, LANES) // cpd
-    rows = flat(ref)
+    rows = ref[...]
     return [rows[at : at + group, :] for at in range(0, rows.shape[0], group)]
 
 
@@ -338,7 +304,7 @@
 
 def spread_of(solution, agg):
     wide = jnp.broadcast_to(solution, (8, LANES))
-    return along_lanes(wide, jnp.broadcast_to(agg, (8, LANES)), axis=1)[0:1]
+    return along_lanes(wide, jnp.broadcast_to(agg, (8, LANES)))[0:1]
 
 
 def near_spread(weights_ref, info_ref, side, solution):

time: 45.5 us -> 45.5 us (level)
  no operation moved by 1% of the time
where the time goes in v8:
time: 45.5 us; the launch traced here: 45.2 us
  blocking collectives  31.5 us (69%)
  starting transfers between devices  7.25 us (16%)
  Pallas kernels  5.32 us (12%)
  between operations  0.67 us (1%)
    all_to_all x3, blocking collectives, everyone(): return lax.all_to_all(rows, AXES, 0, 0, tiled=True)  31.5 us
    pallas_call x6, Pallas kernels, call(): pl.pallas_call(body, out_shape=[jax.ShapeDtypeStruct(shape, kind) if fina...  5.32 us
    ppermute x2, starting transfers between devices, exchange(): lax.ppermute(even, AXES, moves[1])  4.65 us
    ppermute x1, starting transfers between devices, on_device(): even_pack = lax.ppermute(even, AXES, moves[1])  2.08 us
  transfers between devices with their start and end apart: 6, of which 1 were waited for; matrix products, arithmetic and copies ran while one was open for 0% of the time, Pallas kernels for 3%

profile of v8, /device:TPU:0, one launch (start us, length us, event | category | flops | bytes accessed | tf_op | source)
XLA Modules:
  0.0 45.2 jit_solution(10674346583128283535)
XLA Ops:
  0.6 0.9 %shard_map.131 = (f32[64,128]{1,0:T(8,128)S(1)}, f32[64,128]{1,0:T(8,128)S(1)}, s32[8,128]{1,0:T(8,128)S(1)}) custom-call(f32[64,128]{1,0:T(8,128)} %bitcast.32, s32[1,128]{1,0:T(1,128)} %bitcast.46, s32[2,128]{1,0:T(2,128)} %bitcast.44, s32[2,128]{1,0:T(2,128)} %bitcast.45, s32[1,128]{1,0:T(1,128)} %bitcast.47), custom_call_target="tpu_custom_call" | custom-call | tf_op jit(solution)/shard_map/pallas_call | solution.py:32
  1.6 0.5 %collective-permute-start = (f32[64,128]{1,0:T(8,128)S(1)}, f32[64,128]{1,0:T(8,128)S(1)}, u32[]{:S(2)}, u32[]{:S(2)}) collective-permute-start(f32[64,128]{1,0:T(8,128)S(1)} %get-tuple-element.36), channel_id=1, source_target_pairs={{0,1},{1,0},{2,3},{3,2},{4,8},{5,9},{6,10},{7,11},{8,4},{9,5},{10,... | collective-permute-start | bytes 98312 | tf_op jit(solution)/shard_map/ppermute | solution.py:413
  2.1 4.0 %collective-permute-start.1 = (f32[64,128]{1,0:T(8,128)S(1)}, f32[64,128]{1,0:T(8,128)S(1)}, u32[]{:S(2)}, u32[]{:S(2)}) collective-permute-start(f32[64,128]{1,0:T(8,128)S(1)} %get-tuple-element.37), channel_id=1, source_target_pairs={{0,4},{1,5},{2,6},{3,7},{4,0},{5,1},{6,2},{7,3},{8,12},{9,13},{10,... | collective-permute-start | bytes 98312 | tf_op jit(solution)/shard_map/ppermute | solution.py:413
  6.1 0.0 copy-start
  6.1 0.0 copy-start.1
  6.1 1.5 %shard_map.132 = (f32[64,128]{1,0:T(8,128)S(1)}, bf16[256,128]{1,0:T(8,128)(2,1)S(1)}, bf16[128,128]{1,0:T(8,128)(2,1)S(1)}, bf16[848,128]{1,0:T(8,128)(2,1)S(1)...) custom-call(s32[1,2]{1,0:T(1,128)} %bitcast.48, f32[64,128]{1,0:T(8,128)} %bitcast.33, ...), custom_call_target="tpu_custom_call" | custom-call | tf_op jit(solution)/shard_map/pallas_call | solution.py:32
  7.6 0.0 collective-permute-done.refs_1_
  7.6 0.4 collective-permute-done.1.refs_2_
  8.0 0.0 copy-done
  8.0 0.0 copy-done.1
  8.0 0.3 shard_map.133
  8.3 2.1 %collective-permute-start.2 = (bf16[848,128]{1,0:T(8,128)(2,1)S(1)}, bf16[848,128]{1,0:T(8,128)(2,1)S(1)}, u32[]{:S(2)}, u32[]{:S(2)}) collective-permute-start(bf16[848,128]{1,0:T(8,128)(2,1)S(1)} %get-tuple-element.44), channel_id=1, source_target_pairs={{0,4},{1,5},{2,6},{3,7},{4,0},{5,1},{6,2},{7,3},{8,12},{9,13},{10,... | collective-permute-start | bytes 651272 | tf_op jit(solution)/shard_map/ppermute | solution.py:445
  10.4 0.0 collective-permute-start.3
  10.4 12.3 %all_to_all.33 = f32[32,1,128]{2,1,0:T(1,128)S(1)} all-to-all(f32[32,1,128]{2,1,0:T(1,128)S(1)} %bitcast.41), channel_id=1, replica_groups=mesh['sub'=8,'grp'=4] {'sub','grp'}, dimensions={0} | all-to-all | bytes 32768 | tf_op jit(solution)/shard_map/all_to_all | solution.py:416
  22.7 0.0 collective-permute-done.2.refs_2_
  22.7 0.0 collective-permute-done.3.refs_3_
  22.7 1.0 %shard_map.134 = (f32[64,128]{1,0:T(8,128)S(1)}, f32[64,128]{1,0:T(8,128)S(1)}, f32[64,128]{1,0:T(8,128)S(1)}, f32[32,128]{1,0:T(8,128)S(1)}, f32[64,128]{1,0:T(...) custom-call(f32[32,128]{1,0:T(8,128)S(1)} %bitcast.35, ...), custom_call_target="tpu_custom_call" | custom-call | tf_op jit(solution)/shard_map/pallas_call | solution.py:32
  23.7 0.6 %collective-permute-start.4 = (f32[64,128]{1,0:T(8,128)S(1)}, f32[64,128]{1,0:T(8,128)S(1)}, u32[]{:S(2)}, u32[]{:S(2)}) collective-permute-start(f32[64,128]{1,0:T(8,128)S(1)} %get-tuple-element.48), channel_id=1, source_target_pairs={{0,4},{1,5},{2,6},{3,7},{4,0},{5,1},{6,2},{7,3},{8,12},{9,13},{10,... | collective-permute-start | bytes 98312 | tf_op jit(solution)/shard_map/ppermute | solution.py:413
  24.3 0.0 collective-permute-start.5
  24.3 10.3 %all_to_all.34 = f32[32,1,128]{2,1,0:T(1,128)S(1)} all-to-all(f32[32,1,128]{2,1,0:T(1,128)S(1)} %bitcast.39), channel_id=1, replica_groups=mesh['sub'=8,'grp'=4] {'sub','grp'}, dimensions={0} | all-to-all | bytes 32768 | tf_op jit(solution)/shard_map/all_to_all | solution.py:416
  34.6 0.0 collective-permute-done.4.refs_2_
  34.6 0.0 collective-permute-done.5.refs_3_
  34.6 0.9 %shard_map.135 = (f32[64,128]{1,0:T(8,128)S(1)}, f32[64,128]{1,0:T(8,128)S(1)}, f32[64,128]{1,0:T(8,128)S(1)}, f32[8,128]{1,0:T(8,128)S(1)}, f32[32,128]{1,0:T(8,128)S(1)}) custom-call(f32[32,128]{1,0:T(8,128)S(1)} %bitcast.37, f32[32,128]{1,0:T(8,128)S(1)} %bitcast.36, f32[64,128]{1,0:T(8,128)S(1)} %collective-permute-done.4.refs_2_, ...), custom_call_target="tpu_custom_call" | custom-call | tf_op jit(solution)/shard_map/pallas_call | solution.py:32
  35.5 0.0 copy-start.2
  35.5 9.0 %all_to_all.35 = f32[32,1,128]{2,1,0:T(1,128)S(1)} all-to-all(f32[32,1,128]{2,1,0:T(1,128)S(1)} %bitcast.40), channel_id=1, replica_groups=mesh['sub'=8,'grp'=4] {'sub','grp'}, dimensions={0} | all-to-all | bytes 32768 | tf_op jit(solution)/shard_map/all_to_all | solution.py:416
  44.4 0.0 copy-done.2
  44.4 0.7 %shard_map.136 = (f32[64,128]{1,0:T(8,128)}, f32[64,128]{1,0:T(8,128)}) custom-call(f32[32,128]{1,0:T(8,128)S(1)} %bitcast.38, f32[8,128]{1,0:T(8,128)S(1)} %get-tuple-element.59.scalars_ref, f32[64,128]{1,0:T(8,128)S(1)} %bitcast.34, f32[64,128]{1,0:T(8,128)S(1)} %get-tuple-element.56.refs_10_.basis_ref, f32[64,128]{1,0:T(8,128)S(1)} %get-tuple-element.60.basis_two_ref, ...), custom_call_target="tpu_custom_call" | custom-call | tf_op jit(solution)/shard_map/pallas_call | solution.py:32
Async XLA Ops:
  1.6 6.1 %collective-permute-start = (f32[64,128]{1,0:T(8,128)S(1)}, f32[64,128]{1,0:T(8,128)S(1)}, u32[]{:S(2)}, u32[]{:S(2)}) collective-permute-start(f32[64,128]{1,0:T(8,128)S(1)} %get-tuple-element.36), channel_id=1, source_target_pairs={{0,1},{1,0},{2,3},{3,2},{4,8},{5,9},{6,10},{7,11},{8,4},{9,5},{10,... | collective-permute-start | bytes 98312 | tf_op jit(solution)/shard_map/ppermute | solution.py:413
  2.1 5.9 %collective-permute-start.1 = (f32[64,128]{1,0:T(8,128)S(1)}, f32[64,128]{1,0:T(8,128)S(1)}, u32[]{:S(2)}, u32[]{:S(2)}) collective-permute-start(f32[64,128]{1,0:T(8,128)S(1)} %get-tuple-element.37), channel_id=1, source_target_pairs={{0,4},{1,5},{2,6},{3,7},{4,0},{5,1},{6,2},{7,3},{8,12},{9,13},{10,... | collective-permute-start | bytes 98312 | tf_op jit(solution)/shard_map/ppermute | solution.py:413
  6.1 1.9 %copy-start = (f32[1,1,64,128]{3,2,1,0:T(8,128)S(1)}, f32[1,1,64,128]{3,2,1,0:T(8,128)}, u32[]{:S(2)}) copy-start(f32[1,1,64,128]{3,2,1,0:T(8,128)} %param.17) | copy-start | bytes 98308
  6.1 1.9 %copy-start.1 = (f32[1,1,64,128]{3,2,1,0:T(8,128)S(1)}, f32[1,1,64,128]{3,2,1,0:T(8,128)}, u32[]{:S(2)}) copy-start(f32[1,1,64,128]{3,2,1,0:T(8,128)} %param.16) | copy-start | bytes 98308
  8.3 14.4 %collective-permute-start.2 = (bf16[848,128]{1,0:T(8,128)(2,1)S(1)}, bf16[848,128]{1,0:T(8,128)(2,1)S(1)}, u32[]{:S(2)}, u32[]{:S(2)}) collective-permute-start(bf16[848,128]{1,0:T(8,128)(2,1)S(1)} %get-tuple-element.44), channel_id=1, source_target_pairs={{0,4},{1,5},{2,6},{3,7},{4,0},{5,1},{6,2},{7,3},{8,12},{9,13},{10,... | collective-permute-start | bytes 651272 | tf_op jit(solution)/shard_map/ppermute | solution.py:445
  10.4 12.3 %collective-permute-start.3 = (bf16[848,128]{1,0:T(8,128)(2,1)S(1)}, bf16[848,128]{1,0:T(8,128)(2,1)S(1)}, u32[]{:S(2)}, u32[]{:S(2)}) collective-permute-start(bf16[848,128]{1,0:T(8,128)(2,1)S(1)} %get-tuple-element.43.refs_1_), channel_id=1, source_target_pairs={{0,1},{1,0},{2,3},{3,2},{4,8},{5,9},{6,10},{7,11},{8,4},{9,5},{10,... | collective-permute-start | bytes 651272 | tf_op jit(solution)/shard_map/ppermute | solution.py:446
  23.7 10.9 %collective-permute-start.4 = (f32[64,128]{1,0:T(8,128)S(1)}, f32[64,128]{1,0:T(8,128)S(1)}, u32[]{:S(2)}, u32[]{:S(2)}) collective-permute-start(f32[64,128]{1,0:T(8,128)S(1)} %get-tuple-element.48), channel_id=1, source_target_pairs={{0,4},{1,5},{2,6},{3,7},{4,0},{5,1},{6,2},{7,3},{8,12},{9,13},{10,... | collective-permute-start | bytes 98312 | tf_op jit(solution)/shard_map/ppermute | solution.py:413
  24.3 10.3 %collective-permute-start.5 = (f32[64,128]{1,0:T(8,128)S(1)}, f32[64,128]{1,0:T(8,128)S(1)}, u32[]{:S(2)}, u32[]{:S(2)}) collective-permute-start(f32[64,128]{1,0:T(8,128)S(1)} %get-tuple-element.49), channel_id=1, source_target_pairs={{0,1},{1,0},{2,3},{3,2},{4,8},{5,9},{6,10},{7,11},{8,4},{9,5},{10,... | collective-permute-start | bytes 98312 | tf_op jit(solution)/shard_map/ppermute | solution.py:413
  35.5 9.0 %copy-start.2 = (f32[1,1,64,128]{3,2,1,0:T(8,128)S(1)}, f32[1,1,64,128]{3,2,1,0:T(8,128)}, u32[]{:S(2)}) copy-start(f32[1,1,64,128]{3,2,1,0:T(8,128)} %param.13) | copy-start | bytes 98308

commit v9 on v8

--- a/solution.py
+++ b/solution.py
@@ -140,20 +140,11 @@
     return copies
 
 
-def first_send(guess_hbm, agg_hbm, send_hbm, recv_hbm, valve_hbm, odd_ref, even_ref, notes_ref,
-               guess_ref, agg_ref, send_ref, recv_ref, valve_ref, sems):
-    pairs = (
-        (send_hbm, send_ref), (guess_hbm, guess_ref), (agg_hbm, agg_ref), (recv_hbm, recv_ref),
-        (valve_hbm, valve_ref),
-    )
-    for copy in copy_all(pairs, sems):
+def first_send(guess_hbm, send_hbm, odd_ref, even_ref, guess_ref, send_ref, sems):
+    for copy in copy_all(((send_hbm, send_ref), (guess_hbm, guess_ref)), sems):
         copy.wait()
     for side, ref in enumerate((odd_ref, even_ref)):
         ref[...] = pick(guess_ref[...], row_of(send_ref, parity(side)))
-    notes_ref[...] = jnp.concatenate(
-        [send_ref[...], recv_ref[...], agg_ref[...], valve_ref[...], jnp.zeros((2, LANES), jnp.int32)],
-        axis=0,
-    )
 
 
 def wide(row):
@@ -177,18 +168,26 @@
     ref[base + 2 * size : base + 2 * size + 16, :] = jnp.concatenate(rows, axis=0).astype(bf16)
 
 
-def prepare(live_hbm, guess_hbm, rhs_hbm, blocks_hbm, coff_hbm, prolong_hbm, cdiag_hbm, notes_ref,
-            local_ref, arrive_ref, gather_ref, odd_ref, even_ref, blocks_ref,
-            live_ref, guess_ref, rhs_ref, coff_ref, prolong_ref, cdiag_ref, sems):
+def prepare(agg_hbm, send_hbm, recv_hbm, valve_hbm, live_hbm, guess_hbm, rhs_hbm, blocks_hbm,
+            coff_hbm, prolong_hbm, cdiag_hbm, local_ref, arrive_ref, gather_ref, odd_ref, even_ref,
+            blocks_ref, notes_ref, agg_ref, send_ref, recv_ref, valve_ref, live_ref, guess_ref,
+            rhs_ref, coff_ref, prolong_ref, cdiag_ref, sems):
     size = guess_ref.shape[0]
     chunk = size // 4
-    pairs = [(coff_hbm, coff_ref), (prolong_hbm, prolong_ref), (cdiag_hbm, cdiag_ref),
-             (live_hbm, live_ref), (guess_hbm, guess_ref)]
+    pairs = [
+        (agg_hbm, agg_ref), (send_hbm, send_ref), (recv_hbm, recv_ref), (valve_hbm, valve_ref),
+        (coff_hbm, coff_ref), (prolong_hbm, prolong_ref), (cdiag_hbm, cdiag_ref),
+        (live_hbm, live_ref), (guess_hbm, guess_ref),
+    ]
     for at in range(0, size, chunk):
         pairs.append((blocks_hbm.at[at : at + chunk], blocks_ref.at[at : at + chunk]))
     copies = copy_all(pairs + [(rhs_hbm, rhs_ref)], sems)
-    for copy in copies[:4]:
+    for copy in copies[:8]:
         copy.wait()
+    notes_ref[...] = jnp.concatenate(
+        [send_ref[...], recv_ref[...], agg_ref[...], valve_ref[...], jnp.zeros((2, LANES), jnp.int32)],
+        axis=0,
+    )
     cdiag = wide(cdiag_ref[...])
     for side, ref in enumerate((odd_ref, even_ref)):
         places = row_of(notes_ref.at[SEND], parity(side))
@@ -207,12 +206,12 @@
         live = jnp.where(there, live_ref[0, which], 0)
         hit = (row_of(notes_ref.at[RECV], which) == row) & (slot < live)
         arrive_ref[side * slots : (side + 1) * slots, :] = jnp.where(hit, 1.0, 0.0).T.astype(bf16)
-    copies[4].wait()
+    copies[8].wait()
     guess = guess_ref[...]
     penalty = penalty_gain * notes_ref[VALVE].astype(f32)
     for at in range(0, size, 8):
         if at % chunk == 0:
-            copies[5 + at // chunk].wait()
+            copies[9 + at // chunk].wait()
         part = slice(at, at + 8)
         local_ref[part, :] = block_rows(blocks_ref[part], guess) + penalty * guess[part]
     copies[-1].wait()
@@ -419,23 +418,25 @@
     near = ((size, slots), f32)
     rows_out = ((devices, LANES), f32)
     small = ((8, LANES), f32)
-    items = (guess, agg, send, recv, valve)
-    odd, even, notes = call(
-        first_send, [near, near, ((8, LANES), jnp.int32)], *items, hbm=range(5), limit=16,
+    items = (guess, send)
+    odd, even = call(
+        first_send, [near, near], *items, hbm=range(2), limit=16,
         scratch=[pltpu.VMEM(item.shape, item.dtype) for item in items]
-        + [pltpu.SemaphoreType.DMA((5,))],
+        + [pltpu.SemaphoreType.DMA((2,))],
     )
     odd_guess, even_guess = exchange(odd, even)
     packed = ((cpd * (coff.shape[1] // LANES) + 4 * size + 16, LANES), bf16)
+    small_items = (agg, send, recv, valve)
     items = (guess, rhs, coff, prolong, cdiag)
-    local, arrive, gather, odd, even, blocks = call(
+    local, arrive, gather, odd, even, blocks, notes = call(
         prepare,
         [field, ((2 * slots, count), bf16), ((count, LANES), bf16), packed, packed,
-         (blocks.shape, bf16)],
-        live, guess, rhs, blocks, coff, prolong, cdiag, notes, hbm=range(7),
-        scratch=[pltpu.SMEM(live.shape, live.dtype)]
+         (blocks.shape, bf16), ((8, LANES), jnp.int32)],
+        *small_items, live, guess, rhs, blocks, coff, prolong, cdiag, hbm=range(11),
+        scratch=[pltpu.VMEM(item.shape, item.dtype) for item in small_items]
+        + [pltpu.SMEM(live.shape, live.dtype)]
         + [pltpu.VMEM(item.shape, item.dtype) for item in items]
-        + [pltpu.SemaphoreType.DMA((10,))],
+        + [pltpu.SemaphoreType.DMA((14,))],
     )
     first, rows, odd, even = call(
         lambda *refs: residual(*refs[:10], cpd, *refs[10:]), [field, rows_out, packed, packed],

time: 45.5 us -> 45.5 us (level)
  transfers between devices with their start and end apart: 6 -> 6, of which waited for: 1 -> 1; matrix products, arithmetic and copies ran while one was open for 0% -> 0% of each run, Pallas kernels for 3% -> 4%
where the time goes in v9:
time: 45.5 us; the launch traced here: 45.1 us
  blocking collectives  31.5 us (69%)
  starting transfers between devices  7.25 us (16%)
  Pallas kernels  5.39 us (12%)
  between operations  0.67 us (1%)
    all_to_all x3, blocking collectives, everyone(): return lax.all_to_all(rows, AXES, 0, 0, tiled=True)  31.5 us
    pallas_call x6, Pallas kernels, call(): pl.pallas_call(body, out_shape=[jax.ShapeDtypeStruct(shape, kind) if fina...  5.39 us
    ppermute x2, starting transfers between devices, exchange(): lax.ppermute(even, AXES, moves[1])  4.65 us
    ppermute x1, starting transfers between devices, on_device(): even_pack = lax.ppermute(even, AXES, moves[1])  2.08 us
  transfers between devices with their start and end apart: 6, of which 1 were waited for; matrix products, arithmetic and copies ran while one was open for 0% of the time, Pallas kernels for 4%

profile of v9, /device:TPU:0, one launch (start us, length us, event | category | flops | bytes accessed | tf_op | source)
XLA Modules:
  0.0 45.1 jit_solution(9773202691089118865)
XLA Ops:
  0.6 0.9 %shard_map.132 = (f32[64,128]{1,0:T(8,128)S(1)}, f32[64,128]{1,0:T(8,128)S(1)}) custom-call(f32[64,128]{1,0:T(8,128)} %bitcast.32, s32[2,128]{1,0:T(2,128)} %bitcast.44), custom_call_target="tpu_custom_call" | custom-call | tf_op jit(solution)/shard_map/pallas_call | solution.py:32
  1.5 0.5 %collective-permute-start = (f32[64,128]{1,0:T(8,128)S(1)}, f32[64,128]{1,0:T(8,128)S(1)}, u32[]{:S(2)}, u32[]{:S(2)}) collective-permute-start(f32[64,128]{1,0:T(8,128)S(1)} %get-tuple-element.35), channel_id=1, source_target_pairs={{0,1},{1,0},{2,3},{3,2},{4,8},{5,9},{6,10},{7,11},{8,4},{9,5},{10,... | collective-permute-start | bytes 98312 | tf_op jit(solution)/shard_map/ppermute | solution.py:412
  2.0 4.0 %collective-permute-start.1 = (f32[64,128]{1,0:T(8,128)S(1)}, f32[64,128]{1,0:T(8,128)S(1)}, u32[]{:S(2)}, u32[]{:S(2)}) collective-permute-start(f32[64,128]{1,0:T(8,128)S(1)} %get-tuple-element.36), channel_id=1, source_target_pairs={{0,4},{1,5},{2,6},{3,7},{4,0},{5,1},{6,2},{7,3},{8,12},{9,13},{10,... | collective-permute-start | bytes 98312 | tf_op jit(solution)/shard_map/ppermute | solution.py:412
  6.1 0.0 copy-start
  6.1 0.0 copy-start.1
  6.1 1.6 %shard_map.131 = (f32[64,128]{1,0:T(8,128)S(1)}, bf16[256,128]{1,0:T(8,128)(2,1)S(1)}, bf16[128,128]{1,0:T(8,128)(2,1)S(1)}, bf16[848,128]{1,0:T(8,128)(2,1)S(1)...) custom-call(s32[1,128]{1,0:T(1,128)} %bitcast.47, s32[2,128]{1,0:T(2,128)} %bitcast.45, ...), custom_call_target="tpu_custom_call" | custom-call | tf_op jit(solution)/shard_map/pallas_call | solution.py:32
  7.7 0.0 collective-permute-done.refs_1_
  7.7 0.3 collective-permute-done.1.refs_2_
  8.0 0.0 copy-done
  8.0 0.0 copy-done.1
  8.0 0.3 shard_map.133
  8.3 2.1 %collective-permute-start.2 = (bf16[848,128]{1,0:T(8,128)(2,1)S(1)}, bf16[848,128]{1,0:T(8,128)(2,1)S(1)}, u32[]{:S(2)}, u32[]{:S(2)}) collective-permute-start(bf16[848,128]{1,0:T(8,128)(2,1)S(1)} %get-tuple-element.44), channel_id=1, source_target_pairs={{0,4},{1,5},{2,6},{3,7},{4,0},{5,1},{6,2},{7,3},{8,12},{9,13},{10,... | collective-permute-start | bytes 651272 | tf_op jit(solution)/shard_map/ppermute | solution.py:446
  10.4 0.0 collective-permute-start.3
  10.4 12.3 %all_to_all.33 = f32[32,1,128]{2,1,0:T(1,128)S(1)} all-to-all(f32[32,1,128]{2,1,0:T(1,128)S(1)} %bitcast.41), channel_id=1, replica_groups=mesh['sub'=8,'grp'=4] {'sub','grp'}, dimensions={0} | all-to-all | bytes 32768 | tf_op jit(solution)/shard_map/all_to_all | solution.py:415
  22.7 0.0 collective-permute-done.2.refs_2_
  22.7 0.0 collective-permute-done.3.refs_3_
  22.7 1.0 %shard_map.134 = (f32[64,128]{1,0:T(8,128)S(1)}, f32[64,128]{1,0:T(8,128)S(1)}, f32[64,128]{1,0:T(8,128)S(1)}, f32[32,128]{1,0:T(8,128)S(1)}, f32[64,128]{1,0:T(...) custom-call(f32[32,128]{1,0:T(8,128)S(1)} %bitcast.35, ...), custom_call_target="tpu_custom_call" | custom-call | tf_op jit(solution)/shard_map/pallas_call | solution.py:32
  23.7 0.6 %collective-permute-start.4 = (f32[64,128]{1,0:T(8,128)S(1)}, f32[64,128]{1,0:T(8,128)S(1)}, u32[]{:S(2)}, u32[]{:S(2)}) collective-permute-start(f32[64,128]{1,0:T(8,128)S(1)} %get-tuple-element.48), channel_id=1, source_target_pairs={{0,4},{1,5},{2,6},{3,7},{4,0},{5,1},{6,2},{7,3},{8,12},{9,13},{10,... | collective-permute-start | bytes 98312 | tf_op jit(solution)/shard_map/ppermute | solution.py:412
  24.3 0.0 collective-permute-start.5
  24.3 10.3 %all_to_all.34 = f32[32,1,128]{2,1,0:T(1,128)S(1)} all-to-all(f32[32,1,128]{2,1,0:T(1,128)S(1)} %bitcast.39), channel_id=1, replica_groups=mesh['sub'=8,'grp'=4] {'sub','grp'}, dimensions={0} | all-to-all | bytes 32768 | tf_op jit(solution)/shard_map/all_to_all | solution.py:415
  34.6 0.0 collective-permute-done.4.refs_2_
  34.6 0.0 collective-permute-done.5.refs_3_
  34.6 0.9 %shard_map.135 = (f32[64,128]{1,0:T(8,128)S(1)}, f32[64,128]{1,0:T(8,128)S(1)}, f32[64,128]{1,0:T(8,128)S(1)}, f32[8,128]{1,0:T(8,128)S(1)}, f32[32,128]{1,0:T(8,128)S(1)}) custom-call(f32[32,128]{1,0:T(8,128)S(1)} %bitcast.37, f32[32,128]{1,0:T(8,128)S(1)} %bitcast.36, f32[64,128]{1,0:T(8,128)S(1)} %collective-permute-done.4.refs_2_, ...), custom_call_target="tpu_custom_call" | custom-call | tf_op jit(solution)/shard_map/pallas_call | solution.py:32
  35.4 0.0 copy-start.2
  35.4 9.0 %all_to_all.35 = f32[32,1,128]{2,1,0:T(1,128)S(1)} all-to-all(f32[32,1,128]{2,1,0:T(1,128)S(1)} %bitcast.40), channel_id=1, replica_groups=mesh['sub'=8,'grp'=4] {'sub','grp'}, dimensions={0} | all-to-all | bytes 32768 | tf_op jit(solution)/shard_map/all_to_all | solution.py:415
  44.4 0.0 copy-done.2
  44.4 0.7 %shard_map.136 = (f32[64,128]{1,0:T(8,128)}, f32[64,128]{1,0:T(8,128)}) custom-call(f32[32,128]{1,0:T(8,128)S(1)} %bitcast.38, f32[8,128]{1,0:T(8,128)S(1)} %get-tuple-element.59.scalars_ref, f32[64,128]{1,0:T(8,128)S(1)} %bitcast.34, f32[64,128]{1,0:T(8,128)S(1)} %get-tuple-element.56.refs_10_.basis_ref, f32[64,128]{1,0:T(8,128)S(1)} %get-tuple-element.60.basis_two_ref, ...), custom_call_target="tpu_custom_call" | custom-call | tf_op jit(solution)/shard_map/pallas_call | solution.py:32
Async XLA Ops:
  1.5 6.2 %collective-permute-start = (f32[64,128]{1,0:T(8,128)S(1)}, f32[64,128]{1,0:T(8,128)S(1)}, u32[]{:S(2)}, u32[]{:S(2)}) collective-permute-start(f32[64,128]{1,0:T(8,128)S(1)} %get-tuple-element.35), channel_id=1, source_target_pairs={{0,1},{1,0},{2,3},{3,2},{4,8},{5,9},{6,10},{7,11},{8,4},{9,5},{10,... | collective-permute-start | bytes 98312 | tf_op jit(solution)/shard_map/ppermute | solution.py:412
  2.0 5.9 %collective-permute-start.1 = (f32[64,128]{1,0:T(8,128)S(1)}, f32[64,128]{1,0:T(8,128)S(1)}, u32[]{:S(2)}, u32[]{:S(2)}) collective-permute-start(f32[64,128]{1,0:T(8,128)S(1)} %get-tuple-element.36), channel_id=1, source_target_pairs={{0,4},{1,5},{2,6},{3,7},{4,0},{5,1},{6,2},{7,3},{8,12},{9,13},{10,... | collective-permute-start | bytes 98312 | tf_op jit(solution)/shard_map/ppermute | solution.py:412
  6.1 1.9 %copy-start = (f32[1,1,64,128]{3,2,1,0:T(8,128)S(1)}, f32[1,1,64,128]{3,2,1,0:T(8,128)}, u32[]{:S(2)}) copy-start(f32[1,1,64,128]{3,2,1,0:T(8,128)} %param.17) | copy-start | bytes 98308
  6.1 1.9 %copy-start.1 = (f32[1,1,64,128]{3,2,1,0:T(8,128)S(1)}, f32[1,1,64,128]{3,2,1,0:T(8,128)}, u32[]{:S(2)}) copy-start(f32[1,1,64,128]{3,2,1,0:T(8,128)} %param.16) | copy-start | bytes 98308
  8.3 14.4 %collective-permute-start.2 = (bf16[848,128]{1,0:T(8,128)(2,1)S(1)}, bf16[848,128]{1,0:T(8,128)(2,1)S(1)}, u32[]{:S(2)}, u32[]{:S(2)}) collective-permute-start(bf16[848,128]{1,0:T(8,128)(2,1)S(1)} %get-tuple-element.44), channel_id=1, source_target_pairs={{0,4},{1,5},{2,6},{3,7},{4,0},{5,1},{6,2},{7,3},{8,12},{9,13},{10,... | collective-permute-start | bytes 651272 | tf_op jit(solution)/shard_map/ppermute | solution.py:446
  10.4 12.3 %collective-permute-start.3 = (bf16[848,128]{1,0:T(8,128)(2,1)S(1)}, bf16[848,128]{1,0:T(8,128)(2,1)S(1)}, u32[]{:S(2)}, u32[]{:S(2)}) collective-permute-start(bf16[848,128]{1,0:T(8,128)(2,1)S(1)} %get-tuple-element.43.refs_1_), channel_id=1, source_target_pairs={{0,1},{1,0},{2,3},{3,2},{4,8},{5,9},{6,10},{7,11},{8,4},{9,5},{10,... | collective-permute-start | bytes 651272 | tf_op jit(solution)/shard_map/ppermute | solution.py:447
  23.7 10.9 %collective-permute-start.4 = (f32[64,128]{1,0:T(8,128)S(1)}, f32[64,128]{1,0:T(8,128)S(1)}, u32[]{:S(2)}, u32[]{:S(2)}) collective-permute-start(f32[64,128]{1,0:T(8,128)S(1)} %get-tuple-element.48), channel_id=1, source_target_pairs={{0,4},{1,5},{2,6},{3,7},{4,0},{5,1},{6,2},{7,3},{8,12},{9,13},{10,... | collective-permute-start | bytes 98312 | tf_op jit(solution)/shard_map/ppermute | solution.py:412
  24.3 10.3 %collective-permute-start.5 = (f32[64,128]{1,0:T(8,128)S(1)}, f32[64,128]{1,0:T(8,128)S(1)}, u32[]{:S(2)}, u32[]{:S(2)}) collective-permute-start(f32[64,128]{1,0:T(8,128)S(1)} %get-tuple-element.49), channel_id=1, source_target_pairs={{0,1},{1,0},{2,3},{3,2},{4,8},{5,9},{6,10},{7,11},{8,4},{9,5},{10,... | collective-permute-start | bytes 98312 | tf_op jit(solution)/shard_map/ppermute | solution.py:412
  35.4 9.0 %copy-start.2 = (f32[1,1,64,128]{3,2,1,0:T(8,128)S(1)}, f32[1,1,64,128]{3,2,1,0:T(8,128)}, u32[]{:S(2)}) copy-start(f32[1,1,64,128]{3,2,1,0:T(8,128)} %param.13) | copy-start | bytes 98308

commit v10 on v9

--- a/solution.py
+++ b/solution.py
@@ -280,6 +280,31 @@
     return [cdiag * row + share for cdiag, row, share in zip(cdiags, near_rows, shares)]
 
 
+def solve_at_blocks(parts, matrix_ref, near_rows, cdiags, aggs, cpd):
+    group = parts[0].shape[0]
+    shape = (group, LANES)
+    row = lax.broadcasted_iota(jnp.int32, shape, 0)
+    lane = lax.broadcasted_iota(jnp.int32, shape, 1)
+    masks = [(at + lane) // cpd == row for at in range(0, group * cpd, LANES)]
+    source = lax.rem(lane - cpd * row + cpd * group, LANES)
+    tiles = []
+    for part in parts:
+        shifted = along_lanes(part, source)
+        for mask in masks:
+            tiles.append(jnp.sum(jnp.where(mask, shifted, 0.0), axis=0, keepdims=True))
+    vector = jnp.concatenate(tiles, axis=1)
+    product = lax.dot_general(
+        matrix_ref[...], jnp.broadcast_to(vector, (LANES, vector.shape[1])).astype(bf16),
+        (((1,), (1,)), ((), ())), preferred_element_type=f32,
+    )
+    unknown = lax.broadcasted_iota(jnp.int32, (cpd, LANES), 0)
+    spreads = []
+    for slot, (cdiag, near_row, agg) in enumerate(zip(cdiags, near_rows, aggs)):
+        share = jnp.where(unknown == agg, product[slot * SLOT : slot * SLOT + cpd], 0.0)
+        spreads.append(spread_of(cdiag * near_row, agg) + jnp.sum(share, axis=0, keepdims=True))
+    return spreads
+
+
 def parts_of(ref, cpd):
     group = math.lcm(cpd, LANES) // cpd
     rows = ref[...]
@@ -320,16 +345,16 @@
     inverse = 1.0 / jnp.sqrt(summed(got_ref, cpd, 1)[0])
     parts = [part * inverse for part in parts_of(got_ref, cpd)]
     cdiags = [info_ref[at : at + 1, :] for at in range(3)]
-    solved = solve_coarse(parts, matrix_ref, rows_near(parts, grp_size), cdiags, cpd)
+    aggs = [notes_ref[AGG]] + [info_ref[at : at + 1, :].astype(jnp.int32) for at in (3, 4)]
+    spreads = solve_at_blocks(parts, matrix_ref, rows_near(parts, grp_size), cdiags, aggs, cpd)
     basis = first_ref[...] * inverse
     basis_ref[...] = basis
-    spread = spread_of(solved[0], notes_ref[AGG])
     jscale, prolong = jscale_ref[...], prolong_ref[...]
-    direction = jscale * basis + prolong * spread
+    direction = jscale * basis + prolong * spreads[0]
     direction_ref[...] = direction
     near = [
-        odd_near_ref[...] * inverse + near_spread(odd_weights_ref, info_ref, 0, solved[1]),
-        even_near_ref[...] * inverse + near_spread(even_weights_ref, info_ref, 1, solved[2]),
+        odd_near_ref[...] * inverse + odd_weights_ref[...] * spreads[1],
+        even_near_ref[...] * inverse + even_weights_ref[...] * spreads[2],
     ]
     image = local_product(blocks_ref, notes_ref[VALVE], direction)
     image = image - coupling * received(near, arrive_ref)

time: 45.5 us -> 45.4 us (level)
  no operation moved by 1% of the time
where the time goes in v10:
time: 45.4 us; the launch traced here: 45.1 us
  blocking collectives  31.5 us (69%)
  starting transfers between devices  7.25 us (16%)
  Pallas kernels  5.32 us (12%)
  between operations  0.67 us (1%)
    all_to_all x3, blocking collectives, everyone(): return lax.all_to_all(rows, AXES, 0, 0, tiled=True)  31.5 us
    pallas_call x6, Pallas kernels, call(): pl.pallas_call(body, out_shape=[jax.ShapeDtypeStruct(shape, kind) if fina...  5.32 us
    ppermute x2, starting transfers between devices, exchange(): lax.ppermute(even, AXES, moves[1])  4.65 us
    ppermute x1, starting transfers between devices, on_device(): even_pack = lax.ppermute(even, AXES, moves[1])  2.08 us
  transfers between devices with their start and end apart: 6, of which 1 were waited for; matrix products, arithmetic and copies ran while one was open for 0% of the time, Pallas kernels for 4%

profile of v10, /device:TPU:0, one launch (start us, length us, event | category | flops | bytes accessed | tf_op | source)
XLA Modules:
  0.0 45.1 jit_solution(8979926671824557085)
XLA Ops:
  0.6 0.9 %shard_map.132 = (f32[64,128]{1,0:T(8,128)S(1)}, f32[64,128]{1,0:T(8,128)S(1)}) custom-call(f32[64,128]{1,0:T(8,128)} %bitcast.32, s32[2,128]{1,0:T(2,128)} %bitcast.44), custom_call_target="tpu_custom_call" | custom-call | tf_op jit(solution)/shard_map/pallas_call | solution.py:32
  1.5 0.5 %collective-permute-start = (f32[64,128]{1,0:T(8,128)S(1)}, f32[64,128]{1,0:T(8,128)S(1)}, u32[]{:S(2)}, u32[]{:S(2)}) collective-permute-start(f32[64,128]{1,0:T(8,128)S(1)} %get-tuple-element.35), channel_id=1, source_target_pairs={{0,1},{1,0},{2,3},{3,2},{4,8},{5,9},{6,10},{7,11},{8,4},{9,5},{10,... | collective-permute-start | bytes 98312 | tf_op jit(solution)/shard_map/ppermute | solution.py:437
  2.0 4.0 %collective-permute-start.1 = (f32[64,128]{1,0:T(8,128)S(1)}, f32[64,128]{1,0:T(8,128)S(1)}, u32[]{:S(2)}, u32[]{:S(2)}) collective-permute-start(f32[64,128]{1,0:T(8,128)S(1)} %get-tuple-element.36), channel_id=1, source_target_pairs={{0,4},{1,5},{2,6},{3,7},{4,0},{5,1},{6,2},{7,3},{8,12},{9,13},{10,... | collective-permute-start | bytes 98312 | tf_op jit(solution)/shard_map/ppermute | solution.py:437
  6.1 0.0 copy-start
  6.1 0.0 copy-start.1
  6.1 1.6 %shard_map.131 = (f32[64,128]{1,0:T(8,128)S(1)}, bf16[256,128]{1,0:T(8,128)(2,1)S(1)}, bf16[128,128]{1,0:T(8,128)(2,1)S(1)}, bf16[848,128]{1,0:T(8,128)(2,1)S(1)...) custom-call(s32[1,128]{1,0:T(1,128)} %bitcast.47, s32[2,128]{1,0:T(2,128)} %bitcast.45, ...), custom_call_target="tpu_custom_call" | custom-call | tf_op jit(solution)/shard_map/pallas_call | solution.py:32
  7.7 0.0 collective-permute-done.refs_1_
  7.7 0.3 collective-permute-done.1.refs_2_
  8.0 0.0 copy-done
  8.0 0.0 copy-done.1
  8.0 0.3 shard_map.133
  8.3 2.1 %collective-permute-start.2 = (bf16[848,128]{1,0:T(8,128)(2,1)S(1)}, bf16[848,128]{1,0:T(8,128)(2,1)S(1)}, u32[]{:S(2)}, u32[]{:S(2)}) collective-permute-start(bf16[848,128]{1,0:T(8,128)(2,1)S(1)} %get-tuple-element.44), channel_id=1, source_target_pairs={{0,4},{1,5},{2,6},{3,7},{4,0},{5,1},{6,2},{7,3},{8,12},{9,13},{10,... | collective-permute-start | bytes 651272 | tf_op jit(solution)/shard_map/ppermute | solution.py:471
  10.4 0.0 collective-permute-start.3
  10.4 12.3 %all_to_all.33 = f32[32,1,128]{2,1,0:T(1,128)S(1)} all-to-all(f32[32,1,128]{2,1,0:T(1,128)S(1)} %bitcast.41), channel_id=1, replica_groups=mesh['sub'=8,'grp'=4] {'sub','grp'}, dimensions={0} | all-to-all | bytes 32768 | tf_op jit(solution)/shard_map/all_to_all | solution.py:440
  22.7 0.0 collective-permute-done.2.refs_2_
  22.7 0.0 collective-permute-done.3.refs_3_
  22.7 0.9 %shard_map.134 = (f32[64,128]{1,0:T(8,128)S(1)}, f32[64,128]{1,0:T(8,128)S(1)}, f32[64,128]{1,0:T(8,128)S(1)}, f32[32,128]{1,0:T(8,128)S(1)}, f32[64,128]{1,0:T(...) custom-call(f32[32,128]{1,0:T(8,128)S(1)} %bitcast.35, ...), custom_call_target="tpu_custom_call" | custom-call | tf_op jit(solution)/shard_map/pallas_call | solution.py:32
  23.6 0.6 %collective-permute-start.4 = (f32[64,128]{1,0:T(8,128)S(1)}, f32[64,128]{1,0:T(8,128)S(1)}, u32[]{:S(2)}, u32[]{:S(2)}) collective-permute-start(f32[64,128]{1,0:T(8,128)S(1)} %get-tuple-element.48), channel_id=1, source_target_pairs={{0,4},{1,5},{2,6},{3,7},{4,0},{5,1},{6,2},{7,3},{8,12},{9,13},{10,... | collective-permute-start | bytes 98312 | tf_op jit(solution)/shard_map/ppermute | solution.py:437
  24.2 0.0 collective-permute-start.5
  24.2 10.3 %all_to_all.34 = f32[32,1,128]{2,1,0:T(1,128)S(1)} all-to-all(f32[32,1,128]{2,1,0:T(1,128)S(1)} %bitcast.39), channel_id=1, replica_groups=mesh['sub'=8,'grp'=4] {'sub','grp'}, dimensions={0} | all-to-all | bytes 32768 | tf_op jit(solution)/shard_map/all_to_all | solution.py:440
  34.5 0.0 collective-permute-done.4.refs_2_
  34.5 0.0 collective-permute-done.5.refs_3_
  34.5 0.9 %shard_map.135 = (f32[64,128]{1,0:T(8,128)S(1)}, f32[64,128]{1,0:T(8,128)S(1)}, f32[64,128]{1,0:T(8,128)S(1)}, f32[8,128]{1,0:T(8,128)S(1)}, f32[32,128]{1,0:T(8,128)S(1)}) custom-call(f32[32,128]{1,0:T(8,128)S(1)} %bitcast.37, f32[32,128]{1,0:T(8,128)S(1)} %bitcast.36, f32[64,128]{1,0:T(8,128)S(1)} %collective-permute-done.4.refs_2_, ...), custom_call_target="tpu_custom_call" | custom-call | tf_op jit(solution)/shard_map/pallas_call | solution.py:32
  35.4 0.0 copy-start.2
  35.4 9.0 %all_to_all.35 = f32[32,1,128]{2,1,0:T(1,128)S(1)} all-to-all(f32[32,1,128]{2,1,0:T(1,128)S(1)} %bitcast.40), channel_id=1, replica_groups=mesh['sub'=8,'grp'=4] {'sub','grp'}, dimensions={0} | all-to-all | bytes 32768 | tf_op jit(solution)/shard_map/all_to_all | solution.py:440
  44.3 0.0 copy-done.2
  44.3 0.7 %shard_map.136 = (f32[64,128]{1,0:T(8,128)}, f32[64,128]{1,0:T(8,128)}) custom-call(f32[32,128]{1,0:T(8,128)S(1)} %bitcast.38, f32[8,128]{1,0:T(8,128)S(1)} %get-tuple-element.59.scalars_ref, f32[64,128]{1,0:T(8,128)S(1)} %bitcast.34, f32[64,128]{1,0:T(8,128)S(1)} %get-tuple-element.56.refs_10_.basis_ref, f32[64,128]{1,0:T(8,128)S(1)} %get-tuple-element.60.basis_two_ref, ...), custom_call_target="tpu_custom_call" | custom-call | tf_op jit(solution)/shard_map/pallas_call | solution.py:32
Async XLA Ops:
  1.5 6.2 %collective-permute-start = (f32[64,128]{1,0:T(8,128)S(1)}, f32[64,128]{1,0:T(8,128)S(1)}, u32[]{:S(2)}, u32[]{:S(2)}) collective-permute-start(f32[64,128]{1,0:T(8,128)S(1)} %get-tuple-element.35), channel_id=1, source_target_pairs={{0,1},{1,0},{2,3},{3,2},{4,8},{5,9},{6,10},{7,11},{8,4},{9,5},{10,... | collective-permute-start | bytes 98312 | tf_op jit(solution)/shard_map/ppermute | solution.py:437
  2.0 5.9 %collective-permute-start.1 = (f32[64,128]{1,0:T(8,128)S(1)}, f32[64,128]{1,0:T(8,128)S(1)}, u32[]{:S(2)}, u32[]{:S(2)}) collective-permute-start(f32[64,128]{1,0:T(8,128)S(1)} %get-tuple-element.36), channel_id=1, source_target_pairs={{0,4},{1,5},{2,6},{3,7},{4,0},{5,1},{6,2},{7,3},{8,12},{9,13},{10,... | collective-permute-start | bytes 98312 | tf_op jit(solution)/shard_map/ppermute | solution.py:437
  6.1 1.9 %copy-start = (f32[1,1,64,128]{3,2,1,0:T(8,128)S(1)}, f32[1,1,64,128]{3,2,1,0:T(8,128)}, u32[]{:S(2)}) copy-start(f32[1,1,64,128]{3,2,1,0:T(8,128)} %param.17) | copy-start | bytes 98308
  6.1 1.9 %copy-start.1 = (f32[1,1,64,128]{3,2,1,0:T(8,128)S(1)}, f32[1,1,64,128]{3,2,1,0:T(8,128)}, u32[]{:S(2)}) copy-start(f32[1,1,64,128]{3,2,1,0:T(8,128)} %param.16) | copy-start | bytes 98308
  8.3 14.4 %collective-permute-start.2 = (bf16[848,128]{1,0:T(8,128)(2,1)S(1)}, bf16[848,128]{1,0:T(8,128)(2,1)S(1)}, u32[]{:S(2)}, u32[]{:S(2)}) collective-permute-start(bf16[848,128]{1,0:T(8,128)(2,1)S(1)} %get-tuple-element.44), channel_id=1, source_target_pairs={{0,4},{1,5},{2,6},{3,7},{4,0},{5,1},{6,2},{7,3},{8,12},{9,13},{10,... | collective-permute-start | bytes 651272 | tf_op jit(solution)/shard_map/ppermute | solution.py:471
  10.4 12.3 %collective-permute-start.3 = (bf16[848,128]{1,0:T(8,128)(2,1)S(1)}, bf16[848,128]{1,0:T(8,128)(2,1)S(1)}, u32[]{:S(2)}, u32[]{:S(2)}) collective-permute-start(bf16[848,128]{1,0:T(8,128)(2,1)S(1)} %get-tuple-element.43.refs_1_), channel_id=1, source_target_pairs={{0,1},{1,0},{2,3},{3,2},{4,8},{5,9},{6,10},{7,11},{8,4},{9,5},{10,... | collective-permute-start | bytes 651272 | tf_op jit(solution)/shard_map/ppermute | solution.py:472
  23.6 10.9 %collective-permute-start.4 = (f32[64,128]{1,0:T(8,128)S(1)}, f32[64,128]{1,0:T(8,128)S(1)}, u32[]{:S(2)}, u32[]{:S(2)}) collective-permute-start(f32[64,128]{1,0:T(8,128)S(1)} %get-tuple-element.48), channel_id=1, source_target_pairs={{0,4},{1,5},{2,6},{3,7},{4,0},{5,1},{6,2},{7,3},{8,12},{9,13},{10,... | collective-permute-start | bytes 98312 | tf_op jit(solution)/shard_map/ppermute | solution.py:437
  24.2 10.3 %collective-permute-start.5 = (f32[64,128]{1,0:T(8,128)S(1)}, f32[64,128]{1,0:T(8,128)S(1)}, u32[]{:S(2)}, u32[]{:S(2)}) collective-permute-start(f32[64,128]{1,0:T(8,128)S(1)} %get-tuple-element.49), channel_id=1, source_target_pairs={{0,1},{1,0},{2,3},{3,2},{4,8},{5,9},{6,10},{7,11},{8,4},{9,5},{10,... | collective-permute-start | bytes 98312 | tf_op jit(solution)/shard_map/ppermute | solution.py:437
  35.4 9.0 %copy-start.2 = (f32[1,1,64,128]{3,2,1,0:T(8,128)S(1)}, f32[1,1,64,128]{3,2,1,0:T(8,128)}, u32[]{:S(2)}) copy-start(f32[1,1,64,128]{3,2,1,0:T(8,128)} %param.13) | copy-start | bytes 98308

commit v11 on v10

--- a/solution.py
+++ b/solution.py
@@ -342,7 +342,7 @@
                odd_weights_ref, even_weights_ref, odd_near_ref, even_near_ref, info_ref):
     unpack(own_pack_ref, even_pack_ref, odd_pack_ref, cpd, matrix_ref, odd_weights_ref,
            even_weights_ref, odd_near_ref, even_near_ref, info_ref)
-    inverse = 1.0 / jnp.sqrt(summed(got_ref, cpd, 1)[0])
+    inverse = lax.rsqrt(summed(got_ref, cpd, 1)[0])
     parts = [part * inverse for part in parts_of(got_ref, cpd)]
     cdiags = [info_ref[at : at + 1, :] for at in range(3)]
     aggs = [notes_ref[AGG]] + [info_ref[at : at + 1, :].astype(jnp.int32) for at in (3, 4)]
@@ -375,7 +375,7 @@
     along, energy = summed(got_ref, cpd, 2)
     height = jnp.sqrt(jnp.maximum(energy - along * along, 0.01 * energy))
     inverse = 1.0 / height
-    slope = along / beta
+    slope = along * (1.0 / beta)
 
     def mixed(new, old):
         return (new - slope * old) * inverse

time: 45.4 us -> 45.4 us (level)
  no operation moved by 1% of the time
where the time goes in v11:
time: 45.4 us; the launch traced here: 45.1 us
  blocking collectives  31.5 us (69%)
  starting transfers between devices  7.25 us (16%)
  Pallas kernels  5.32 us (12%)
  between operations  0.67 us (1%)
    all_to_all x3, blocking collectives, everyone(): return lax.all_to_all(rows, AXES, 0, 0, tiled=True)  31.5 us
    pallas_call x6, Pallas kernels, call(): pl.pallas_call(body, out_shape=[jax.ShapeDtypeStruct(shape, kind) if fina...  5.32 us
    ppermute x2, starting transfers between devices, exchange(): lax.ppermute(even, AXES, moves[1])  4.65 us
    ppermute x1, starting transfers between devices, on_device(): even_pack = lax.ppermute(even, AXES, moves[1])  2.08 us
  transfers between devices with their start and end apart: 6, of which 1 were waited for; matrix products, arithmetic and copies ran while one was open for 0% of the time, Pallas kernels for 4%

profile of v11, /device:TPU:0, one launch (start us, length us, event | category | flops | bytes accessed | tf_op | source)
XLA Modules:
  0.0 45.1 jit_solution(8629667792944326457)
XLA Ops:
  0.6 0.9 %shard_map.132 = (f32[64,128]{1,0:T(8,128)S(1)}, f32[64,128]{1,0:T(8,128)S(1)}) custom-call(f32[64,128]{1,0:T(8,128)} %bitcast.32, s32[2,128]{1,0:T(2,128)} %bitcast.44), custom_call_target="tpu_custom_call" | custom-call | tf_op jit(solution)/shard_map/pallas_call | solution.py:32
  1.5 0.5 %collective-permute-start = (f32[64,128]{1,0:T(8,128)S(1)}, f32[64,128]{1,0:T(8,128)S(1)}, u32[]{:S(2)}, u32[]{:S(2)}) collective-permute-start(f32[64,128]{1,0:T(8,128)S(1)} %get-tuple-element.35), channel_id=1, source_target_pairs={{0,1},{1,0},{2,3},{3,2},{4,8},{5,9},{6,10},{7,11},{8,4},{9,5},{10,... | collective-permute-start | bytes 98312 | tf_op jit(solution)/shard_map/ppermute | solution.py:437
  2.0 4.0 %collective-permute-start.1 = (f32[64,128]{1,0:T(8,128)S(1)}, f32[64,128]{1,0:T(8,128)S(1)}, u32[]{:S(2)}, u32[]{:S(2)}) collective-permute-start(f32[64,128]{1,0:T(8,128)S(1)} %get-tuple-element.36), channel_id=1, source_target_pairs={{0,4},{1,5},{2,6},{3,7},{4,0},{5,1},{6,2},{7,3},{8,12},{9,13},{10,... | collective-permute-start | bytes 98312 | tf_op jit(solution)/shard_map/ppermute | solution.py:437
  6.1 0.0 copy-start
  6.1 0.0 copy-start.1
  6.1 1.6 %shard_map.131 = (f32[64,128]{1,0:T(8,128)S(1)}, bf16[256,128]{1,0:T(8,128)(2,1)S(1)}, bf16[128,128]{1,0:T(8,128)(2,1)S(1)}, bf16[848,128]{1,0:T(8,128)(2,1)S(1)...) custom-call(s32[1,128]{1,0:T(1,128)} %bitcast.47, s32[2,128]{1,0:T(2,128)} %bitcast.45, ...), custom_call_target="tpu_custom_call" | custom-call | tf_op jit(solution)/shard_map/pallas_call | solution.py:32
  7.7 0.0 collective-permute-done.refs_1_
  7.7 0.3 collective-permute-done.1.refs_2_
  8.0 0.0 copy-done
  8.0 0.0 copy-done.1
  8.0 0.3 shard_map.133
  8.3 2.1 %collective-permute-start.2 = (bf16[848,128]{1,0:T(8,128)(2,1)S(1)}, bf16[848,128]{1,0:T(8,128)(2,1)S(1)}, u32[]{:S(2)}, u32[]{:S(2)}) collective-permute-start(bf16[848,128]{1,0:T(8,128)(2,1)S(1)} %get-tuple-element.44), channel_id=1, source_target_pairs={{0,4},{1,5},{2,6},{3,7},{4,0},{5,1},{6,2},{7,3},{8,12},{9,13},{10,... | collective-permute-start | bytes 651272 | tf_op jit(solution)/shard_map/ppermute | solution.py:471
  10.4 0.0 collective-permute-start.3
  10.4 12.3 %all_to_all.33 = f32[32,1,128]{2,1,0:T(1,128)S(1)} all-to-all(f32[32,1,128]{2,1,0:T(1,128)S(1)} %bitcast.41), channel_id=1, replica_groups=mesh['sub'=8,'grp'=4] {'sub','grp'}, dimensions={0} | all-to-all | bytes 32768 | tf_op jit(solution)/shard_map/all_to_all | solution.py:440
  22.7 0.0 collective-permute-done.2.refs_2_
  22.7 0.0 collective-permute-done.3.refs_3_
  22.7 0.9 %shard_map.134 = (f32[64,128]{1,0:T(8,128)S(1)}, f32[64,128]{1,0:T(8,128)S(1)}, f32[64,128]{1,0:T(8,128)S(1)}, f32[32,128]{1,0:T(8,128)S(1)}, f32[64,128]{1,0:T(...) custom-call(f32[32,128]{1,0:T(8,128)S(1)} %bitcast.35, ...), custom_call_target="tpu_custom_call" | custom-call | tf_op jit(solution)/shard_map/pallas_call | solution.py:32
  23.6 0.6 %collective-permute-start.4 = (f32[64,128]{1,0:T(8,128)S(1)}, f32[64,128]{1,0:T(8,128)S(1)}, u32[]{:S(2)}, u32[]{:S(2)}) collective-permute-start(f32[64,128]{1,0:T(8,128)S(1)} %get-tuple-element.48), channel_id=1, source_target_pairs={{0,4},{1,5},{2,6},{3,7},{4,0},{5,1},{6,2},{7,3},{8,12},{9,13},{10,... | collective-permute-start | bytes 98312 | tf_op jit(solution)/shard_map/ppermute | solution.py:437
  24.2 0.0 collective-permute-start.5
  24.2 10.3 %all_to_all.34 = f32[32,1,128]{2,1,0:T(1,128)S(1)} all-to-all(f32[32,1,128]{2,1,0:T(1,128)S(1)} %bitcast.39), channel_id=1, replica_groups=mesh['sub'=8,'grp'=4] {'sub','grp'}, dimensions={0} | all-to-all | bytes 32768 | tf_op jit(solution)/shard_map/all_to_all | solution.py:440
  34.5 0.0 collective-permute-done.4.refs_2_
  34.5 0.0 collective-permute-done.5.refs_3_
  34.5 0.9 %shard_map.135 = (f32[64,128]{1,0:T(8,128)S(1)}, f32[64,128]{1,0:T(8,128)S(1)}, f32[64,128]{1,0:T(8,128)S(1)}, f32[8,128]{1,0:T(8,128)S(1)}, f32[32,128]{1,0:T(8,128)S(1)}) custom-call(f32[32,128]{1,0:T(8,128)S(1)} %bitcast.37, f32[32,128]{1,0:T(8,128)S(1)} %bitcast.36, f32[64,128]{1,0:T(8,128)S(1)} %collective-permute-done.4.refs_2_, ...), custom_call_target="tpu_custom_call" | custom-call | tf_op jit(solution)/shard_map/pallas_call | solution.py:32
  35.4 0.0 copy-start.2
  35.4 9.0 %all_to_all.35 = f32[32,1,128]{2,1,0:T(1,128)S(1)} all-to-all(f32[32,1,128]{2,1,0:T(1,128)S(1)} %bitcast.40), channel_id=1, replica_groups=mesh['sub'=8,'grp'=4] {'sub','grp'}, dimensions={0} | all-to-all | bytes 32768 | tf_op jit(solution)/shard_map/all_to_all | solution.py:440
  44.3 0.0 copy-done.2
  44.3 0.7 %shard_map.136 = (f32[64,128]{1,0:T(8,128)}, f32[64,128]{1,0:T(8,128)}) custom-call(f32[32,128]{1,0:T(8,128)S(1)} %bitcast.38, f32[8,128]{1,0:T(8,128)S(1)} %get-tuple-element.59.scalars_ref, f32[64,128]{1,0:T(8,128)S(1)} %bitcast.34, f32[64,128]{1,0:T(8,128)S(1)} %get-tuple-element.56.refs_10_.basis_ref, f32[64,128]{1,0:T(8,128)S(1)} %get-tuple-element.60.basis_two_ref, ...), custom_call_target="tpu_custom_call" | custom-call | tf_op jit(solution)/shard_map/pallas_call | solution.py:32
Async XLA Ops:
  1.5 6.2 %collective-permute-start = (f32[64,128]{1,0:T(8,128)S(1)}, f32[64,128]{1,0:T(8,128)S(1)}, u32[]{:S(2)}, u32[]{:S(2)}) collective-permute-start(f32[64,128]{1,0:T(8,128)S(1)} %get-tuple-element.35), channel_id=1, source_target_pairs={{0,1},{1,0},{2,3},{3,2},{4,8},{5,9},{6,10},{7,11},{8,4},{9,5},{10,... | collective-permute-start | bytes 98312 | tf_op jit(solution)/shard_map/ppermute | solution.py:437
  2.0 5.9 %collective-permute-start.1 = (f32[64,128]{1,0:T(8,128)S(1)}, f32[64,128]{1,0:T(8,128)S(1)}, u32[]{:S(2)}, u32[]{:S(2)}) collective-permute-start(f32[64,128]{1,0:T(8,128)S(1)} %get-tuple-element.36), channel_id=1, source_target_pairs={{0,4},{1,5},{2,6},{3,7},{4,0},{5,1},{6,2},{7,3},{8,12},{9,13},{10,... | collective-permute-start | bytes 98312 | tf_op jit(solution)/shard_map/ppermute | solution.py:437
  6.1 1.9 %copy-start = (f32[1,1,64,128]{3,2,1,0:T(8,128)S(1)}, f32[1,1,64,128]{3,2,1,0:T(8,128)}, u32[]{:S(2)}) copy-start(f32[1,1,64,128]{3,2,1,0:T(8,128)} %param.17) | copy-start | bytes 98308
  6.1 1.9 %copy-start.1 = (f32[1,1,64,128]{3,2,1,0:T(8,128)S(1)}, f32[1,1,64,128]{3,2,1,0:T(8,128)}, u32[]{:S(2)}) copy-start(f32[1,1,64,128]{3,2,1,0:T(8,128)} %param.16) | copy-start | bytes 98308
  8.3 14.4 %collective-permute-start.2 = (bf16[848,128]{1,0:T(8,128)(2,1)S(1)}, bf16[848,128]{1,0:T(8,128)(2,1)S(1)}, u32[]{:S(2)}, u32[]{:S(2)}) collective-permute-start(bf16[848,128]{1,0:T(8,128)(2,1)S(1)} %get-tuple-element.44), channel_id=1, source_target_pairs={{0,4},{1,5},{2,6},{3,7},{4,0},{5,1},{6,2},{7,3},{8,12},{9,13},{10,... | collective-permute-start | bytes 651272 | tf_op jit(solution)/shard_map/ppermute | solution.py:471
  10.4 12.3 %collective-permute-start.3 = (bf16[848,128]{1,0:T(8,128)(2,1)S(1)}, bf16[848,128]{1,0:T(8,128)(2,1)S(1)}, u32[]{:S(2)}, u32[]{:S(2)}) collective-permute-start(bf16[848,128]{1,0:T(8,128)(2,1)S(1)} %get-tuple-element.43.refs_1_), channel_id=1, source_target_pairs={{0,1},{1,0},{2,3},{3,2},{4,8},{5,9},{6,10},{7,11},{8,4},{9,5},{10,... | collective-permute-start | bytes 651272 | tf_op jit(solution)/shard_map/ppermute | solution.py:472
  23.6 10.9 %collective-permute-start.4 = (f32[64,128]{1,0:T(8,128)S(1)}, f32[64,128]{1,0:T(8,128)S(1)}, u32[]{:S(2)}, u32[]{:S(2)}) collective-permute-start(f32[64,128]{1,0:T(8,128)S(1)} %get-tuple-element.48), channel_id=1, source_target_pairs={{0,4},{1,5},{2,6},{3,7},{4,0},{5,1},{6,2},{7,3},{8,12},{9,13},{10,... | collective-permute-start | bytes 98312 | tf_op jit(solution)/shard_map/ppermute | solution.py:437
  24.2 10.3 %collective-permute-start.5 = (f32[64,128]{1,0:T(8,128)S(1)}, f32[64,128]{1,0:T(8,128)S(1)}, u32[]{:S(2)}, u32[]{:S(2)}) collective-permute-start(f32[64,128]{1,0:T(8,128)S(1)} %get-tuple-element.49), channel_id=1, source_target_pairs={{0,1},{1,0},{2,3},{3,2},{4,8},{5,9},{6,10},{7,11},{8,4},{9,5},{10,... | collective-permute-start | bytes 98312 | tf_op jit(solution)/shard_map/ppermute | solution.py:437
  35.4 9.0 %copy-start.2 = (f32[1,1,64,128]{3,2,1,0:T(8,128)S(1)}, f32[1,1,64,128]{3,2,1,0:T(8,128)}, u32[]{:S(2)}) copy-start(f32[1,1,64,128]{3,2,1,0:T(8,128)} %param.13) | copy-start | bytes 98308
